TPU v7x, 128 devices: a whole 4x4x4 slice. The times are simulated.
128 devices in a mesh: grp: 2 (over x_hi), slab: 64 (over y, z, x_lo, core).
Axes of the slice: x: 4 (x_hi: 2, x_lo: 2; x = x_hi * 2 + x_lo), y: 4, z: 4, core: 2. Of those that a mesh axis runs over, the one named last changes fastest.
Arguments:
- patterns: bfloat16 [2, 16384, 16384], P('grp', 'slab'), may hold values from 0.099609375 to 10
- probabilities: bfloat16 [2, 16384, 32], P('grp', 'slab'), may hold values from 1.9431114e-05 to 0.001953125
- source_row: int32 [2, 64, 64, 80], P('grp', 'slab'), may hold values from -1 to 4095, as said below
- target_row: int32 [2, 64, 64, 80], P('grp', 'slab'), may hold values from 0 to 2047
- support: int32 [256, 256, 256], P('slab', 'grp'), may hold values 0 or 1
- density: float32 [256, 256, 256], P('slab', 'grp'), may hold values from -6 to 6
Outputs:
- intensity: float32 [256, 256, 256], P('slab', 'grp')
- phased_density: float32 [256, 256, 256], P('slab', 'grp')
Inputs may be any that keep to these rules, and one draw needn't show every extreme that they name: `source_row`: each device's table holds every one of its slice rows 0 to 4095 exactly once; -1 marks an empty slot; one slab owner, drawn from the seed, has all 80 slots filled from every device. target_row[g, o, s, c] is the half-row of owner o's slab for slot c of source_row[g, s, o]; it is arbitrary where that slot is -1.
All inputs are finite; a program needn't handle non-finite values. No bound on the sum of `support` on one device may be relied on, other than what follows from the above.
Results may differ from a plain program's by a relative error of at most 0.0015.
Values may be sent and summed in bfloat16 or wider, within the bound.
No kernel may reach another device: no remote copies, remote signals or barrier semaphores. Data moves between devices by JAX's collectives and lax.ppermute only.
A program may use at most 128 MiB of HBM per device.

v0:
```python
import math

import jax
import jax.numpy as jnp
from jax import lax
from jax.sharding import PartitionSpec as P

DET = 128
ITERS = 2


BETA = 0.9
SOFTEN = 0.25
BLOCK_SLOTS = 1024


def dft_tables(length):
    index = jnp.arange(length, dtype=jnp.int32)
    product = index[:, None] * index[None, :] % length
    angle = 2.0 * math.pi / length * product.astype(jnp.float32)
    factor = 1.0 / math.sqrt(length)
    return (jnp.cos(angle) * factor, jnp.sin(angle) * factor)


def along(field, table, axis):
    letters_in = ["a", "b", "c"]
    letters_out = ["a", "b", "c"]
    letters_in[axis] = "n"
    letters_out[axis] = "k"
    form = "".join(letters_in) + ",nk->" + "".join(letters_out)
    return jnp.einsum(form, field, table, precision=lax.Precision.HIGHEST)


def real_forward(field, tables, axis):
    return (along(field, tables[0], axis), -along(field, tables[1], axis))


def forward_pass(real_part, imag_part, tables, axis):
    new_real = along(real_part, tables[0], axis) + along(imag_part, tables[1], axis)
    new_imag = along(imag_part, tables[0], axis) - along(real_part, tables[1], axis)
    return (new_real, new_imag)


def inverse_pass(real_part, imag_part, tables, axis):
    new_real = along(real_part, tables[0], axis) - along(imag_part, tables[1], axis)
    new_imag = along(imag_part, tables[0], axis) + along(real_part, tables[1], axis)
    return (new_real, new_imag)


def real_inverse(real_part, imag_part, tables, axis):
    return along(real_part, tables[0], axis) - along(imag_part, tables[1], axis)


def project(real_part, imag_part, amplitude):
    scale = amplitude / jnp.sqrt(real_part * real_part + imag_part * imag_part + SOFTEN)
    return (real_part * scale, imag_part * scale)


def mean_of(summed, weights):
    planes, rows_here, width = summed.shape
    divisor = jnp.maximum(weights, 1.0)[..., None]
    return (summed.reshape(planes, rows_here, 2, DET) / divisor).reshape(planes, rows_here, width)


def owner_step(owners, slots):
    step = max(1, BLOCK_SLOTS // slots)
    while owners % step != 0:
        step = step - 1
    return step


def pick_rows(slice_rows, row_weight, source):
    owners, slots = source.shape
    step = owner_step(owners, slots)
    blocks = source.reshape(owners // step, step * slots)
    column = jnp.arange(slice_rows.shape[0], dtype=jnp.int32)

    def one_block(block):
        onehot = (block[:, None] == column[None, :]).astype(jnp.bfloat16)
        picked = jnp.dot(onehot, slice_rows, preferred_element_type=jnp.float32).astype(
            jnp.bfloat16
        )
        picked_weight = jnp.dot(onehot, row_weight, preferred_element_type=jnp.float32).astype(
            jnp.bfloat16
        )
        return (picked, picked_weight)

    picked, picked_weight = lax.map(one_block, blocks)
    return (picked.reshape(owners, slots, -1), picked_weight.reshape(owners, slots))


def place_rows(got_rows, got_weight, target, half_rows):
    owners, slots, width = got_rows.shape
    step = owner_step(owners, slots)
    count = owners // step
    row_blocks = got_rows.reshape(count, step * slots, width)
    weight_blocks = got_weight.reshape(count, step * slots)
    target_blocks = target.reshape(count, step * slots)
    column = jnp.arange(half_rows, dtype=jnp.int32)

    def add_block(carry, inputs):
        summed, weights = carry
        rows, weight_part, where_to = inputs
        onehot = (where_to[:, None] == column[None, :]).astype(jnp.bfloat16)
        summed = summed + jnp.einsum("sh,sd->hd", onehot, rows, preferred_element_type=jnp.float32)
        weights = weights + jnp.einsum(
            "sh,s->h", onehot, weight_part, preferred_element_type=jnp.float32
        )
        return ((summed, weights), None)

    start = (jnp.zeros((half_rows, width), jnp.float32), jnp.zeros((half_rows,), jnp.float32))
    (summed, weights), unused = lax.scan(
        add_block, start, (row_blocks, weight_blocks, target_blocks)
    )
    return (summed, weights)


def local(patterns, probabilities, source_row, target_row, support, density):
    block_probs = probabilities[0]
    slices = jnp.einsum("kr,kp->rp", block_probs, patterns[0], preferred_element_type=jnp.float32)
    slice_rows = slices.astype(jnp.bfloat16).reshape(-1, DET)
    weight = jnp.sum(block_probs.astype(jnp.float32), axis=0).astype(jnp.bfloat16)
    row_weight = jnp.repeat(weight, DET)
    send_rows, send_weight = pick_rows(slice_rows, row_weight, source_row[0, 0])
    got_rows, got_weight = (
        lax.all_to_all(send_rows, "slab", split_axis=0, concat_axis=0, tiled=True),
        lax.all_to_all(send_weight, "slab", split_axis=0, concat_axis=0, tiled=True),
    )
    planes = support.shape[0]
    volume_edge = support.shape[2]
    half_rows = 2 * planes * volume_edge
    summed, weights = place_rows(got_rows, got_weight, target_row[0, 0], half_rows)
    summed = summed.reshape(planes, volume_edge, volume_edge)
    weights = weights.reshape(planes, volume_edge, 2)
    tables = dft_tables(volume_edge)
    summed, weights = lax.psum((summed, weights), "grp")
    intensity = mean_of(summed, weights)
    amplitude = lax.all_to_all(jnp.sqrt(intensity), "slab", split_axis=1, concat_axis=0, tiled=True)
    share = density.shape[1]
    offset = lax.axis_index("grp") * share
    inside = support == 1
    field = density
    for step in range(ITERS):
        whole = lax.all_gather(field, "grp", axis=1, tiled=True)
        real_part, imag_part = real_forward(whole, tables, 2)
        real_part, imag_part = forward_pass(real_part, imag_part, tables, 1)
        real_part, imag_part = (
            lax.all_to_all(real_part, "slab", split_axis=1, concat_axis=0, tiled=True),
            lax.all_to_all(imag_part, "slab", split_axis=1, concat_axis=0, tiled=True),
        )
        real_part, imag_part = forward_pass(real_part, imag_part, tables, 0)
        real_part, imag_part = project(real_part, imag_part, amplitude)
        real_part, imag_part = inverse_pass(real_part, imag_part, tables, 0)
        real_part, imag_part = (
            lax.all_to_all(real_part, "slab", split_axis=0, concat_axis=1, tiled=True),
            lax.all_to_all(imag_part, "slab", split_axis=0, concat_axis=1, tiled=True),
        )
        real_part, imag_part = inverse_pass(real_part, imag_part, tables, 1)
        image = real_inverse(real_part, imag_part, tables, 2)
        image = lax.dynamic_slice_in_dim(image, offset, share, 1)
        field = jnp.where(inside, image, field - BETA * image)
    return (lax.dynamic_slice_in_dim(intensity, offset, share, 1), field)


def solution(mesh):
    return jax.shard_map(
        local,
        mesh=mesh,
        in_specs=(
            P("grp", "slab", None),
            P("grp", "slab", None),
            P("grp", "slab", None, None),
            P("grp", "slab", None, None),
            P("slab", "grp", None),
            P("slab", "grp", None),
        ),
        out_specs=(P("slab", "grp", None), P("slab", "grp", None)),
        check_vma=False,
    )
```

profile of v0, /device:TPU:1, one launch (start us, length us, event | category | flops | bytes accessed | tf_op | source)
XLA Modules:
  0.0 469.2 jit_solution(6282356553967577110)
XLA Ops:
  9.6 4.9 %convolution_convert_fusion = bf16[32,16384]{1,0:T(8,128)(2,1)S(1)} fusion(bf16[1,256,16384]{2,1,0:T(8,128)(2,1)} %param.10, bf16[1,256,32]{1,2,0:T(8,128)(2,1)} %param.11), kind=kOutput, calls=%fused_computation.28 | convolution fusion | flops 268959744 | bytes 9453568 | tf_op jit(solution)/shard_map/kr,kp->rp/dot_general | solution.py:120
  15.1 37.7 %while.26 = (s32[]{:T(128)}, bf16[8,640,128]{2,1,0:T(8,128)(2,1)}, bf16[8,640]{1,0:T(8,128)(2,1)S(1)}, s32[8,640]{1,0:T(8,128)S(1)}, bf16[4096,128]{1,0:T(8,128)...) while((s32[]{:T(128)}, bf16[8,640,128]{2,1,0:T(8,128)(2,1)}, ...), condition=%wide.region_2.3_spmd.clone, body=%wide.region_1.2_spmd.clone.sunk | while | flops 681656320 | bytes 1261993 | solution.py:88
  53.5 10.9 %all-to-all-start.1 = ((bf16[64,1,80]{2,1,0:T(2,128)(2,1)}), bf16[64,1,80]{2,1,0:T(2,128)(2,1)S(1)}, u32[]{:S(2)}, u32[]{:S(2)}) async-start(bf16[64,1,80]{2,1,0:T(2,128)(2,1)} %all_to_all.165), calls=%async_computation.1 | async-start | bytes 65536 | tf_op jit(solution)/shard_map/all_to_all | solution.py:127
  64.5 7.6 %all-to-all-done.1 = bf16[64,1,80]{2,1,0:T(2,128)(2,1)S(1)} async-done(((bf16[64,1,80]{2,1,0:T(2,128)(2,1)}), bf16[64,1,80]{2,1,0:T(2,128)(2,1)S(1)}, u32[]{:S(2)}, u32[]{:S(2)}) %all-to-all-start.1) | async-done | bytes 10272 | tf_op jit(solution)/shard_map/all_to_all | solution.py:127
  72.1 5.8 %all-to-all-start = ((bf16[64,80,128]{2,1,0:T(8,128)(2,1)}), bf16[64,80,128]{2,1,0:T(8,128)(2,1)}, u32[]{:S(2)}, u32[]{:S(2)}) async-start(bf16[64,80,128]{2,1,0:T(8,128)(2,1)} %bitcast.2), calls=%async_computation | async-start | bytes 2621440 | tf_op jit(solution)/shard_map/all_to_all | solution.py:126
  78.1 4.1 convolution_bitcast_fusion
  98.8 5.6 %all-to-all-start.2 = ((f32[4,256,256]{2,0,1:T(4,128)}), f32[4,256,256]{2,0,1:T(4,128)S(1)}, u32[]{:S(2)}, u32[]{:S(2)}) async-start(f32[4,256,256]{2,0,1:T(4,128)} %copy.224), calls=%async_computation.2 | async-start | bytes 2097152 | tf_op jit(solution)/shard_map/all_to_all | solution.py:148
  104.5 39.7 %while.27 = (s32[]{:T(128)}, f32[2048,128]{1,0:T(8,128)}, f32[2048]{0:T(1024)S(1)}, s32[8,640]{1,0:T(8,128)S(1)}, bf16[8,640,128]{2,1,0:T(8,128)(2,1)}, /*index=5*/bf16[8,640]{1,0:T(8,128)(2,1)S(1)}, s32[]{:T(128)}, s32[]{:T(128)}) while((s32[]{:T(128)}, f32[2048,128]{1,0:T(8,128)}, f32[2048]{0:T(1024)S(1)}, ...), condition=%wide.region_4.5_spmd.clone, body=%wide.region_3.4_spmd.clone.sunk | while | flops 341315584 | bytes 2308212 | solution.py:112
  110.1 4.0 fusion.364
  115.1 4.0 fusion.364
  120.1 4.0 fusion.364
  125.2 4.0 fusion.364
  135.2 4.0 fusion.364
  140.2 4.0 fusion.364
  151.2 8.8 %all-to-all-start.3 = ((f32[4,256,256]{2,0,1:T(4,128)}), f32[4,256,256]{2,0,1:T(4,128)S(1)}, u32[]{:S(2)}, u32[]{:S(2)}) async-start(f32[4,256,256]{2,0,1:T(4,128)} %copy.231), calls=%async_computation.3 | async-start | bytes 2097152 | tf_op jit(solution)/shard_map/all_to_all | solution.py:149
  160.7 21.7 %psum.15 = f32[4,256,2]{1,0,2:T(4,128)S(1)} all-reduce(f32[4,256,2]{1,0,2:T(4,128)S(1)} %copy.215), channel_id=1, replica_groups=mesh['grp'=2,'slab'=64] {'grp'}, use_global_device_ids=true, to_apply=%region_6.7 | all-reduce | flops 2048 | bytes 16384 | tf_op jit(solution)/shard_map/psum | solution.py:136
  186.1 17.0 %all-reduce.2.cloned.1.call-done = f32[4,256,256]{2,1,0:T(8,128)} async-done(((f32[4,256,256]{2,1,0:T(8,128)}), f32[4,256,256]{2,1,0:T(8,128)}) %all-reduce.2.cloned.1.call-update) | async-done | bytes 1048592 | tf_op jit(solution)/shard_map/psum | solution.py:136
  207.5 8.5 %all-to-all-start.4 = ((f32[4,256,256]{2,0,1:T(4,128)}), f32[4,256,256]{2,0,1:T(4,128)}, u32[]{:S(2)}, u32[]{:S(2)}) async-start(f32[4,256,256]{2,0,1:T(4,128)} %copy.234), calls=%async_computation.4 | async-start | bytes 2097152 | tf_op jit(solution)/shard_map/all_to_all | solution.py:138
  224.2 9.9 %all-to-all-done.4 = f32[4,256,256]{2,0,1:T(4,128)} async-done(((f32[4,256,256]{2,0,1:T(4,128)}), f32[4,256,256]{2,0,1:T(4,128)}, u32[]{:S(2)}, u32[]{:S(2)}) %all-to-all-start.4) | async-done | bytes 1048608 | tf_op jit(solution)/shard_map/all_to_all | solution.py:138
  244.5 5.5 %all-to-all-start.6 = ((f32[256,4,256]{2,1,0:T(4,128)}), f32[256,4,256]{2,1,0:T(4,128)}, u32[]{:S(2)}, u32[]{:S(2)}) async-start(f32[256,4,256]{2,1,0:T(4,128)} %copy.246), calls=%async_computation.6 | async-start | bytes 2097152 | tf_op jit(solution)/shard_map/all_to_all | solution.py:156
  256.1 12.2 %all-to-all-done.6 = f32[256,4,256]{2,1,0:T(4,128)} async-done(((f32[256,4,256]{2,1,0:T(4,128)}), f32[256,4,256]{2,1,0:T(4,128)}, u32[]{:S(2)}, u32[]{:S(2)}) %all-to-all-start.6) | async-done | bytes 1048608 | tf_op jit(solution)/shard_map/all_to_all | solution.py:156
  268.3 5.4 %all-to-all-start.5 = ((f32[256,4,256]{2,1,0:T(4,128)}), f32[256,4,256]{2,1,0:T(4,128)}, u32[]{:S(2)}, u32[]{:S(2)}) async-start(f32[256,4,256]{2,1,0:T(4,128)} %copy.240), calls=%async_computation.5 | async-start | bytes 2097152 | tf_op jit(solution)/shard_map/all_to_all | solution.py:155
  277.8 14.3 %all-to-all-done.5 = f32[256,4,256]{2,1,0:T(4,128)} async-done(((f32[256,4,256]{2,1,0:T(4,128)}), f32[256,4,256]{2,1,0:T(4,128)}, u32[]{:S(2)}, u32[]{:S(2)}) %all-to-all-start.5) | async-done | bytes 1048608 | tf_op jit(solution)/shard_map/all_to_all | solution.py:155
  304.9 21.3 %all-gather.5.cloned.1.call-done = f32[4,256,256]{2,1,0:T(8,128)} async-done(((f32[4,128,256]{2,1,0:T(8,128)}), f32[4,256,256]{2,1,0:T(8,128)}) %all-gather.5.cloned.1.call-update) | async-done | bytes 1048592 | tf_op jit(solution)/shard_map/all_gather | solution.py:144
  337.3 8.3 %all-to-all-start.7 = ((f32[4,256,256]{2,0,1:T(4,128)}), f32[4,256,256]{2,0,1:T(4,128)}, u32[]{:S(2)}, u32[]{:S(2)}) async-start(f32[4,256,256]{2,0,1:T(4,128)} %copy.256), calls=%async_computation.7 | async-start | bytes 2097152 | tf_op jit(solution)/shard_map/all_to_all | solution.py:148
  351.3 12.5 %all-to-all-done.7 = f32[4,256,256]{2,0,1:T(4,128)} async-done(((f32[4,256,256]{2,0,1:T(4,128)}), f32[4,256,256]{2,0,1:T(4,128)}, u32[]{:S(2)}, u32[]{:S(2)}) %all-to-all-start.7) | async-done | bytes 1048608 | tf_op jit(solution)/shard_map/all_to_all | solution.py:148
  363.8 5.1 %all-to-all-start.8 = ((f32[4,256,256]{2,0,1:T(4,128)}), f32[4,256,256]{2,0,1:T(4,128)S(1)}, u32[]{:S(2)}, u32[]{:S(2)}) async-start(f32[4,256,256]{2,0,1:T(4,128)} %copy.261), calls=%async_computation.8 | async-start | bytes 2097152 | tf_op jit(solution)/shard_map/all_to_all | solution.py:149
  372.9 14.0 %all-to-all-done.8 = f32[4,256,256]{2,0,1:T(4,128)S(1)} async-done(((f32[4,256,256]{2,0,1:T(4,128)}), f32[4,256,256]{2,0,1:T(4,128)S(1)}, u32[]{:S(2)}, u32[]{:S(2)}) %all-to-all-start.8) | async-done | bytes 1048608 | tf_op jit(solution)/shard_map/all_to_all | solution.py:149
  404.2 5.4 %all-to-all-start.10 = ((f32[256,4,256]{2,1,0:T(4,128)}), f32[256,4,256]{2,1,0:T(4,128)}, u32[]{:S(2)}, u32[]{:S(2)}) async-start(f32[256,4,256]{2,1,0:T(4,128)} %copy.274), calls=%async_computation.10 | async-start | bytes 2097152 | tf_op jit(solution)/shard_map/all_to_all | solution.py:156
  415.8 12.2 %all-to-all-done.10 = f32[256,4,256]{2,1,0:T(4,128)} async-done(((f32[256,4,256]{2,1,0:T(4,128)}), f32[256,4,256]{2,1,0:T(4,128)}, u32[]{:S(2)}, u32[]{:S(2)}) %all-to-all-start.10) | async-done | bytes 1048608 | tf_op jit(solution)/shard_map/all_to_all | solution.py:156
  428.0 4.9 %all-to-all-start.9 = ((f32[256,4,256]{2,1,0:T(4,128)}), f32[256,4,256]{2,1,0:T(4,128)S(1)}, u32[]{:S(2)}, u32[]{:S(2)}) async-start(f32[256,4,256]{2,1,0:T(4,128)} %copy.268), calls=%async_computation.9 | async-start | bytes 2097152 | tf_op jit(solution)/shard_map/all_to_all | solution.py:155
  437.3 13.8 %all-to-all-done.9 = f32[256,4,256]{2,1,0:T(4,128)S(1)} async-done(((f32[256,4,256]{2,1,0:T(4,128)}), f32[256,4,256]{2,1,0:T(4,128)S(1)}, u32[]{:S(2)}, u32[]{:S(2)}) %all-to-all-start.9) | async-done | bytes 1048608 | tf_op jit(solution)/shard_map/all_to_all | solution.py:155
  (198 shorter events, 190.5 us)
Async XLA Ops:
  7.2 70.9 %all-gather.3.cloned.1.call-start = ((), (), s32[]{:S(2)}) async-start(), calls=%async_computation.12 | async-start | bytes 1572864 | tf_op jit(solution)/shard_map/all_gather | solution.py:144
  15.1 49.3 %copy-start.10 = (s32[1,1,64,80]{3,2,1,0:T(8,128)S(1)}, s32[1,1,64,80]{3,2,1,0:T(8,128)}, u32[]{:S(2)}) copy-start(s32[1,1,64,80]{3,2,1,0:T(8,128)} %param.13) | copy-start | bytes 61444
  53.5 18.6 %all-to-all-start.1 = ((bf16[64,1,80]{2,1,0:T(2,128)(2,1)}), bf16[64,1,80]{2,1,0:T(2,128)(2,1)S(1)}, u32[]{:S(2)}, u32[]{:S(2)}) async-start(bf16[64,1,80]{2,1,0:T(2,128)(2,1)} %all_to_all.165), calls=%async_computation.1 | async-start | bytes 65536 | tf_op jit(solution)/shard_map/all_to_all | solution.py:127
  72.1 26.8 %all-to-all-start = ((bf16[64,80,128]{2,1,0:T(8,128)(2,1)}), bf16[64,80,128]{2,1,0:T(8,128)(2,1)}, u32[]{:S(2)}, u32[]{:S(2)}) async-start(bf16[64,80,128]{2,1,0:T(8,128)(2,1)} %bitcast.2), calls=%async_computation | async-start | bytes 2621440 | tf_op jit(solution)/shard_map/all_to_all | solution.py:126
  78.1 6.9 %copy-start.5 = (f32[4,256,256]{2,1,0:T(8,128)S(1)}, f32[4,256,256]{2,1,0:T(8,128)}, u32[]{:S(2)}) copy-start(f32[4,256,256]{2,1,0:T(8,128)} %all-gather.3.cloned.1.call-done) | copy-start | bytes 3145732
  98.8 52.3 %all-to-all-start.2 = ((f32[4,256,256]{2,0,1:T(4,128)}), f32[4,256,256]{2,0,1:T(4,128)S(1)}, u32[]{:S(2)}, u32[]{:S(2)}) async-start(f32[4,256,256]{2,0,1:T(4,128)} %copy.224), calls=%async_computation.2 | async-start | bytes 2097152 | tf_op jit(solution)/shard_map/all_to_all | solution.py:148
  104.4 98.6 %all-reduce.2.cloned.1.call-start = ((), (), s32[]{:S(2)}) async-start(), calls=%async_computation.11 | async-start | bytes 2097152 | tf_op jit(solution)/shard_map/psum | solution.py:136
  151.2 34.3 %all-to-all-start.3 = ((f32[4,256,256]{2,0,1:T(4,128)}), f32[4,256,256]{2,0,1:T(4,128)S(1)}, u32[]{:S(2)}, u32[]{:S(2)}) async-start(f32[4,256,256]{2,0,1:T(4,128)} %copy.231), calls=%async_computation.3 | async-start | bytes 2097152 | tf_op jit(solution)/shard_map/all_to_all | solution.py:149
  186.1 30.0 %copy-start = (f32[256,4,256]{2,0,1:T(8,128)}, f32[256,4,256]{2,0,1:T(8,128)S(1)}, u32[]{:S(2)}) copy-start(f32[256,4,256]{2,0,1:T(8,128)S(1)} %all_to_all.136) | copy-start | bytes 3145732
  207.5 26.5 %all-to-all-start.4 = ((f32[4,256,256]{2,0,1:T(4,128)}), f32[4,256,256]{2,0,1:T(4,128)}, u32[]{:S(2)}, u32[]{:S(2)}) async-start(f32[4,256,256]{2,0,1:T(4,128)} %copy.234), calls=%async_computation.4 | async-start | bytes 2097152 | tf_op jit(solution)/shard_map/all_to_all | solution.py:138
  218.1 4.1 copy-start.1
  244.5 23.8 %all-to-all-start.6 = ((f32[256,4,256]{2,1,0:T(4,128)}), f32[256,4,256]{2,1,0:T(4,128)}, u32[]{:S(2)}, u32[]{:S(2)}) async-start(f32[256,4,256]{2,1,0:T(4,128)} %copy.246), calls=%async_computation.6 | async-start | bytes 2097152 | tf_op jit(solution)/shard_map/all_to_all | solution.py:156
  268.3 23.8 %all-to-all-start.5 = ((f32[256,4,256]{2,1,0:T(4,128)}), f32[256,4,256]{2,1,0:T(4,128)}, u32[]{:S(2)}, u32[]{:S(2)}) async-start(f32[256,4,256]{2,1,0:T(4,128)} %copy.240), calls=%async_computation.5 | async-start | bytes 2097152 | tf_op jit(solution)/shard_map/all_to_all | solution.py:155
  273.7 52.5 %all-gather.5.cloned.1.call-start = ((), (), s32[]{:S(2)}) async-start(), calls=%async_computation.13 | async-start | bytes 1572864 | tf_op jit(solution)/shard_map/all_gather | solution.py:144
  299.8 4.2 copy-start.8
  299.8 4.2 copy-start.9
  326.3 5.3 %copy-start.6 = (f32[4,256,256]{2,1,0:T(8,128)S(1)}, f32[4,256,256]{2,1,0:T(8,128)}, u32[]{:S(2)}) copy-start(f32[4,256,256]{2,1,0:T(8,128)} %all-gather.5.cloned.1.call-done) | copy-start | bytes 3145732
  337.3 26.5 %all-to-all-start.7 = ((f32[4,256,256]{2,0,1:T(4,128)}), f32[4,256,256]{2,0,1:T(4,128)}, u32[]{:S(2)}, u32[]{:S(2)}) async-start(f32[4,256,256]{2,0,1:T(4,128)} %copy.256), calls=%async_computation.7 | async-start | bytes 2097152 | tf_op jit(solution)/shard_map/all_to_all | solution.py:148
  363.8 23.1 %all-to-all-start.8 = ((f32[4,256,256]{2,0,1:T(4,128)}), f32[4,256,256]{2,0,1:T(4,128)S(1)}, u32[]{:S(2)}, u32[]{:S(2)}) async-start(f32[4,256,256]{2,0,1:T(4,128)} %copy.261), calls=%async_computation.8 | async-start | bytes 2097152 | tf_op jit(solution)/shard_map/all_to_all | solution.py:149
  389.7 2.0 copy-start.2
  393.7 2.0 copy-start.3
  404.2 23.8 %all-to-all-start.10 = ((f32[256,4,256]{2,1,0:T(4,128)}), f32[256,4,256]{2,1,0:T(4,128)}, u32[]{:S(2)}, u32[]{:S(2)}) async-start(f32[256,4,256]{2,1,0:T(4,128)} %copy.274), calls=%async_computation.10 | async-start | bytes 2097152 | tf_op jit(solution)/shard_map/all_to_all | solution.py:156
  414.2 18.7 %copy-start.7 = (f32[4,256,256]{2,1,0:T(8,128)S(1)}, f32[4,256,256]{2,1,0:T(8,128)}, u32[]{:S(2)}) copy-start(f32[4,256,256]{2,1,0:T(8,128)} %get-tuple-element.150) | copy-start | bytes 3145732
  428.0 23.1 %all-to-all-start.9 = ((f32[256,4,256]{2,1,0:T(4,128)}), f32[256,4,256]{2,1,0:T(4,128)S(1)}, u32[]{:S(2)}, u32[]{:S(2)}) async-start(f32[256,4,256]{2,1,0:T(4,128)} %copy.268), calls=%async_computation.9 | async-start | bytes 2097152 | tf_op jit(solution)/shard_map/all_to_all | solution.py:155
  457.6 4.0 copy-start.4
Sparse Core Ops, SparseCore 0:
  9.6 28.4 all-gather.2
  146.8 56.2 all-reduce.1
  305.0 21.1 all-gather.4
where the time goes:
time: 477 us; the launch traced here: 469 us
  matrix products  171 us (36%)
  waiting for transfers between devices  140 us (29%)
  starting transfers between devices  74.8 us (16%)
  local copies, waits for them, and re-layouts  40.9 us (9%)
  blocking collectives  21.7 us (5%)
  between operations  14.7 us (3%)
  other arithmetic  5.7 us (1%)
    dot_general x40, matrix products, along(): return jnp.einsum(form, field, table, precision=lax.Precision.HIGHEST)  90.4 us
    dot_general x8, matrix products, add_block(): jnp.einsum('sh,sd->hd', onehot, rows, preferred_element_type=jnp.float32)  31.5 us
    all_to_all x2, waiting for transfers between devices, local(): lax.all_to_all(real_part, 'slab', split_axis=0, concat_axis=1, tiled=True)  28.1 us
    all_to_all x2, waiting for transfers between devices, local(): lax.all_to_all(imag_part, 'slab', split_axis=0, concat_axis=1, tiled=True)  24.3 us
    psum x1, blocking collectives, local(): summed, weights = lax.psum((summed, weights), 'grp')  21.7 us
    all_gather x2, waiting for transfers between devices, local(): whole = lax.all_gather(field, 'grp', axis=1, tiled=True)  21.4 us
    dot_general x8, matrix products, one_block(): jnp.dot(onehot, slice_rows, preferred_element_type=jnp.float32)  19.9 us
    psum x1, waiting for transfers between devices, local(): summed, weights = lax.psum((summed, weights), 'grp')  17 us
  transfers between devices with their start and end apart: 14, of which 12 were waited for; matrix products, arithmetic and copies ran while one was open for 31% of the time, Pallas kernels for 0%

commit v1 on v0

v1 whole, which is shorter than its diff:
```python
import functools

import jax
import jax.numpy as jnp
import ml_dtypes
import numpy as np
from jax import lax
from jax.experimental import pallas as pl
from jax.experimental.pallas import tpu as pltpu
from jax.sharding import PartitionSpec as P

N = 256
HALF = N // 2
PLANES = 4
SLABS = 64
DEVS = 128
CAP = 80
ROWS = 4096
BETA = 0.9
SOFTEN = 0.25
BOTH = ("grp", "slab")
VMEM = 48 * 1024 * 1024


def split_table(table):
    high = table.astype(np.float32).astype(ml_dtypes.bfloat16)
    low = (table - high.astype(np.float64)).astype(np.float32).astype(ml_dtypes.bfloat16)
    return (jnp.asarray(high), jnp.asarray(low))


def phase(rows, columns):
    angle = 2.0 * np.pi / N * ((rows[:, None] * columns[None, :]) % N)
    return (np.cos(angle) / np.sqrt(N), np.sin(angle) / np.sqrt(N))


def complex_table(cos, sin):
    return np.block([[cos, -sin], [sin, cos]])


@functools.cache
def tables():
    z = np.arange(N)
    kz = np.arange(HALF)
    cos, sin = phase(z, kz)
    nyquist = np.cos(np.pi * z) / np.sqrt(N)
    forward_z = np.concatenate([cos, -sin], axis=1)
    forward_z[:, HALF] = nyquist
    inverse_z = np.concatenate([2.0 * cos.T, -2.0 * sin.T], axis=0)
    inverse_z[0] = 1.0 / np.sqrt(N)
    inverse_z[HALF] = nyquist
    y = np.arange(HALF)
    first = np.arange(DEVS)
    second = np.where(first == 0, HALF, N - first)
    cos_a, sin_a = phase(first, y)
    cos_b, sin_b = phase(second, y)
    forward_y = np.block([[cos_a, sin_a], [-sin_a, cos_a], [cos_b, sin_b], [-sin_b, cos_b]])
    inverse_y = np.block([[cos_a.T, -sin_a.T, cos_b.T, -sin_b.T], [sin_a.T, cos_a.T, sin_b.T, cos_b.T]])
    order = (np.arange(PLANES)[:, None] + PLANES * np.arange(SLABS)[None, :]).reshape(-1)
    cos, sin = phase(order, order)
    forward_x = complex_table(cos, -sin)
    cos_m, sin_m = phase(-order, order)
    mirror_x = complex_table(cos_m, -sin_m)
    inverse_x = complex_table(cos, sin)
    place = np.argsort(order)
    flip_x = np.zeros((N, N))
    flip_x[np.arange(N), place[(-order) % N]] = 1.0
    flip_z = np.zeros((N, N))
    flip_z[(-z) % N, z] = 1.0
    flip_y = np.zeros((2, HALF, HALF))
    flip_y[0] = np.eye(HALF)
    flip_y[1][y, (-y) % HALF] = 1.0
    return dict(
        forward_z=split_table(forward_z),
        inverse_z=split_table(inverse_z),
        forward_y=split_table(forward_y),
        inverse_y=split_table(inverse_y),
        forward_x=split_table(np.concatenate([forward_x, mirror_x], axis=0)),
        inverse_x=split_table(inverse_x),
        flip_x=jnp.asarray(flip_x.astype(ml_dtypes.bfloat16)),
        flip_z=jnp.asarray(flip_z.astype(ml_dtypes.bfloat16)),
        flip_y=jnp.asarray(flip_y.astype(ml_dtypes.bfloat16)),
    )


def halves(values):
    high = values.astype(jnp.bfloat16)
    return (high, (values - high.astype(jnp.float32)).astype(jnp.bfloat16))


def dot(left, right):
    return jnp.dot(left, right, preferred_element_type=jnp.float32)


def table_times(high, low, values):
    a, b = halves(values)
    return dot(high, a) + (dot(high, b) + dot(low, a))


def times_table(values, high, low):
    a, b = halves(values)
    return dot(a, high) + (dot(b, high) + dot(a, low))


def call(kernel, out_shape, **kwargs):
    return pl.pallas_call(
        kernel,
        out_shape=out_shape,
        compiler_params=pltpu.CompilerParams(vmem_limit_bytes=VMEM),
        **kwargs,
    )


def spec_vmem(count):
    return [pl.BlockSpec(memory_space=pltpu.VMEM)] * count


def smem():
    return pl.BlockSpec(memory_space=pltpu.SMEM)


OWNERS = 8
SLOTS = OWNERS * CAP
SEND = 88
DEEP = 1024


def gather_kernel(weight_ref, column_ref, table_ref, rows_ref, out_ref):
    source = column_ref[...]
    low = source & (DEEP - 1)
    high = source >> 10
    onehot = (low == lax.broadcasted_iota(jnp.int32, (SLOTS, DEEP), 1)).astype(jnp.bfloat16)
    rows = jnp.concatenate([rows_ref[q * DEEP : (q + 1) * DEEP] for q in range(4)], axis=1)
    wide = dot(onehot, rows)
    picked = jnp.where(high == 0, wide[:, :128], 0.0)
    for q in range(1, 4):
        picked = jnp.where(high == q, wide[:, q * 128 : (q + 1) * 128], picked)
    orientation = table_ref[...] >> 7
    weights = jnp.zeros((OWNERS, 128), jnp.float32)
    for r in range(32):
        weights = jnp.where(orientation == r, weight_ref[r], weights)
    top = lax.broadcasted_iota(jnp.int32, (8, 128), 0) == 0
    for o in range(OWNERS):
        last = jnp.where(top, weights[o : o + 1], 0.0)
        both = jnp.concatenate([picked[o * CAP : (o + 1) * CAP], last], axis=0)
        out_ref[o] = both.astype(jnp.bfloat16)


def gather_rows(weight, column, table, rows):
    return call(
        gather_kernel,
        jax.ShapeDtypeStruct((SLABS, SEND, 128), jnp.bfloat16),
        grid=(SLABS // OWNERS,),
        in_specs=[
            smem(),
            pl.BlockSpec((SLOTS, 1), lambda i: (i, 0)),
            pl.BlockSpec((OWNERS, 128), lambda i: (i, 0)),
            pl.BlockSpec((ROWS, 128), lambda i: (0, 0)),
        ],
        out_specs=pl.BlockSpec((OWNERS, SEND, 128), lambda i: (i, 0, 0)),
    )(weight, column, table, rows)


PAY = 24


def place_kernel(got_ref, column_ref, row_ref, out_ref, sum_ref, weight_ref):
    step = pl.program_id(0)

    @pl.when(step == 0)
    def start():
        sum_ref[...] = jnp.zeros_like(sum_ref)
        weight_ref[...] = jnp.zeros_like(weight_ref)

    column = column_ref[...]
    row = row_ref[0]
    rows = jnp.concatenate([got_ref[s, :CAP] for s in range(OWNERS)], axis=0)
    onehot = (lax.broadcasted_iota(jnp.int32, (512, SLOTS), 0) == (row & 511)).astype(jnp.bfloat16)
    quarter = column >> 9
    wide = jnp.concatenate([jnp.where(quarter == q, rows, jnp.bfloat16(0)) for q in range(4)], axis=1)
    sum_ref[...] += dot(onehot, wide)
    last = jnp.concatenate([got_ref[s, CAP:SEND].astype(jnp.float32)[:1] for s in range(OWNERS)], axis=0)
    turned = jnp.concatenate([last, jnp.zeros((120, 128), jnp.float32)], axis=0).T
    weights = jnp.concatenate([turned[:CAP, s : s + 1] for s in range(OWNERS)], axis=0)
    lane = lax.broadcasted_iota(jnp.int32, (SLOTS, 128), 1)
    right = jnp.where(lane == (column & 15), weights, 0.0).astype(jnp.bfloat16)
    left = (lax.broadcasted_iota(jnp.int32, (DEVS, SLOTS), 0) == (row >> 4)).astype(jnp.bfloat16)
    weight_ref[...] += dot(left, right)

    @pl.when(step == pl.num_programs(0) - 1)
    def end():
        for q in range(4):
            out_ref[q * 32 : (q + 1) * 32, :16, :] = sum_ref[:, q * 128 : (q + 1) * 128].reshape(32, 16, 128)
        out_ref[:, 16:, :] = jnp.broadcast_to(weight_ref[...][:, None, :], (DEVS, 8, 128))


def place_rows(got, column, row):
    return call(
        place_kernel,
        jax.ShapeDtypeStruct((DEVS, PAY, 128), jnp.float32),
        grid=(SLABS // OWNERS,),
        in_specs=[
            pl.BlockSpec((OWNERS, SEND, 128), lambda i: (i, 0, 0)),
            pl.BlockSpec((SLOTS, 1), lambda i: (i, 0)),
            pl.BlockSpec((1, 1, SLOTS), lambda i: (i, 0, 0)),
        ],
        out_specs=pl.BlockSpec((DEVS, PAY, 128), lambda i: (0, 0, 0)),
        scratch_shapes=[pltpu.VMEM((512, 512), jnp.float32), pltpu.VMEM((DEVS, 128), jnp.float32)],
    )(got, column, row)


def intensity_kernel(group_ref, own_ref, other_ref, flip_ref, out_ref):
    group = group_ref[0]
    weights = own_ref[:, 16, :] + other_ref[:, 8, :]
    divisor = jnp.maximum(jnp.where(group == 0, weights[:, :8], weights[:, 8:16]), 1.0)
    parts = []
    for q in range(8):
        total = jnp.where(group == 0, own_ref[:, q, :], own_ref[:, 8 + q, :]) + other_ref[:, q, :]
        parts.append(total / divisor[:, q : q + 1])
    wide = jnp.concatenate(parts, axis=1)
    flip = jnp.where(group == 0, flip_ref[0], flip_ref[1])
    high = wide.astype(jnp.bfloat16)
    rest = wide - high.astype(jnp.float32)
    middle = rest.astype(jnp.bfloat16)
    least = (rest - middle.astype(jnp.float32)).astype(jnp.bfloat16)
    turned = dot(flip, high) + (dot(flip, middle) + dot(flip, least))
    for x in range(PLANES):
        out_ref[x] = turned[:, x * N : (x + 1) * N]


def intensity_of(group, own, other, flip):
    return call(
        intensity_kernel,
        jax.ShapeDtypeStruct((PLANES, HALF, N), jnp.float32),
        in_specs=[smem()] + spec_vmem(3),
        out_specs=pl.BlockSpec(memory_space=pltpu.VMEM),
    )(group, own, other, flip)


def amplitude_kernel(first_ref, got_ref, flip_x_ref, flip_z_ref, out_ref, nyquist_ref):
    first = first_ref[0]
    divisor = jnp.maximum(got_ref[:SLABS, 16, :] + got_ref[SLABS:, 16, :], 1.0)
    amplitude = []
    for pm in range(2):
        columns = []
        for zh in range(2):
            planes = []
            for x in range(PLANES):
                q = (pm * PLANES + x) * 2 + zh
                total = got_ref[:SLABS, q, :] + got_ref[SLABS:, q, :]
                planes.append(jnp.sqrt(total / divisor[:, q : q + 1]))
            columns.append(jnp.concatenate(planes, axis=0))
        amplitude.append(jnp.concatenate(columns, axis=1))
    flip_x = flip_x_ref[...]
    flip_z = flip_z_ref[...]
    mirrored = []
    for pm in range(2):
        high, low = halves(amplitude[pm])
        high = dot(flip_x, high).astype(jnp.bfloat16)
        low = dot(flip_x, low).astype(jnp.bfloat16)
        mirrored.append(dot(high, flip_z) + dot(low, flip_z))
    for pm in range(2):
        partner = jnp.where(first == 1, mirrored[pm], mirrored[1 - pm])
        even = 0.5 * (amplitude[pm] + partner)
        out_ref[:, pm * HALF : (pm + 1) * HALF] = even[:, :HALF]
        nyquist_ref[:, pm * HALF : (pm + 1) * HALF] = even[:, HALF:]


def amplitude_of(first, got, flip_x, flip_z):
    return call(
        amplitude_kernel,
        (jax.ShapeDtypeStruct((N, N), jnp.float32),) * 2,
        in_specs=[smem()] + spec_vmem(3),
        out_specs=tuple(spec_vmem(2)),
    )(first, got, flip_x, flip_z)


def send_forward(field, forward_z, forward_y, out_ref):
    partly = times_table(field, forward_z[0][...], forward_z[1][...])
    columns = []
    for x in range(PLANES):
        block = partly[x * HALF : (x + 1) * HALF]
        columns.append(jnp.concatenate([block[:, :HALF], block[:, HALF:]], axis=0))
    result = table_times(forward_y[0][...], forward_y[1][...], jnp.concatenate(columns, axis=1))
    for x in range(PLANES):
        for q in range(4):
            out_ref[:, x * 4 + q, :] = result[q * DEVS : (q + 1) * DEVS, x * HALF : (x + 1) * HALF]


def image_from(got_ref, inverse_y, inverse_z):
    columns = []
    for x in range(PLANES):
        columns.append(jnp.concatenate([got_ref[:, x * 4 + q, :] for q in range(4)], axis=0))
    partly = table_times(inverse_y[0][...], inverse_y[1][...], jnp.concatenate(columns, axis=1))
    rows = []
    for x in range(PLANES):
        block = partly[:, x * HALF : (x + 1) * HALF]
        rows.append(jnp.concatenate([block[:HALF], block[HALF:]], axis=1))
    return times_table(jnp.concatenate(rows, axis=0), inverse_z[0][...], inverse_z[1][...])


def updated(image, support_ref, density_ref):
    support = support_ref[...].reshape(PLANES * HALF, N)
    density = density_ref[...].reshape(PLANES * HALF, N)
    return jnp.where(support == 1, image, density - BETA * image)


def first_kernel(density_ref, zh, zl, yh, yl, out_ref):
    send_forward(density_ref[...].reshape(PLANES * HALF, N), (zh, zl), (yh, yl), out_ref)


def middle_kernel(got_ref, support_ref, density_ref, iyh, iyl, izh, izl, zh, zl, yh, yl, field_ref, out_ref):
    field = updated(image_from(got_ref, (iyh, iyl), (izh, izl)), support_ref, density_ref)
    field_ref[...] = field.reshape(PLANES, HALF, N)
    send_forward(field, (zh, zl), (yh, yl), out_ref)


def last_kernel(got_ref, support_ref, density_ref, iyh, iyl, izh, izl, field_ref):
    field = updated(image_from(got_ref, (iyh, iyl), (izh, izl)), support_ref, density_ref)
    field_ref[...] = field.reshape(PLANES, HALF, N)


PACKET = jax.ShapeDtypeStruct((DEVS, 16, 128), jnp.float32)
FIELD = jax.ShapeDtypeStruct((PLANES, HALF, N), jnp.float32)


def first_field(density, t):
    return call(first_kernel, PACKET, in_specs=spec_vmem(5), out_specs=spec_vmem(1)[0])(
        density, *t["forward_z"], *t["forward_y"]
    )


def middle_field(got, support, density, t):
    return call(middle_kernel, (FIELD, PACKET), in_specs=spec_vmem(11), out_specs=tuple(spec_vmem(2)))(
        got, support, density, *t["inverse_y"], *t["inverse_z"], *t["forward_z"], *t["forward_y"]
    )


def last_field(got, support, density, t):
    return call(last_kernel, FIELD, in_specs=spec_vmem(7), out_specs=spec_vmem(1)[0])(
        got, support, density, *t["inverse_y"], *t["inverse_z"]
    )


def project_kernel(place_ref, got_ref, amplitude_ref, nyquist_ref, xh, xl, ixh, ixl, out_ref):
    first = place_ref[0]
    sign = place_ref[1].astype(jnp.float32)
    lanes = []
    for pm in range(2):
        parts = []
        for c in range(2):
            for x in range(PLANES):
                q = x * 4 + pm * 2 + c
                parts.append(got_ref[:SLABS, q, :] + sign * got_ref[SLABS:, q, :])
        lanes.append(jnp.concatenate(parts, axis=0))
    spectrum = table_times(xh[...], xl[...], jnp.concatenate(lanes, axis=1))
    real = spectrum[:N]
    imag = spectrum[N : 2 * N]
    mirror = spectrum[2 * N :]
    mirror = jnp.where(first == 1, mirror, jnp.concatenate([mirror[:, HALF:], mirror[:, :HALF]], axis=1))
    mirror_real = mirror[:N]
    mirror_imag = mirror[N:]
    amplitude = amplitude_ref[...]
    scale = amplitude * lax.rsqrt(real * real + imag * imag + SOFTEN)
    zero_real = 0.5 * (real + mirror_real)
    zero_imag = 0.5 * (imag - mirror_imag)
    top_real = 0.5 * (imag + mirror_imag)
    top_imag = 0.5 * (mirror_real - real)
    zero_scale = amplitude * lax.rsqrt(zero_real * zero_real + zero_imag * zero_imag + SOFTEN)
    top_scale = nyquist_ref[...] * lax.rsqrt(top_real * top_real + top_imag * top_imag + SOFTEN)
    packed = (lax.broadcasted_iota(jnp.int32, (N, N), 1) & (HALF - 1)) == 0
    new_real = jnp.where(packed, zero_scale * zero_real - top_scale * top_imag, scale * real)
    new_imag = jnp.where(packed, zero_scale * zero_imag + top_scale * top_real, scale * imag)
    result = table_times(ixh[...], ixl[...], jnp.concatenate([new_real, new_imag], axis=0))
    for pm in range(2):
        for c in range(2):
            for x in range(PLANES):
                q = x * 4 + pm * 2 + c
                start = (c * PLANES + x) * SLABS
                part = result[start : start + SLABS, pm * HALF : (pm + 1) * HALF]
                out_ref[:SLABS, q, :] = part
                out_ref[SLABS:, q, :] = sign * part


def projected(place, got, amplitude, nyquist, t):
    return call(project_kernel, PACKET, in_specs=[smem()] + spec_vmem(7), out_specs=spec_vmem(1)[0])(
        place, got, amplitude, nyquist, *t["forward_x"], *t["inverse_x"]
    )


def exchange(packet):
    sent = lax.all_to_all(packet.astype(jnp.float16), BOTH, split_axis=0, concat_axis=0, tiled=True)
    return sent.astype(jnp.float32)


def local(patterns, probabilities, source_row, target_row, support, density):
    t = tables()
    group = lax.axis_index("grp")
    device = group * SLABS + lax.axis_index("slab")
    place = jnp.stack([(device == 0).astype(jnp.int32), 1 - 2 * (device & 1)])

    got_field = exchange(first_field(density, t))

    block = probabilities[0]
    slices = jnp.einsum("kr,kp->rp", block, patterns[0], preferred_element_type=jnp.float32)
    rows = slices.astype(jnp.bfloat16).reshape(ROWS, 128)
    weight = jnp.sum(block.astype(jnp.float32), axis=0).astype(jnp.bfloat16).astype(jnp.float32)
    source = source_row[0, 0]
    send = gather_rows(
        weight,
        source.reshape(-1, 1),
        jnp.pad(source, ((0, 0), (0, 128 - CAP)), constant_values=-1),
        rows,
    )
    got = lax.all_to_all(send, "slab", split_axis=0, concat_axis=0, tiled=True)

    target = target_row[0, 0]
    zh = target & 1
    y = (target >> 1) & (N - 1)
    x = target >> 9
    pm = (y >= HALF).astype(jnp.int32)
    j = jnp.where(pm == 1, (N - y) & (HALF - 1), y)
    target = j * 16 + (pm * PLANES + x) * 2 + zh
    sums = place_rows(got, target.reshape(-1, 1), target.reshape(SLABS // OWNERS, 1, SLOTS))

    narrow = sums.astype(jnp.float16)
    got_sums = lax.all_to_all(narrow, BOTH, split_axis=0, concat_axis=0, tiled=True).astype(jnp.float32)
    theirs = lax.dynamic_slice_in_dim(narrow, (1 - group) * 8, 8, 1)
    other = lax.ppermute(jnp.concatenate([theirs, narrow[:, 16:]], axis=1), "grp", [(0, 1), (1, 0)])
    intensity = intensity_of(group.reshape(1), sums, other.astype(jnp.float32), t["flip_y"])

    amplitude, nyquist = amplitude_of(place, got_sums, t["flip_x"], t["flip_z"])
    back = exchange(projected(place, got_field, amplitude, nyquist, t))
    field, packet = middle_field(back, support, density, t)
    back = exchange(projected(place, exchange(packet), amplitude, nyquist, t))
    return (intensity, last_field(back, support, field, t))


def solution(mesh):
    return jax.shard_map(
        local,
        mesh=mesh,
        in_specs=(
            P("grp", "slab", None),
            P("grp", "slab", None),
            P("grp", "slab", None, None),
            P("grp", "slab", None, None),
            P("slab", "grp", None),
            P("slab", "grp", None),
        ),
        out_specs=(P("slab", "grp", None), P("slab", "grp", None)),
        check_vma=False,
    )
```

time: 477 us -> 188 us (0.39); the launches traced: 469 us -> 187 us
  matrix products: 171 us -> 5.94 us
  waiting for transfers between devices: 140 us -> 43.8 us
  Pallas kernels: 0 us -> 36.1 us
  starting transfers between devices: 74.8 us -> 41.4 us
  local copies, waits for them, and re-layouts: 40.9 us -> 24.3 us
  between operations: 14.7 us -> 1.29 us
  other arithmetic: 5.7 us -> 16.5 us
    dot_general x73 -> x1, matrix products: 171 us -> 5.94 us  [local(): jnp.einsum('kr,kp->rp', block, patterns[0], preferred_element_type=jnp.fl...]
    all_to_all x11 -> x5, waiting for transfers between devices: 101 us -> 43.8 us  [the longest x3 17.7 us: exchange(): lax.all_to_all(packet.astype(jnp.float16), BOTH, split_axis=0, concat_axi...]
    pallas_call x0 -> x9, Pallas kernels: none -> 36.1 us  [the longest x1 8.15 us: place_rows(): call(place_kernel, jax.ShapeDtypeStruct((DEVS, PAY, 128), jnp.float32), g...]
    all_to_all x11 -> x5, starting transfers between devices: 74.2 us -> 38.5 us  [the longest x3 17.2 us: exchange(): lax.all_to_all(packet.astype(jnp.float16), BOTH, split_axis=0, concat_axi...]
    psum x1 -> x0, blocking collectives: 21.7 us -> none  [local(): summed, weights = lax.psum((summed, weights), 'grp')]
    all_gather x2 -> x0, waiting for transfers between devices: 21.4 us -> none  [local(): whole = lax.all_gather(field, 'grp', axis=1, tiled=True)]
    all_to_all x0 -> x1, blocking collectives: none -> 18 us  [exchange(): lax.all_to_all(packet.astype(jnp.float16), BOTH, split_axis=0, concat_axi...]
    all_to_all x15 -> x0, local copies, waits for them, and re-layouts: 17.2 us -> none  [the longest x4 4.52 us: local(): lax.all_to_all(real_part, 'slab', split_axis=1, concat_axis=0, tiled=True)]
  transfers between devices with their start and end apart: 14 -> 6, of which waited for: 12 -> 4; matrix products, arithmetic and copies ran while one was open for 31% -> 12% of each run, Pallas kernels for 0% -> 9%
where the time goes in v1:
time: 188 us; the launch traced here: 187 us
  waiting for transfers between devices  43.8 us (23%)
  starting transfers between devices  41.4 us (22%)
  Pallas kernels  36.1 us (19%)
  local copies, waits for them, and re-layouts  24.3 us (13%)
  blocking collectives  18 us (10%)
  other arithmetic  16.5 us (9%)
  matrix products  5.94 us (3%)
    all_to_all x1, blocking collectives, exchange(): lax.all_to_all(packet.astype(jnp.float16), BOTH, split_axis=0, concat_axi...  18 us
    all_to_all x3, waiting for transfers between devices, exchange(): lax.all_to_all(packet.astype(jnp.float16), BOTH, split_axis=0, concat_axi...  17.7 us
    all_to_all x3, starting transfers between devices, exchange(): lax.all_to_all(packet.astype(jnp.float16), BOTH, split_axis=0, concat_axi...  17.2 us
    all_to_all x1, waiting for transfers between devices, local(): lax.all_to_all(narrow, BOTH, split_axis=0, concat_axis=0, tiled=True)  14.7 us
    all_to_all x1, waiting for transfers between devices, local(): got = lax.all_to_all(send, 'slab', split_axis=0, concat_axis=0, tiled=True)  11.5 us
    all_to_all x1, starting transfers between devices, local(): got = lax.all_to_all(send, 'slab', split_axis=0, concat_axis=0, tiled=True)  11.1 us
    all_to_all x1, starting transfers between devices, local(): lax.all_to_all(narrow, BOTH, split_axis=0, concat_axis=0, tiled=True)  10.2 us
    unnamed x80, local copies, waits for them, and re-layouts  10.1 us
  transfers between devices with their start and end apart: 6, of which 4 were waited for; matrix products, arithmetic and copies ran while one was open for 12% of the time, Pallas kernels for 9%

profile of v1, /device:TPU:1, one launch (start us, length us, event | category | flops | bytes accessed | tf_op | source)
XLA Modules:
  0.0 187.2 jit_solution(16989791414845720719)
XLA Ops:
  0.6 2.1 %reshape_squeeze.4.column_ref = s32[5120,1]{1,0:T(8,128)S(1)} reshape(s32[1,1,64,80]{3,2,1,0:T(8,128)} %param.23) | data formatting | bytes 40960 | tf_op jit(solution)/shard_map/reshape;squeeze | solution.py:410
  2.7 5.9 %convolution_convert_fusion = bf16[32,16384]{1,0:T(8,128)(2,1)} fusion(bf16[1,256,16384]{2,1,0:T(8,128)(2,1)} %param.21, bf16[1,256,32]{1,2,0:T(8,128)(2,1)S(1)} %copy-done.38), kind=kOutput, calls=%fused_computation | convolution fusion | flops 268959744 | bytes 9453568 | tf_op jit(solution)/shard_map/kr,kp->rp/dot_general | solution.py:404
  8.7 2.3 %reshape.163.rows_ref = bf16[4096,128]{1,0:T(8,128)(2,1)} reshape(bf16[32,16384]{1,0:T(8,128)(2,1)} %convolution_convert_fusion) | data formatting | bytes 2097152 | tf_op jit(solution)/shard_map/reshape | solution.py:405
  11.1 1.2 copy-done.2
  12.4 8.0 %shard_map.212 = bf16[64,88,128]{2,1,0:T(8,128)(2,1)S(1)} custom-call(f32[32]{0:T(128)S(1)} %convert_element_type.61.weight_ref, s32[5120,1]{1,0:T(8,128)S(1)} %reshape_squeeze.4.column_ref, s32[64,128]{1,0:T(8,128)S(1)} %pad.4.table_ref, bf16[4096,128]{1,0:T(8,128)(2,1)S(1)} %copy-done.2), custom_call_target="tpu_custom_call" | custom-call | tf_op jit(solution)/shard_map/pallas_call | solution.py:149
  21.5 11.1 %all-to-all-start = ((bf16[64,88,128]{2,1,0:T(8,128)(2,1)}), bf16[64,88,128]{2,1,0:T(8,128)(2,1)S(1)}, u32[]{:S(2)}, u32[]{:S(2)}) async-start(bf16[64,88,128]{2,1,0:T(8,128)(2,1)} %copy-done.1), calls=%async_computation | async-start | bytes 2883584 | tf_op jit(solution)/shard_map/all_to_all | solution.py:414
  32.6 2.8 %and.90 = s32[5120,1]{1,0:T(8,128)} reshape(s32[1,1,64,80]{3,2,1,0:T(8,128)S(1)} %get-tuple-element.13) | data formatting | bytes 40960 | tf_op jit(solution)/shard_map/and | solution.py:417
  35.4 2.8 %and.91 = s32[5120,1]{1,0:T(8,128)} reshape(s32[1,1,64,80]{3,2,1,0:T(8,128)S(1)} %get-tuple-element.12) | data formatting | bytes 40960 | tf_op jit(solution)/shard_map/and | solution.py:418
  38.2 2.8 %shift_right_arithmetic.50 = s32[5120,1]{1,0:T(8,128)} reshape(s32[1,1,64,80]{3,2,1,0:T(8,128)S(1)} %get-tuple-element.14) | data formatting | bytes 40960 | tf_op jit(solution)/shard_map/shift_right_arithmetic | solution.py:419
  41.0 1.7 shard_map.215
  43.6 11.5 %all-to-all-done.got_ref = bf16[64,88,128]{2,1,0:T(8,128)(2,1)S(1)} async-done(((bf16[64,88,128]{2,1,0:T(8,128)(2,1)}), bf16[64,88,128]{2,1,0:T(8,128)(2,1)S(1)}, u32[]{:S(2)}, u32[]{:S(2)}) %all-to-all-start) | async-done | bytes 1441824 | tf_op jit(solution)/shard_map/all_to_all | solution.py:414
  55.0 5.3 %all-to-all-start.1 = ((f16[128,16,128]{2,1,0:T(8,128)(2,1)}), f16[128,16,128]{2,1,0:T(8,128)(2,1)}, u32[]{:S(2)}, u32[]{:S(2)}) async-start(f16[128,16,128]{2,1,0:T(8,128)(2,1)} %convert_element_type.67), calls=%async_computation.1 | async-start | bytes 1048576 | tf_op jit(solution)/shard_map/all_to_all | solution.py:391
  60.4 5.7 %add_add_fusion.column_ref = s32[5120,1]{1,0:T(8,128)} fusion(s32[5120,1]{1,0:T(8,128)} %and.90, s32[5120,1]{1,0:T(8,128)} %shift_right_arithmetic.50, s32[5120,1]{1,0:T(8,128)} %and.91), kind=kLoop, calls=%fused_computation.2 | loop fusion | flops 61440 | bytes 81920 | tf_op jit(solution)/shard_map/add | solution.py:422
  66.4 1.7 copy-done
  68.2 8.1 %shard_map.213.own_ref = f32[128,24,128]{2,1,0:T(8,128)S(1)} custom-call(bf16[64,88,128]{2,1,0:T(8,128)(2,1)S(1)} %all-to-all-done.got_ref, s32[5120,1]{1,0:T(8,128)S(1)} %copy-done, s32[8,1,640]{2,1,0:T(1,128)S(1)} %add_add_fusion.1.row_ref), custom_call_target="tpu_custom_call" | custom-call | tf_op jit(solution)/shard_map/pallas_call | solution.py:197
  77.3 10.2 %all-to-all-start.2 = ((f16[128,24,128]{2,1,0:T(8,128)(2,1)}), f16[128,24,128]{2,1,0:T(8,128)(2,1)}, u32[]{:S(2)}, u32[]{:S(2)}) async-start(f16[128,24,128]{2,1,0:T(8,128)(2,1)} %convert_element_type.65), calls=%async_computation.2 | async-start | bytes 1572864 | tf_op jit(solution)/shard_map/all_to_all | solution.py:426
  87.6 1.2 convert_element_type.68.got_ref
  88.8 14.7 %all-to-all-done.2 = f16[128,24,128]{2,1,0:T(8,128)(2,1)} async-done(((f16[128,24,128]{2,1,0:T(8,128)(2,1)}), f16[128,24,128]{2,1,0:T(8,128)(2,1)}, u32[]{:S(2)}, u32[]{:S(2)}) %all-to-all-start.2) | async-done | bytes 786464 | tf_op jit(solution)/shard_map/all_to_all | solution.py:426
  103.5 1.4 convert_element_type.69.got_ref
  106.7 2.9 %shard_map.216 = (f32[256,256]{1,0:T(8,128)S(1)}, f32[256,256]{1,0:T(8,128)S(1)}) custom-call(s32[2]{0:T(128)S(1)} %pad_add_fusion.first_ref.place_ref, f32[128,24,128]{2,1,0:T(8,128)S(1)} %convert_element_type.69.got_ref, bf16[256,256]{1,0:T(8,128)(2,1)S(1)} %copy-done.34, bf16[256,256]{1,0:T(8,128)(2,1)S(1)} %copy-done.35), custom_call_target="tpu_custom_call" | custom-call | tf_op jit(solution)/shard_map/pallas_call | solution.py:269
  109.6 3.9 %shard_map.217 = f32[128,16,128]{2,1,0:T(8,128)S(1)} custom-call(s32[2]{0:T(128)S(1)} %pad_add_fusion.first_ref.place_ref, f32[128,16,128]{2,1,0:T(8,128)S(1)} %convert_element_type.68.got_ref, f32[256,256]{1,0:T(8,128)S(1)} %get-tuple-element.6.amplitude_ref, f32[256,256]{1,0:T(8,128)S(1)} %get-tuple-element.7.nyquist_ref, bf16[1024,512]{1,0:T(8,128)(2,1)S(1)} %copy-done.3, ...), custom_call_target="tpu_custom_call" | custom-call | tf_op jit(solution)/shard_map/pallas_call | solution.py:385
  113.7 18.0 %all_to_all.30 = f16[128,16,128]{2,1,0:T(8,128)(2,1)S(1)} all-to-all(f16[128,16,128]{2,1,0:T(8,128)(2,1)S(1)} %convert_element_type.70), channel_id=1, replica_groups=mesh['grp'=2,'slab'=64] {'grp','slab'}, dimensions={0} | all-to-all | bytes 1048576 | tf_op jit(solution)/shard_map/all_to_all | solution.py:391
  131.8 2.9 %shard_map.218 = (f32[4,128,256]{2,1,0:T(8,128)S(1)}, f32[128,16,128]{2,1,0:T(8,128)S(1)}) custom-call(f32[128,16,128]{2,1,0:T(8,128)S(1)} %convert_element_type.71.got_ref, s32[4,128,256]{2,1,0:T(8,128)S(1)} %copy-done.12, f32[4,128,256]{2,1,0:T(8,128)S(1)} %copy-done.11, bf16[256,512]{1,0:T(8,128)(2,1)S(1)} %copy-done.17, bf16[256,512]{1,0:T(8,128)(2,1)S(1)} %copy-done.19, ...), custom_call_target="tpu_custom_call" | custom-call | tf_op jit(solution)/shard_map/pallas_call | solution.py:333
  136.3 5.8 %all-to-all-start.4 = ((f16[128,16,128]{2,1,0:T(8,128)(2,1)}), f16[128,16,128]{2,1,0:T(8,128)(2,1)}, u32[]{:S(2)}, u32[]{:S(2)}) async-start(f16[128,16,128]{2,1,0:T(8,128)(2,1)} %convert_element_type.72), calls=%async_computation.4 | async-start | bytes 1048576 | tf_op jit(solution)/shard_map/all_to_all | solution.py:391
  144.2 2.9 %collective-permute-start = (f16[128,16,128]{2,1,0:T(8,128)(2,1)}, f16[128,16,128]{2,1,0:T(8,128)(2,1)}, u32[]{:S(2)}, u32[]{:S(2)}) collective-permute-start(f16[128,16,128]{2,1,0:T(8,128)(2,1)} %pad_maximum_fusion), channel_id=1, source_target_pairs={{0,64},{64,0},{1,65},{65,1},{2,66},{66,2},{3,67},{67,3},{4,68},{68... | collective-permute-start | bytes 1572872 | tf_op jit(solution)/shard_map/ppermute | solution.py:428
  147.1 8.2 %all-to-all-done.4 = f16[128,16,128]{2,1,0:T(8,128)(2,1)} async-done(((f16[128,16,128]{2,1,0:T(8,128)(2,1)}), f16[128,16,128]{2,1,0:T(8,128)(2,1)}, u32[]{:S(2)}, u32[]{:S(2)}) %all-to-all-start.4) | async-done | bytes 524320 | tf_op jit(solution)/shard_map/all_to_all | solution.py:391
  156.5 1.2 copy-done.6
  159.7 3.9 %shard_map.219 = f32[128,16,128]{2,1,0:T(8,128)S(1)} custom-call(s32[2]{0:T(128)S(1)} %pad_add_fusion.first_ref.place_ref, f32[128,16,128]{2,1,0:T(8,128)S(1)} %convert_element_type.73.got_ref, f32[256,256]{1,0:T(8,128)S(1)} %copy-done.22, f32[256,256]{1,0:T(8,128)S(1)} %copy-done.24, bf16[1024,512]{1,0:T(8,128)(2,1)S(1)} %copy-done.4, ...), custom_call_target="tpu_custom_call" | custom-call | tf_op jit(solution)/shard_map/pallas_call | solution.py:385
  164.5 6.1 %all-to-all-start.5 = ((f16[128,16,128]{2,1,0:T(8,128)(2,1)}), f16[128,16,128]{2,1,0:T(8,128)(2,1)}, u32[]{:S(2)}, u32[]{:S(2)}) async-start(f16[128,16,128]{2,1,0:T(8,128)(2,1)} %convert_element_type.74), calls=%async_computation.5 | async-start | bytes 1048576 | tf_op jit(solution)/shard_map/all_to_all | solution.py:391
  171.8 2.6 %shard_map.214 = f32[4,128,256]{2,1,0:T(8,128)} custom-call(s32[1]{0:T(128)} %bitcast.group_ref, f32[128,24,128]{2,1,0:T(8,128)S(1)} %shard_map.213.own_ref, f32[128,16,128]{2,1,0:T(8,128)S(1)} %convert_element_type.66.other_ref, bf16[2,128,128]{2,1,0:T(8,128)(2,1)S(1)} %copy-done.36), custom_call_target="tpu_custom_call" | custom-call | tf_op jit(solution)/shard_map/pallas_call | solution.py:231
  174.4 9.4 %all-to-all-done.5 = f16[128,16,128]{2,1,0:T(8,128)(2,1)} async-done(((f16[128,16,128]{2,1,0:T(8,128)(2,1)}), f16[128,16,128]{2,1,0:T(8,128)(2,1)}, u32[]{:S(2)}, u32[]{:S(2)}) %all-to-all-start.5) | async-done | bytes 524320 | tf_op jit(solution)/shard_map/all_to_all | solution.py:391
  185.0 2.2 %shard_map.220 = f32[4,128,256]{2,1,0:T(8,128)} custom-call(f32[128,16,128]{2,1,0:T(8,128)S(1)} %convert_element_type.75.got_ref, s32[4,128,256]{2,1,0:T(8,128)S(1)} %copy-done.13, f32[4,128,256]{2,1,0:T(8,128)S(1)} %copy-done.29, bf16[256,512]{1,0:T(8,128)(2,1)S(1)} %copy-done.18, bf16[256,512]{1,0:T(8,128)(2,1)S(1)} %copy-done.20, ...), custom_call_target="tpu_custom_call" | custom-call | tf_op jit(solution)/shard_map/pallas_call | solution.py:339
  (99 shorter events, 15.6 us)
Async XLA Ops:
  2.7 8.4 %copy-start.37 = (s32[1,1,64,80]{3,2,1,0:T(8,128)S(1)}, s32[1,1,64,80]{3,2,1,0:T(8,128)}, u32[]{:S(2)}) copy-start(s32[1,1,64,80]{3,2,1,0:T(8,128)} %param.23) | copy-start | bytes 61444
  21.5 11.1 %copy-start.39 = (s32[1,1,64,80]{3,2,1,0:T(8,128)S(1)}, s32[1,1,64,80]{3,2,1,0:T(8,128)}, u32[]{:S(2)}) copy-start(s32[1,1,64,80]{3,2,1,0:T(8,128)} %param.24) | copy-start | bytes 61444
  21.5 33.5 %all-to-all-start = ((bf16[64,88,128]{2,1,0:T(8,128)(2,1)}), bf16[64,88,128]{2,1,0:T(8,128)(2,1)S(1)}, u32[]{:S(2)}, u32[]{:S(2)}) async-start(bf16[64,88,128]{2,1,0:T(8,128)(2,1)} %copy-done.1), calls=%async_computation | async-start | bytes 2883584 | tf_op jit(solution)/shard_map/all_to_all | solution.py:414
  35.4 5.6 %copy-start.15 = (bf16[512,256]{1,0:T(8,128)(2,1)S(1)}, bf16[512,256]{1,0:T(8,128)(2,1)}, u32[]{:S(2)}) copy-start(bf16[512,256]{1,0:T(8,128)(2,1)} %constant.78.clone.yl) | copy-start | bytes 786436
  35.4 5.6 %copy-start.25 = (bf16[256,256]{1,0:T(8,128)(2,1)S(1)}, bf16[256,256]{1,0:T(8,128)(2,1)}, u32[]{:S(2)}) copy-start(bf16[256,256]{1,0:T(8,128)(2,1)} %constant.73.clone.zh) | copy-start | bytes 393220
  35.4 5.6 %copy-start.26 = (bf16[256,256]{1,0:T(8,128)(2,1)S(1)}, bf16[256,256]{1,0:T(8,128)(2,1)}, u32[]{:S(2)}) copy-start(bf16[256,256]{1,0:T(8,128)(2,1)} %constant.74.clone.zl) | copy-start | bytes 393220
  55.0 22.3 %all-to-all-start.1 = ((f16[128,16,128]{2,1,0:T(8,128)(2,1)}), f16[128,16,128]{2,1,0:T(8,128)(2,1)}, u32[]{:S(2)}, u32[]{:S(2)}) async-start(f16[128,16,128]{2,1,0:T(8,128)(2,1)} %convert_element_type.67), calls=%async_computation.1 | async-start | bytes 1048576 | tf_op jit(solution)/shard_map/all_to_all | solution.py:391
  77.3 26.1 %all-to-all-start.2 = ((f16[128,24,128]{2,1,0:T(8,128)(2,1)}), f16[128,24,128]{2,1,0:T(8,128)(2,1)}, u32[]{:S(2)}, u32[]{:S(2)}) async-start(f16[128,24,128]{2,1,0:T(8,128)(2,1)} %convert_element_type.65), calls=%async_computation.2 | async-start | bytes 1572864 | tf_op jit(solution)/shard_map/all_to_all | solution.py:426
  87.6 22.0 %copy-start.7 = (bf16[512,512]{1,0:T(8,128)(2,1)S(1)}, bf16[512,512]{1,0:T(8,128)(2,1)}, u32[]{:S(2)}) copy-start(bf16[512,512]{1,0:T(8,128)(2,1)} %constant.83.clone.ixh) | copy-start | bytes 1572868
  103.4 6.1 %copy-start.3 = (bf16[1024,512]{1,0:T(8,128)(2,1)S(1)}, bf16[1024,512]{1,0:T(8,128)(2,1)}, u32[]{:S(2)}) copy-start(bf16[1024,512]{1,0:T(8,128)(2,1)} %constant.81.clone.xh) | copy-start | bytes 3145732
  103.4 6.1 %copy-start.5 = (bf16[1024,512]{1,0:T(8,128)(2,1)S(1)}, bf16[1024,512]{1,0:T(8,128)(2,1)}, u32[]{:S(2)}) copy-start(bf16[1024,512]{1,0:T(8,128)(2,1)} %constant.82.clone.xl) | copy-start | bytes 3145732
  103.4 6.1 %copy-start.8 = (bf16[512,512]{1,0:T(8,128)(2,1)S(1)}, bf16[512,512]{1,0:T(8,128)(2,1)}, u32[]{:S(2)}) copy-start(bf16[512,512]{1,0:T(8,128)(2,1)} %constant.84.clone.ixl) | copy-start | bytes 1572868
  113.5 18.2 %copy-start.11 = (f32[4,128,256]{2,1,0:T(8,128)S(1)}, f32[4,128,256]{2,1,0:T(8,128)}, u32[]{:S(2)}) copy-start(f32[4,128,256]{2,1,0:T(8,128)} %density_ref.3) | copy-start | bytes 1572868
  113.5 18.2 %copy-start.12 = (s32[4,128,256]{2,1,0:T(8,128)S(1)}, s32[4,128,256]{2,1,0:T(8,128)}, u32[]{:S(2)}) copy-start(s32[4,128,256]{2,1,0:T(8,128)} %support_ref.3) | copy-start | bytes 1572868
  113.5 18.2 %copy-start.16 = (bf16[512,256]{1,0:T(8,128)(2,1)S(1)}, bf16[512,256]{1,0:T(8,128)(2,1)}, u32[]{:S(2)}) copy-start(bf16[512,256]{1,0:T(8,128)(2,1)} %constant.78.clone.yl) | copy-start | bytes 786436
  113.5 18.2 %copy-start.17 = (bf16[256,512]{1,0:T(8,128)(2,1)S(1)}, bf16[256,512]{1,0:T(8,128)(2,1)}, u32[]{:S(2)}) copy-start(bf16[256,512]{1,0:T(8,128)(2,1)} %constant.79.clone.iyh) | copy-start | bytes 786436
  113.6 18.2 %copy-start.19 = (bf16[256,512]{1,0:T(8,128)(2,1)S(1)}, bf16[256,512]{1,0:T(8,128)(2,1)}, u32[]{:S(2)}) copy-start(bf16[256,512]{1,0:T(8,128)(2,1)} %constant.80.clone.iyl) | copy-start | bytes 786436
  113.6 18.2 %copy-start.27 = (bf16[256,256]{1,0:T(8,128)(2,1)S(1)}, bf16[256,256]{1,0:T(8,128)(2,1)}, u32[]{:S(2)}) copy-start(bf16[256,256]{1,0:T(8,128)(2,1)} %constant.74.clone.zl) | copy-start | bytes 393220
  113.6 18.2 %copy-start.30 = (bf16[256,256]{1,0:T(8,128)(2,1)S(1)}, bf16[256,256]{1,0:T(8,128)(2,1)}, u32[]{:S(2)}) copy-start(bf16[256,256]{1,0:T(8,128)(2,1)} %constant.75.clone.izh) | copy-start | bytes 393220
  113.6 18.2 %copy-start.32 = (bf16[256,256]{1,0:T(8,128)(2,1)S(1)}, bf16[256,256]{1,0:T(8,128)(2,1)}, u32[]{:S(2)}) copy-start(bf16[256,256]{1,0:T(8,128)(2,1)} %constant.76.clone.izl) | copy-start | bytes 393220
  136.3 20.1 %copy-start.4 = (bf16[1024,512]{1,0:T(8,128)(2,1)S(1)}, bf16[1024,512]{1,0:T(8,128)(2,1)}, u32[]{:S(2)}) copy-start(bf16[1024,512]{1,0:T(8,128)(2,1)} %constant.81.clone.xh) | copy-start | bytes 3145732
  136.3 20.2 %copy-start.22 = (f32[256,256]{1,0:T(8,128)S(1)}, f32[256,256]{1,0:T(8,128)}, u32[]{:S(2)}) copy-start(f32[256,256]{1,0:T(8,128)} %copy-done.21) | copy-start | bytes 786436
  136.3 19.0 %all-to-all-start.4 = ((f16[128,16,128]{2,1,0:T(8,128)(2,1)}), f16[128,16,128]{2,1,0:T(8,128)(2,1)}, u32[]{:S(2)}, u32[]{:S(2)}) async-start(f16[128,16,128]{2,1,0:T(8,128)(2,1)} %convert_element_type.72), calls=%async_computation.4 | async-start | bytes 1048576 | tf_op jit(solution)/shard_map/all_to_all | solution.py:391
  144.2 26.4 %collective-permute-start = (f16[128,16,128]{2,1,0:T(8,128)(2,1)}, f16[128,16,128]{2,1,0:T(8,128)(2,1)}, u32[]{:S(2)}, u32[]{:S(2)}) collective-permute-start(f16[128,16,128]{2,1,0:T(8,128)(2,1)} %pad_maximum_fusion), channel_id=1, source_target_pairs={{0,64},{64,0},{1,65},{65,1},{2,66},{66,2},{3,67},{67,3},{4,68},{68... | collective-permute-start | bytes 1572872 | tf_op jit(solution)/shard_map/ppermute | solution.py:428
  163.6 8.2 %copy-start.36 = (bf16[2,128,128]{2,1,0:T(8,128)(2,1)S(1)}, bf16[2,128,128]{2,1,0:T(8,128)(2,1)}, u32[]{:S(2)}) copy-start(bf16[2,128,128]{2,1,0:T(8,128)(2,1)} %constant.87.clone.flip_ref) | copy-start | bytes 196612
  164.5 19.3 %all-to-all-start.5 = ((f16[128,16,128]{2,1,0:T(8,128)(2,1)}), f16[128,16,128]{2,1,0:T(8,128)(2,1)}, u32[]{:S(2)}, u32[]{:S(2)}) async-start(f16[128,16,128]{2,1,0:T(8,128)(2,1)} %convert_element_type.74), calls=%async_computation.5 | async-start | bytes 1048576 | tf_op jit(solution)/shard_map/all_to_all | solution.py:391
  171.7 13.2 %copy-start.13 = (s32[4,128,256]{2,1,0:T(8,128)S(1)}, s32[4,128,256]{2,1,0:T(8,128)}, u32[]{:S(2)}) copy-start(s32[4,128,256]{2,1,0:T(8,128)} %support_ref.3) | copy-start | bytes 1572868
  171.8 13.2 %copy-start.18 = (bf16[256,512]{1,0:T(8,128)(2,1)S(1)}, bf16[256,512]{1,0:T(8,128)(2,1)}, u32[]{:S(2)}) copy-start(bf16[256,512]{1,0:T(8,128)(2,1)} %constant.79.clone.iyh) | copy-start | bytes 786436
  171.8 13.2 %copy-start.20 = (bf16[256,512]{1,0:T(8,128)(2,1)S(1)}, bf16[256,512]{1,0:T(8,128)(2,1)}, u32[]{:S(2)}) copy-start(bf16[256,512]{1,0:T(8,128)(2,1)} %constant.80.clone.iyl) | copy-start | bytes 786436
  171.8 13.2 %copy-start.29 = (f32[4,128,256]{2,1,0:T(8,128)S(1)}, f32[4,128,256]{2,1,0:T(8,128)}, u32[]{:S(2)}) copy-start(f32[4,128,256]{2,1,0:T(8,128)} %copy-done.28) | copy-start | bytes 1572868
  171.8 13.2 %copy-start.31 = (bf16[256,256]{1,0:T(8,128)(2,1)S(1)}, bf16[256,256]{1,0:T(8,128)(2,1)}, u32[]{:S(2)}) copy-start(bf16[256,256]{1,0:T(8,128)(2,1)} %constant.75.clone.izh) | copy-start | bytes 393220
  171.8 13.2 %copy-start.33 = (bf16[256,256]{1,0:T(8,128)(2,1)S(1)}, bf16[256,256]{1,0:T(8,128)(2,1)}, u32[]{:S(2)}) copy-start(bf16[256,256]{1,0:T(8,128)(2,1)} %constant.76.clone.izl) | copy-start | bytes 393220
  (14 other events, 31.2 us)

commit v2 on v0

v2 whole, which is shorter than its diff:
```python
import functools

import jax
import jax.numpy as jnp
import ml_dtypes
import numpy as np
from jax import lax
from jax.experimental import pallas as pl
from jax.experimental.pallas import tpu as pltpu
from jax.sharding import PartitionSpec as P

N = 256
HALF = N // 2
PLANES = 4
SLABS = 64
DEVS = 128
CAP = 80
ROWS = 4096
BETA = 0.9
SOFTEN = 0.25
BOTH = ("grp", "slab")
MIB = 1024 * 1024


def split_table(table):
    high = table.astype(np.float32).astype(ml_dtypes.bfloat16)
    low = (table - high.astype(np.float64)).astype(np.float32).astype(ml_dtypes.bfloat16)
    return (jnp.asarray(high), jnp.asarray(low))


def phase(rows, columns):
    angle = 2.0 * np.pi / N * ((rows[:, None] * columns[None, :]) % N)
    return (np.cos(angle) / np.sqrt(N), np.sin(angle) / np.sqrt(N))


@functools.cache
def tables():
    z = np.arange(N)
    cos, sin = phase(z, np.arange(HALF))
    nyquist = np.cos(np.pi * z) / np.sqrt(N)
    forward_z = np.concatenate([cos, -sin], axis=1)
    forward_z[:, HALF] = nyquist
    inverse_z = np.concatenate([2.0 * cos.T, -2.0 * sin.T], axis=0)
    inverse_z[0] = 1.0 / np.sqrt(N)
    inverse_z[HALF] = nyquist
    first = np.arange(DEVS)
    frequency = np.concatenate([first, np.where(first == 0, HALF, N - first)])
    cos_y, sin_y = phase(frequency, z)
    order = (np.arange(PLANES)[:, None] + PLANES * np.arange(SLABS)[None, :]).reshape(-1)
    cos_x, sin_x = phase(order, order)
    place = np.argsort(order)
    flips = np.zeros((3, N, N))
    flips[0, np.arange(N), place[(-order) % N]] = 1.0
    flips[1, (-z) % N, z] = 1.0
    flips[2, first, first] = 1.0
    flips[2, HALF + first, (-first) % HALF] = 1.0

    def split(parts):
        rows = []
        for part in parts:
            high = part.astype(np.float32).astype(ml_dtypes.bfloat16)
            rows += [high, (part - high.astype(np.float64)).astype(np.float32).astype(ml_dtypes.bfloat16)]
        return jnp.asarray(np.concatenate(rows, axis=0))

    return dict(
        forward=split([cos_y, sin_y, forward_z]),
        inverse=split([cos_y.T, sin_y.T, inverse_z]),
        slab=split([cos_x, sin_x]),
        flips=jnp.asarray(flips.astype(ml_dtypes.bfloat16)),
    )


def halves(values):
    high = values.astype(jnp.bfloat16)
    return (high, (values - high.astype(jnp.float32)).astype(jnp.bfloat16))


def dot(left, right):
    return jnp.dot(left, right, preferred_element_type=jnp.float32)


def table_left(ref, index, length=N):
    high = ref[2 * index * N : 2 * index * N + length]
    low = ref[(2 * index + 1) * N : (2 * index + 1) * N + length]
    return [high, low, high]


def times_table(values, ref, index):
    high, low = halves(values)
    top = ref[2 * index * N : (2 * index + 1) * N]
    rest = ref[(2 * index + 1) * N : (2 * index + 2) * N]
    return dot(jnp.concatenate([high, low, high], axis=1), jnp.concatenate([top, top, rest], axis=0))


def turn(ref, real, imag, sign, length=N):
    real = halves(real)
    imag = halves(imag)
    straight = [jnp.concatenate([a, b], axis=1) for a, b in zip(real, imag)]
    if sign > 0:
        crossed = [jnp.concatenate([-b, a], axis=1) for a, b in zip(real, imag)]
    else:
        crossed = [jnp.concatenate([b, -a], axis=1) for a, b in zip(real, imag)]
    left = jnp.concatenate(table_left(ref, 0, length) + table_left(ref, 1, length), axis=1)
    right = [straight[0], straight[0], straight[1], crossed[0], crossed[0], crossed[1]]
    return dot(left, jnp.concatenate(right, axis=0))


FINE = 2.0**14
OCTAVE = 32767.0 / 30.0
LOG2 = float(np.log(2.0))


def coded(values):
    size = jnp.minimum(jnp.log(1.0 + FINE * jnp.abs(values)) * (OCTAVE / LOG2), 32767.0)
    whole = (size + 0.5).astype(jnp.int32)
    return jnp.where(values < 0.0, -whole, whole).astype(jnp.int16)


def decoded(codes):
    values = codes.astype(jnp.int32).astype(jnp.float32)
    size = (jnp.exp(jnp.abs(values) * (LOG2 / OCTAVE)) - 1.0) * (1.0 / FINE)
    return jnp.where(values < 0.0, -size, size)


def call(kernel, out_shape, mib=16, **kwargs):
    return pl.pallas_call(
        kernel,
        out_shape=out_shape,
        compiler_params=pltpu.CompilerParams(vmem_limit_bytes=mib * MIB),
        **kwargs,
    )


def spec_vmem(count):
    return [pl.BlockSpec(memory_space=pltpu.VMEM)] * count


def smem():
    return pl.BlockSpec(memory_space=pltpu.SMEM)


def hbm():
    return pl.BlockSpec(memory_space=pltpu.HBM)


def fetch(source, target, sem):
    copy = pltpu.make_async_copy(source, target, sem)
    copy.start()
    return copy


BLOCKS = 4


def send_out(rows_ref, code_ref, out_ref, sems):
    count = code_ref.shape[1]
    copies = []
    for block in range(BLOCKS):
        devices = pl.ds(block * (DEVS // BLOCKS), DEVS // BLOCKS)
        code_ref[devices] = coded(rows_ref[devices, :count, :])
        copies.append(fetch(code_ref.at[devices], out_ref.at[devices], sems.at[block]))
    return copies


def table_scratch(rows):
    return pltpu.VMEM((rows, N), jnp.bfloat16)


def code_scratch(rows):
    return pltpu.VMEM((DEVS, rows, 128), jnp.int16)


def sems(count):
    return pltpu.SemaphoreType.DMA((count,))


CUTS = 8
CUT = DEVS // CUTS
EMPTY = 8
SEND = 88


def gather_kernel(index_ref, table_ref, probabilities_ref, patterns_ref, out_ref, block_ref, rows_ref, picked_ref, sem):
    def copy(cut):
        part = pl.ds(cut * CUT * 128, CUT * 128)
        return pltpu.make_async_copy(patterns_ref.at[:, part], block_ref.at[:, part], sem.at[cut])

    for cut in range(CUTS):
        copy(cut).start()
    rows_ref[:EMPTY] = jnp.zeros((EMPTY, 128), jnp.float32)
    turned = probabilities_ref[...].astype(jnp.float32).T
    left = turned.astype(jnp.bfloat16)
    for cut in range(CUTS):
        copy(cut).wait()
        part = dot(left, block_ref[:, cut * CUT * 128 : (cut + 1) * CUT * 128])
        part = part.astype(jnp.bfloat16).astype(jnp.float32)
        for d in range(CUT):
            rows_ref[pl.ds(EMPTY + cut * CUT + d, 32, stride=128), :] = part[:, d * 128 : (d + 1) * 128]

    def pick(step, unused):
        for o in range(2):
            owner = step * 2 + o
            for c in range(CAP):
                picked_ref[pl.ds(owner * CAP + c, 1), :] = rows_ref[pl.ds(EMPTY + index_ref[owner, c], 1), :]
        return unused

    lax.fori_loop(0, SLABS // 2, pick, 0)
    out_ref[:, :CAP, :] = picked_ref[...].astype(jnp.bfloat16).reshape(SLABS, CAP, 128)
    weight = jnp.sum(turned, axis=1, keepdims=True).astype(jnp.bfloat16).astype(jnp.float32)
    orientation = table_ref[...] >> 7
    weights = jnp.zeros((SLABS, CAP), jnp.float32)
    for r in range(32):
        weights = jnp.where(orientation == r, weight[r : r + 1], weights)
    weights = jnp.concatenate([weights, jnp.zeros((SLABS, 128 - CAP), jnp.float32)], axis=1)
    out_ref[:, CAP:, :] = jnp.broadcast_to(weights[:, None, :], (SLABS, 8, 128)).astype(jnp.bfloat16)


def gather_rows(source, probabilities, patterns):
    return call(
        gather_kernel,
        jax.ShapeDtypeStruct((SLABS, SEND, 128), jnp.bfloat16),
        mib=60,
        cost_estimate=pl.CostEstimate(flops=2 * 32 * 256 * 16384, bytes_accessed=32 * MIB, transcendentals=0),
        in_specs=[smem()] + spec_vmem(2) + [hbm()],
        out_specs=spec_vmem(1)[0],
        scratch_shapes=[
            pltpu.VMEM((256, DEVS * 128), jnp.bfloat16),
            pltpu.VMEM((EMPTY + ROWS, 128), jnp.float32),
            pltpu.VMEM((SLABS * CAP, 128), jnp.float32),
            pltpu.SemaphoreType.DMA((CUTS,)),
        ],
    )(source, source, probabilities, patterns)


SOURCES = 16
TAKEN = SOURCES * CAP
SLOTS = SLABS * CAP


def moved(target):
    y = (target >> 1) & (N - 1)
    pm = y >> 7
    j = jnp.where(pm == 1, (N - y) & (HALF - 1), y)
    return j * 16 + pm * 8 + (target >> 9) * 2 + (target & 1)


def columns_of(table):
    count = table.shape[0]
    square = jnp.concatenate([table, jnp.zeros((128 - count, 128), table.dtype)], axis=0).T
    return jnp.concatenate([square[:CAP, s : s + 1] for s in range(count)], axis=0)


def prepare_kernel(column_ref, out_ref, mark_ref, sem):
    copies = []
    for step in range(SLABS // SOURCES):
        slots = pl.ds(step * TAKEN, TAKEN)
        column = columns_of(moved(column_ref[step * SOURCES : (step + 1) * SOURCES]))
        mark = ((column >> 9) * 16 + (column & 15)).astype(jnp.float32)
        mark_ref[slots] = jnp.broadcast_to(mark, (TAKEN, 128)).astype(jnp.bfloat16)
        copies.append(fetch(mark_ref.at[slots], out_ref.at[slots], sem.at[step]))
    for copy in copies:
        copy.wait()


def prepare(column):
    return call(
        prepare_kernel,
        jax.ShapeDtypeStruct((SLOTS, 128), jnp.bfloat16),
        in_specs=spec_vmem(1),
        out_specs=hbm(),
        scratch_shapes=[pltpu.VMEM((SLOTS, 128), jnp.bfloat16), sems(SLABS // SOURCES)],
    )(column)


def place_kernel(got_ref, row_ref, mark_hbm, packet_ref, out_ref, sum_ref, mark_ref, code_ref, sem):
    steps = SLABS // SOURCES
    copies = []
    for step in range(steps):
        slots = pl.ds(step * TAKEN, TAKEN)
        copies.append(fetch(mark_hbm.at[slots], mark_ref.at[slots], sem.at[step]))
    code_ref[:, 24:, :] = packet_ref[...]
    weights = columns_of(got_ref[:, CAP:, :].astype(jnp.float32)[:, 0, :])
    total = jnp.zeros((DEVS, 128), jnp.float32)
    for step in range(steps):
        row = moved(row_ref[step])
        onehot = (lax.broadcasted_iota(jnp.int32, (512, TAKEN), 0) == (row & 511)).astype(jnp.bfloat16)
        left = (lax.broadcasted_iota(jnp.int32, (DEVS, TAKEN), 0) == (row >> 4)).astype(jnp.bfloat16)
        rows = got_ref[step * SOURCES : (step + 1) * SOURCES, :CAP].reshape(TAKEN, 128)
        copies[step].wait()
        mark = mark_ref[step * TAKEN : (step + 1) * TAKEN]
        zero = jnp.bfloat16(0)
        above = [rows] + [jnp.where(mark >= jnp.bfloat16(16 * q), rows, zero) for q in range(1, 4)]
        parts = [jnp.where(mark < jnp.bfloat16(16 * q + 16), above[q], zero) for q in range(3)] + [above[3]]
        part = dot(onehot, jnp.concatenate(parts, axis=1))
        sum_ref[...] = part if step == 0 else sum_ref[...] + part
        entry = mark.astype(jnp.float32).astype(jnp.int32) & 15
        lane = lax.broadcasted_iota(jnp.int32, (TAKEN, 128), 1)
        right = jnp.where(lane == entry, weights[step * TAKEN : (step + 1) * TAKEN], 0.0)
        total += dot(left, right.astype(jnp.bfloat16))
    total = coded(total)
    sent = []
    for q in range(4):
        devices = pl.ds(q * 32, 32)
        part = sum_ref[:, q * 128 : (q + 1) * 128].reshape(32, 16, 128)
        code_ref[devices, :16, :] = coded(part)
        code_ref[devices, 16:24, :] = jnp.broadcast_to(total[q * 32 : (q + 1) * 32][:, None, :], (32, 8, 128))
        sent.append(fetch(code_ref.at[devices], out_ref.at[devices], sem.at[q]))
    for copy in sent:
        copy.wait()


def place_rows(got, row, marks, packet):
    return call(
        place_kernel,
        jax.ShapeDtypeStruct((DEVS, 32, 128), jnp.int16),
        mib=28,
        in_specs=spec_vmem(2) + [hbm()] + spec_vmem(1),
        out_specs=hbm(),
        scratch_shapes=[
            pltpu.VMEM((512, 512), jnp.float32),
            pltpu.VMEM((SLOTS, 128), jnp.bfloat16),
            code_scratch(32),
            sems(4),
        ],
    )(got, row, marks, packet)


def intensity_kernel(group_ref, own_ref, other_ref, flip_ref, out_ref):
    group = group_ref[0]
    own = decoded(own_ref[:, :24, :])
    other = decoded(other_ref[...])
    total = jnp.where(group == 0, own[:, :8, :], own[:, 8:16, :]) + other[:, :8, :]
    weights = own[:, 16, :] + other[:, 8, :]
    divisor = jnp.maximum(jnp.where(group == 0, weights[:, :8], weights[:, 8:16]), 1.0)
    wide = jnp.concatenate([total[:, q, :] / divisor[:, q : q + 1] for q in range(8)], axis=1)
    flip = jnp.where(group == 0, flip_ref[2, :HALF, :HALF], flip_ref[2, HALF:, :HALF])
    high, low = halves(wide)
    turned = dot(flip, high) + dot(flip, low)
    for x in range(PLANES):
        out_ref[x] = turned[:, x * N : (x + 1) * N]


def intensity_of(group, own, other, flips):
    return call(
        intensity_kernel,
        jax.ShapeDtypeStruct((PLANES, HALF, N), jnp.float32),
        in_specs=[smem()] + spec_vmem(3),
        out_specs=pl.BlockSpec(memory_space=pltpu.VMEM),
    )(group, own, other, flips)


def amplitudes(first, got_ref, flip_ref):
    divisor = jnp.maximum(got_ref[:SLABS, 16, :] + got_ref[SLABS:, 16, :], 1.0)
    amplitude = []
    for pm in range(2):
        columns = []
        for zh in range(2):
            planes = []
            for x in range(PLANES):
                q = (pm * PLANES + x) * 2 + zh
                total = got_ref[:SLABS, q, :] + got_ref[SLABS:, q, :]
                planes.append(jnp.sqrt(total / divisor[:, q : q + 1]))
            columns.append(jnp.concatenate(planes, axis=0))
        amplitude.append(jnp.concatenate(columns, axis=1))
    mirrored = []
    for pm in range(2):
        high, low = halves(amplitude[pm])
        high = dot(flip_ref[0], high).astype(jnp.bfloat16)
        low = dot(flip_ref[0], low).astype(jnp.bfloat16)
        mirrored.append(dot(high, flip_ref[1]) + dot(low, flip_ref[1]))
    even = []
    for pm in range(2):
        partner = jnp.where(first == 1, mirrored[pm], mirrored[1 - pm])
        even.append(0.5 * (amplitude[pm] + partner))
    return (
        jnp.concatenate([part[:, :HALF] for part in even], axis=1),
        jnp.concatenate([part[:, HALF:] for part in even], axis=1),
    )


def tile(values, row, column):
    return values[row * 128 : (row + 1) * 128, column * 128 : (column + 1) * 128]


def send_forward(field, table_ref, rows_ref):
    partly = times_table(field, table_ref, 2)
    parts = []
    for c in range(2):
        parts.append(jnp.concatenate([partly[x * N : (x + 1) * N, c * HALF : (c + 1) * HALF] for x in range(2)], axis=1))
    result = turn(table_ref, parts[0], parts[1], -1)
    for x in range(2):
        for pm in range(2):
            for c in range(2):
                rows_ref[:, x * 4 + pm * 2 + c, :] = tile(result, pm, c * 2 + x)


def image_from(rows_ref, table_ref, length):
    planes = rows_ref.shape[1] // 4
    parts = []
    for c in range(2):
        columns = []
        for x in range(planes):
            columns.append(jnp.concatenate([rows_ref[:, x * 4 + pm * 2 + c, :] for pm in range(2)], axis=0))
        parts.append(jnp.concatenate(columns, axis=1))
    partly = turn(table_ref, parts[0], parts[1], 1, length)
    rows = []
    for x in range(planes):
        real = partly[:, x * HALF : (x + 1) * HALF]
        imag = partly[:, (planes + x) * HALF : (planes + x + 1) * HALF]
        rows.append(jnp.concatenate([real, imag], axis=1))
    return times_table(jnp.concatenate(rows, axis=0), table_ref, 2)


def first_kernel(density_ref, table_hbm, out_ref, rows_ref, table_ref, sem):
    fetch(table_hbm, table_ref, sem.at[0]).wait()
    send_forward(density_ref[...].reshape(2 * N, N), table_ref, rows_ref)
    out_ref[...] = coded(rows_ref[...])


def middle_kernel(
    got_ref, support_hbm, density_hbm, inverse_hbm, forward_hbm,
    field_hbm, code_hbm, out_ref,
    rows_ref, packet_ref, support_ref, density_ref, inverse_ref, forward_ref, field_ref, code_ref, sem,
):
    sources = ((inverse_hbm, inverse_ref), (support_hbm, support_ref), (density_hbm, density_ref), (forward_hbm, forward_ref))
    copies = [fetch(a, b, sem.at[i]) for i, (a, b) in enumerate(sources)]
    rows_ref[...] = decoded(got_ref[...])
    copies[0].wait()
    image = image_from(rows_ref, inverse_ref, N)
    copies[1].wait()
    copies[2].wait()
    support = support_ref[...].reshape(2 * N, N)
    density = density_ref[...].reshape(2 * N, N)
    field = jnp.where(support > 0.5, image, density - BETA * image)
    field_ref[...] = field.reshape(2, N, N)
    saved = [fetch(field_ref, field_hbm, sem.at[0])]
    copies[3].wait()
    send_forward(field, forward_ref, rows_ref)
    sent = send_out(rows_ref, packet_ref, out_ref, sem.at[pl.ds(4, BLOCKS)])
    code_ref[...] = coded(field_ref[...])
    saved.append(fetch(code_ref, code_hbm, sem.at[1]))
    for copy in sent + saved:
        copy.wait()


def last_kernel(
    group_ref, got_ref, support_hbm, own_hbm, other_ref, inverse_hbm,
    field_ref, rows_ref, support_ref, own_ref, inverse_ref, sem,
):
    group = group_ref[0]
    mine = own_hbm.at[:, pl.ds(pl.multiple_of(group * HALF, HALF), HALF), :]
    sources = ((inverse_hbm, inverse_ref), (support_hbm, support_ref), (mine, own_ref))
    copies = [fetch(a, b, sem.at[i]) for i, (a, b) in enumerate(sources)]
    rows_ref[...] = decoded(got_ref[...])
    copies[0].wait()
    image = image_from(rows_ref, inverse_ref, HALF).reshape(PLANES, HALF, N)
    other = decoded(other_ref[...])
    copies[1].wait()
    copies[2].wait()
    own = own_ref[...]
    for p in range(2):
        before = jnp.where(group == p, own, other)
        part = image[2 * p : 2 * p + 2]
        inside = support_ref[2 * p : 2 * p + 2] == 1
        field_ref[2 * p : 2 * p + 2] = jnp.where(inside, part, before - BETA * part)


PACKET = jax.ShapeDtypeStruct((DEVS, 8, 128), jnp.int16)
WIDE_PACKET = jax.ShapeDtypeStruct((DEVS, 16, 128), jnp.int16)


def scratch(rows):
    return pltpu.VMEM((DEVS, rows, 128), jnp.float32)


def first_field(density, t):
    return call(
        first_kernel,
        PACKET,
        in_specs=spec_vmem(1) + [hbm()],
        out_specs=spec_vmem(1)[0],
        scratch_shapes=[scratch(8), table_scratch(6 * N), sems(1)],
    )(density, t["forward"])


def middle_field(got, support, density, t):
    planes = (2, N, N)
    return call(
        middle_kernel,
        (jax.ShapeDtypeStruct(planes, jnp.float32), jax.ShapeDtypeStruct(planes, jnp.int16), PACKET),
        in_specs=spec_vmem(1) + [hbm()] * 4,
        out_specs=(hbm(),) * 3,
        scratch_shapes=[
            scratch(8),
            code_scratch(8),
            pltpu.VMEM(planes, jnp.float32),
            pltpu.VMEM(planes, jnp.float32),
            table_scratch(6 * N),
            table_scratch(6 * N),
            pltpu.VMEM(planes, jnp.float32),
            pltpu.VMEM(planes, jnp.int16),
            sems(4 + BLOCKS),
        ],
    )(got, support, density, t["inverse"], t["forward"])


def last_field(group, got, support, own, other, t):
    return call(
        last_kernel,
        jax.ShapeDtypeStruct((PLANES, HALF, N), jnp.float32),
        in_specs=[smem()] + spec_vmem(1) + [hbm()] * 2 + spec_vmem(1) + [hbm()],
        out_specs=spec_vmem(1)[0],
        scratch_shapes=[
            scratch(16),
            pltpu.VMEM((PLANES, HALF, N), jnp.int32),
            pltpu.VMEM((2, HALF, N), jnp.float32),
            table_scratch(6 * N),
            sems(3),
        ],
    )(group, got, support, own, other, t["inverse"])


def project(first, rows_ref, start, amplitude, nyquist, table_ref):
    lanes = []
    for c in range(2):
        for pm in range(2):
            parts = []
            for g in range(2):
                for x in range(2):
                    parts.append(rows_ref[g * SLABS : (g + 1) * SLABS, start + x * 4 + pm * 2 + c, :])
            lanes.append(jnp.concatenate(parts, axis=0))
    high, low = halves(jnp.concatenate(lanes, axis=1))
    right = jnp.concatenate([high, high, low], axis=0)
    by_cos = dot(jnp.concatenate(table_left(table_ref, 0), axis=1), right)
    by_sin = dot(jnp.concatenate(table_left(table_ref, 1), axis=1), right)
    real = by_cos[:, :N] + by_sin[:, N:]
    imag = by_cos[:, N:] - by_sin[:, :N]
    mirror_real = by_cos[:, :N] - by_sin[:, N:]
    mirror_imag = by_cos[:, N:] + by_sin[:, :N]

    def partner(mirror):
        return jnp.where(first == 1, mirror, jnp.concatenate([mirror[:, HALF:], mirror[:, :HALF]], axis=1))

    mirror_real = partner(mirror_real)
    mirror_imag = partner(mirror_imag)
    scale = amplitude * lax.rsqrt(real * real + imag * imag + SOFTEN)
    zero_real = 0.5 * (real + mirror_real)
    zero_imag = 0.5 * (imag - mirror_imag)
    top_real = 0.5 * (imag + mirror_imag)
    top_imag = 0.5 * (mirror_real - real)
    zero_scale = amplitude * lax.rsqrt(zero_real * zero_real + zero_imag * zero_imag + SOFTEN)
    top_scale = nyquist * lax.rsqrt(top_real * top_real + top_imag * top_imag + SOFTEN)
    packed = (lax.broadcasted_iota(jnp.int32, (N, N), 1) & (HALF - 1)) == 0
    new_real = jnp.where(packed, zero_scale * zero_real - top_scale * top_imag, scale * real)
    new_imag = jnp.where(packed, zero_scale * zero_imag + top_scale * top_real, scale * imag)
    return turn(table_ref, new_real, new_imag, 1)


def part_of(result, x, pm, c):
    lane = (c * 2 + pm) * HALF
    return result[x * SLABS : (x + 1) * SLABS, lane : lane + HALF]


def once_kernel(
    place_ref, got_ref, flip_hbm, table_hbm,
    out_ref, even_hbm,
    rows_ref, code_ref, flip_ref, table_ref, even_ref, sem,
):
    first = place_ref[0]
    copies = [fetch(flip_hbm, flip_ref, sem.at[0]), fetch(table_hbm, table_ref, sem.at[1])]
    rows_ref[...] = decoded(got_ref[...])
    copies[0].wait()
    amplitude, nyquist = amplitudes(first, rows_ref, flip_ref)
    even_ref[:N] = amplitude
    even_ref[N:] = nyquist
    saved = fetch(even_ref, even_hbm, sem.at[0])
    copies[1].wait()
    result = project(first, rows_ref, 24, amplitude, nyquist, table_ref)
    for pm in range(2):
        for c in range(2):
            for g in range(2):
                for x in range(2):
                    rows_ref[g * SLABS : (g + 1) * SLABS, x * 4 + pm * 2 + c, :] = part_of(result, g * 2 + x, pm, c)
    for copy in send_out(rows_ref, code_ref, out_ref, sem.at[pl.ds(2, BLOCKS)]) + [saved]:
        copy.wait()


def again_kernel(
    place_ref, got_ref, even_hbm, table_hbm,
    out_ref,
    rows_ref, code_ref, table_ref, even_ref, sem,
):
    sign = place_ref[1].astype(jnp.float32)
    copies = [fetch(table_hbm, table_ref, sem.at[0]), fetch(even_hbm, even_ref, sem.at[1])]
    rows_ref[:, :8, :] = decoded(got_ref[...])
    for copy in copies:
        copy.wait()
    result = project(place_ref[0], rows_ref, 0, even_ref[:N], even_ref[N:], table_ref)
    for pm in range(2):
        for c in range(2):
            for x in range(PLANES):
                q = x * 4 + pm * 2 + c
                part = part_of(result, x, pm, c)
                rows_ref[:SLABS, q, :] = part
                rows_ref[SLABS:, q, :] = sign * part
    for copy in send_out(rows_ref, code_ref, out_ref, sem.at[pl.ds(2, BLOCKS)]):
        copy.wait()


EVEN = jax.ShapeDtypeStruct((2 * N, N), jnp.float32)


def project_once(place, got, t):
    return call(
        once_kernel,
        (PACKET, EVEN),
        in_specs=[smem()] + spec_vmem(1) + [hbm()] * 2,
        out_specs=(hbm(), hbm()),
        scratch_shapes=[
            scratch(32),
            code_scratch(8),
            pltpu.VMEM((3, N, N), jnp.bfloat16),
            table_scratch(4 * N),
            pltpu.VMEM((2 * N, N), jnp.float32),
            sems(2 + BLOCKS),
        ],
    )(place, got, t["flips"], t["slab"])


def project_again(place, got, even, t):
    return call(
        again_kernel,
        WIDE_PACKET,
        in_specs=[smem()] + spec_vmem(1) + [hbm()] * 2,
        out_specs=hbm(),
        scratch_shapes=[
            scratch(16),
            code_scratch(16),
            table_scratch(4 * N),
            pltpu.VMEM((2 * N, N), jnp.float32),
            sems(2 + BLOCKS),
        ],
    )(place, got, even, t["slab"])


def exchange(packet):
    return lax.all_to_all(packet, BOTH, split_axis=0, concat_axis=0, tiled=True)


def swap(array):
    return lax.ppermute(array, "grp", [(0, 1), (1, 0)])


def local(patterns, probabilities, source_row, target_row, support, density):
    t = tables()
    group = lax.axis_index("grp")
    slab = lax.axis_index("slab")
    device = group * SLABS + slab
    place = jnp.stack([(device == 0).astype(jnp.int32), 1 - 2 * (device & 1)])
    pad = ((0, 0), (0, 128 - CAP))
    target = target_row[0, 0]

    fields = jnp.stack([density, support.astype(jnp.float32)])
    theirs = lax.dynamic_slice_in_dim(fields, 2 * (1 - group), 2, 1).astype(jnp.float16)
    other = swap(theirs)

    send = gather_rows(source_row[0, 0], probabilities[0], patterns[0])
    send, other = lax.optimization_barrier((send, other))
    got = lax.all_to_all(send, "slab", split_axis=0, concat_axis=0, tiled=True)

    own = lax.dynamic_slice_in_dim(fields, 2 * group, 2, 1)
    other = other.astype(jnp.float32)
    planes = jnp.concatenate([jnp.where(group == 0, own, other), jnp.where(group == 0, other, own)], axis=2)
    packet = first_field(planes[0], t)

    marks = prepare(jnp.pad(target, pad))
    sums = place_rows(got, target.reshape(SLABS // SOURCES, 1, TAKEN), marks, packet)
    got_sums = exchange(sums)

    theirs = lax.dynamic_slice_in_dim(sums, (1 - group) * 8, 8, 1)
    other = swap(jnp.concatenate([theirs, sums[:, 16:24]], axis=1))
    intensity = intensity_of(group.reshape(1), sums, other, t["flips"])

    packet, even = project_once(place, got_sums, t)
    field, code, packet = middle_field(exchange(packet), planes[1], planes[0], t)
    other = swap(lax.dynamic_slice_in_dim(code, (1 - group) * HALF, HALF, 1))
    got = exchange(project_again(place, exchange(packet), even, t))
    return (intensity, last_field(group.reshape(1), got, support, field, other, t))


def solution(mesh):
    return jax.shard_map(
        local,
        mesh=mesh,
        in_specs=(
            P("grp", "slab", None),
            P("grp", "slab", None),
            P("grp", "slab", None, None),
            P("grp", "slab", None, None),
            P("slab", "grp", None),
            P("slab", "grp", None),
        ),
        out_specs=(P("slab", "grp", None), P("slab", "grp", None)),
        check_vma=False,
    )
```

time: 477 us -> 156 us (0.33); the launches traced: 469 us -> 155 us
  matrix products: 171 us -> 0 us
  waiting for transfers between devices: 140 us -> 57.7 us
  Pallas kernels: 0 us -> 45.9 us
  starting transfers between devices: 74.8 us -> 36.8 us
  local copies, waits for them, and re-layouts: 40.9 us -> 8.4 us
  blocking collectives: 21.7 us -> 0 us
  between operations: 14.7 us -> 1.09 us
    dot_general x73 -> x0, matrix products: 171 us -> none  [the longest x40 90.4 us: along(): return jnp.einsum(form, field, table, precision=lax.Precision.HIGHEST)]
    all_to_all x11 -> x5, waiting for transfers between devices: 101 us -> 53.7 us  [the longest x4 38.1 us: exchange(): return lax.all_to_all(packet, BOTH, split_axis=0, concat_axis=0, tiled=True)]
    all_to_all x11 -> x5, starting transfers between devices: 74.2 us -> 27.3 us  [the longest x4 17.8 us: exchange(): return lax.all_to_all(packet, BOTH, split_axis=0, concat_axis=0, tiled=True)]
    pallas_call x0 -> x9, Pallas kernels: none -> 45.9 us  [the longest x1 11.3 us: gather_rows(): call(gather_kernel, jax.ShapeDtypeStruct((SLABS, SEND, 128), jnp.bfloat16...]
    psum x1 -> x0, blocking collectives: 21.7 us -> none  [local(): summed, weights = lax.psum((summed, weights), 'grp')]
    all_gather x2 -> x0, waiting for transfers between devices: 21.4 us -> none  [local(): whole = lax.all_gather(field, 'grp', axis=1, tiled=True)]
    all_to_all x15 -> x0, local copies, waits for them, and re-layouts: 17.2 us -> none  [the longest x4 4.52 us: local(): lax.all_to_all(real_part, 'slab', split_axis=1, concat_axis=0, tiled=True)]
    psum x1 -> x0, waiting for transfers between devices: 17 us -> none  [local(): summed, weights = lax.psum((summed, weights), 'grp')]
  transfers between devices with their start and end apart: 14 -> 8, of which waited for: 12 -> 6; matrix products, arithmetic and copies ran while one was open for 31% -> 4% of each run, Pallas kernels for 0% -> 15%
where the time goes in v2:
time: 156 us; the launch traced here: 155 us
  waiting for transfers between devices  57.7 us (37%)
  Pallas kernels  45.9 us (29%)
  starting transfers between devices  36.8 us (24%)
  local copies, waits for them, and re-layouts  8.4 us (5%)
  other arithmetic  5.13 us (3%)
    all_to_all x4, waiting for transfers between devices, exchange(): return lax.all_to_all(packet, BOTH, split_axis=0, concat_axis=0, tiled=True)  38.1 us
    all_to_all x4, starting transfers between devices, exchange(): return lax.all_to_all(packet, BOTH, split_axis=0, concat_axis=0, tiled=True)  17.8 us
    all_to_all x1, waiting for transfers between devices, local(): got = lax.all_to_all(send, 'slab', split_axis=0, concat_axis=0, tiled=True)  15.6 us
    pallas_call x1, Pallas kernels, gather_rows(): call(gather_kernel, jax.ShapeDtypeStruct((SLABS, SEND, 128), jnp.bfloat16...  11.3 us
    ppermute x3, starting transfers between devices, swap(): return lax.ppermute(array, 'grp', [(0, 1), (1, 0)])  9.51 us
    all_to_all x1, starting transfers between devices, local(): got = lax.all_to_all(send, 'slab', split_axis=0, concat_axis=0, tiled=True)  9.5 us
    pallas_call x1, Pallas kernels, place_rows(): call(place_kernel, jax.ShapeDtypeStruct((DEVS, 32, 128), jnp.int16), mib=...  7.99 us
    pallas_call x1, Pallas kernels, project_once(): call(once_kernel, (PACKET, EVEN), in_specs=[smem()] + spec_vmem(1) + [hbm...  7.01 us
  transfers between devices with their start and end apart: 8, of which 6 were waited for; matrix products, arithmetic and copies ran while one was open for 4% of the time, Pallas kernels for 15%

profile of v2, /device:TPU:1, one launch (start us, length us, event | category | flops | bytes accessed | tf_op | source)
XLA Modules:
  0.0 155.0 jit_solution(15504142346250282732)
XLA Ops:
  0.6 1.1 convert_bitcast_fusion
  1.7 1.0 fusion.4
  2.7 3.7 %collective-permute-start = (f16[2,2,128,256]{3,2,1,0:T(8,128)(2,1)S(1)}, f16[2,2,128,256]{3,2,1,0:T(8,128)(2,1)S(1)}, u32[]{:S(2)}, u32[]{:S(2)}) collective-permute-start(f16[2,2,128,256]{3,2,1,0:T(8,128)(2,1)S(1)} %fusion.4), channel_id=1, source_target_pairs={{0,64},{64,0},{1,65},{65,1},{2,66},{66,2},{3,67},{67,3},{4,68},{68... | collective-permute-start | bytes 786440 | tf_op jit(solution)/shard_map/ppermute | solution.py:651
  7.1 11.3 %shard_map.113 = bf16[64,88,128]{2,1,0:T(8,128)(2,1)} custom-call(s32[64,80]{1,0:T(8,128)} %bitcast.20, s32[64,80]{1,0:T(8,128)} %bitcast.21, bf16[256,32]{1,0:T(8,128)(2,1)} %bitcast.19, bf16[256,16384]{1,0:T(8,128)(2,1)} %bitcast.16), custom_call_target="tpu_custom_call" | custom-call | flops 268435456 | bytes 33554432 | tf_op jit(solution)/shard_map/pallas_call | solution.py:219
  18.5 9.5 %all-to-all-start = ((bf16[64,88,128]{2,1,0:T(8,128)(2,1)}), bf16[64,88,128]{2,1,0:T(8,128)(2,1)S(1)}, u32[]{:S(2)}, u32[]{:S(2)}) async-start(bf16[64,88,128]{2,1,0:T(8,128)(2,1)} %shard_map.113), calls=%async_computation | async-start | bytes 2883584 | tf_op jit(solution)/shard_map/all_to_all | solution.py:669
  28.7 2.1 %shard_map.114.mark_hbm = bf16[5120,128]{1,0:T(8,128)(2,1)S(1)} custom-call(s32[64,128]{1,0:T(8,128)S(1)} %pad.4.column_ref), custom_call_target="tpu_custom_call" | custom-call | tf_op jit(solution)/shard_map/pallas_call | solution.py:266
  30.8 1.2 convert_select_fusion
  32.0 0.9 fusion.5
  33.3 1.5 shard_map.115.packet_ref
  34.8 15.6 %all-to-all-done.got_ref = bf16[64,88,128]{2,1,0:T(8,128)(2,1)S(1)} async-done(((bf16[64,88,128]{2,1,0:T(8,128)(2,1)}), bf16[64,88,128]{2,1,0:T(8,128)(2,1)S(1)}, u32[]{:S(2)}, u32[]{:S(2)}) %all-to-all-start) | async-done | bytes 1441824 | tf_op jit(solution)/shard_map/all_to_all | solution.py:669
  51.2 8.0 %shard_map.116.own_ref = s16[128,32,128]{2,1,0:T(8,128)(2,1)} custom-call(bf16[64,88,128]{2,1,0:T(8,128)(2,1)S(1)} %all-to-all-done.got_ref, s32[4,1,1280]{2,1,0:T(1,128)S(1)} %copy-done.13, bf16[5120,128]{1,0:T(8,128)(2,1)S(1)} %shard_map.114.mark_hbm, s16[128,8,128]{2,1,0:T(8,128)(2,1)S(1)} %shard_map.115.packet_ref), custom_call_target="tpu_custom_call" | custom-call | tf_op jit(solution)/shard_map/pallas_call | solution.py:313
  59.2 4.2 %all-to-all-start.1 = ((s16[128,32,128]{2,1,0:T(8,128)(2,1)}), s16[128,32,128]{2,1,0:T(8,128)(2,1)S(1)}, u32[]{:S(2)}, u32[]{:S(2)}) async-start(s16[128,32,128]{2,1,0:T(8,128)(2,1)} %shard_map.116.own_ref), calls=%async_computation.1 | async-start | bytes 2097152 | tf_op jit(solution)/shard_map/all_to_all | solution.py:647
  63.5 18.9 %all-to-all-done.1.got_ref = s16[128,32,128]{2,1,0:T(8,128)(2,1)S(1)} async-done(((s16[128,32,128]{2,1,0:T(8,128)(2,1)}), s16[128,32,128]{2,1,0:T(8,128)(2,1)S(1)}, u32[]{:S(2)}, u32[]{:S(2)}) %all-to-all-start.1) | async-done | bytes 1048608 | tf_op jit(solution)/shard_map/all_to_all | solution.py:647
  82.4 1.0 copy-done.4
  83.5 1.0 copy-done.7
  84.5 7.0 %shard_map.118 = (s16[128,8,128]{2,1,0:T(8,128)(2,1)}, f32[512,256]{1,0:T(8,128)S(1)}) custom-call(s32[2]{0:T(128)S(1)} %pad_add_fusion.1.place_ref, s16[128,32,128]{2,1,0:T(8,128)(2,1)S(1)} %all-to-all-done.1.got_ref, bf16[3,256,256]{2,1,0:T(8,128)(2,1)S(1)} %copy-done.7, bf16[1024,256]{1,0:T(8,128)(2,1)S(1)} %copy-done.4), custom_call_target="tpu_custom_call" | custom-call | tf_op jit(solution)/shard_map/pallas_call | solution.py:614
  92.3 4.7 %all-to-all-start.2 = ((s16[128,8,128]{2,1,0:T(8,128)(2,1)}), s16[128,8,128]{2,1,0:T(8,128)(2,1)S(1)}, u32[]{:S(2)}, u32[]{:S(2)}) async-start(s16[128,8,128]{2,1,0:T(8,128)(2,1)} %get-tuple-element.11), calls=%async_computation.2 | async-start | bytes 524288 | tf_op jit(solution)/shard_map/all_to_all | solution.py:647
  97.0 11.0 %all-to-all-done.2.got_ref = s16[128,8,128]{2,1,0:T(8,128)(2,1)S(1)} async-done(((s16[128,8,128]{2,1,0:T(8,128)(2,1)}), s16[128,8,128]{2,1,0:T(8,128)(2,1)S(1)}, u32[]{:S(2)}, u32[]{:S(2)}) %all-to-all-start.2) | async-done | bytes 262176 | tf_op jit(solution)/shard_map/all_to_all | solution.py:647
  108.0 1.0 copy-done.6
  109.0 4.3 %shard_map.119 = (f32[2,256,256]{2,1,0:T(8,128)S(1)}, s16[2,256,256]{2,1,0:T(8,128)(2,1)S(1)}, s16[128,8,128]{2,1,0:T(8,128)(2,1)}) custom-call(s16[128,8,128]{2,1,0:T(8,128)(2,1)S(1)} %all-to-all-done.2.got_ref, f32[2,256,256]{2,1,0:T(8,128)S(1)} %copy-done.6, f32[2,256,256]{2,1,0:T(8,128)S(1)} %get-tuple-element.19.density_ref.density_hbm, ...), custom_call_target="tpu_custom_call" | custom-call | tf_op jit(solution)/shard_map/pallas_call | solution.py:488
  114.2 4.4 %all-to-all-start.3 = ((s16[128,8,128]{2,1,0:T(8,128)(2,1)}), s16[128,8,128]{2,1,0:T(8,128)(2,1)S(1)}, u32[]{:S(2)}, u32[]{:S(2)}) async-start(s16[128,8,128]{2,1,0:T(8,128)(2,1)} %get-tuple-element.12), calls=%async_computation.3 | async-start | bytes 524288 | tf_op jit(solution)/shard_map/all_to_all | solution.py:647
  118.6 1.1 constant_dynamic-slice_fusion.1
  119.7 0.9 pad_add_fusion
  120.6 2.9 %collective-permute-start.1 = (s16[128,16,128]{2,1,0:T(8,128)(2,1)}, s16[128,16,128]{2,1,0:T(8,128)(2,1)}, u32[]{:S(2)}, u32[]{:S(2)}) collective-permute-start(s16[128,16,128]{2,1,0:T(8,128)(2,1)} %pad_add_fusion), channel_id=1, source_target_pairs={{0,64},{64,0},{1,65},{65,1},{2,66},{66,2},{3,67},{67,3},{4,68},{68... | collective-permute-start | bytes 1572872 | tf_op jit(solution)/shard_map/ppermute | solution.py:651
  123.5 6.2 %all-to-all-done.3.got_ref = s16[128,8,128]{2,1,0:T(8,128)(2,1)S(1)} async-done(((s16[128,8,128]{2,1,0:T(8,128)(2,1)}), s16[128,8,128]{2,1,0:T(8,128)(2,1)S(1)}, u32[]{:S(2)}, u32[]{:S(2)}) %all-to-all-start.3) | async-done | bytes 262176 | tf_op jit(solution)/shard_map/all_to_all | solution.py:647
  129.7 4.4 %shard_map.120 = s16[128,16,128]{2,1,0:T(8,128)(2,1)} custom-call(s32[2]{0:T(128)S(1)} %pad_add_fusion.1.place_ref, s16[128,8,128]{2,1,0:T(8,128)(2,1)S(1)} %all-to-all-done.3.got_ref, f32[512,256]{1,0:T(8,128)S(1)} %copy-done.12, bf16[1024,256]{1,0:T(8,128)(2,1)S(1)} %copy-done.5), custom_call_target="tpu_custom_call" | custom-call | tf_op jit(solution)/shard_map/pallas_call | solution.py:631
  134.0 4.5 %all-to-all-start.4 = ((s16[128,16,128]{2,1,0:T(8,128)(2,1)}), s16[128,16,128]{2,1,0:T(8,128)(2,1)S(1)}, u32[]{:S(2)}, u32[]{:S(2)}) async-start(s16[128,16,128]{2,1,0:T(8,128)(2,1)} %shard_map.120), calls=%async_computation.4 | async-start | bytes 1048576 | tf_op jit(solution)/shard_map/all_to_all | solution.py:647
  138.6 3.0 %collective-permute-start.2 = (s16[2,128,256]{2,1,0:T(8,128)(2,1)S(1)}, s16[2,128,256]{2,1,0:T(8,128)(2,1)S(1)}, u32[]{:S(2)}, u32[]{:S(2)}) collective-permute-start(s16[2,128,256]{2,1,0:T(8,128)(2,1)S(1)} %constant_dynamic-slice_fusion), channel_id=1, source_target_pairs={{0,64},{64,0},{1,65},{65,1},{2,66},{66,2},{3,67},{67,3},{4,68},{68... | collective-permute-start | bytes 393224 | tf_op jit(solution)/shard_map/ppermute | solution.py:651
  141.5 4.4 %shard_map.117 = f32[4,128,256]{2,1,0:T(8,128)} custom-call(s32[1]{0:T(128)} %bitcast.group_ref, s16[128,32,128]{2,1,0:T(8,128)(2,1)} %shard_map.116.own_ref, s16[128,16,128]{2,1,0:T(8,128)(2,1)} %collective-permute-done.1.other_ref, bf16[3,256,256]{2,1,0:T(8,128)(2,1)S(1)} %copy-done.8), custom_call_target="tpu_custom_call" | custom-call | tf_op jit(solution)/shard_map/pallas_call | solution.py:344
  146.0 4.0 %collective-permute-done.2.other_ref = s16[2,128,256]{2,1,0:T(8,128)(2,1)S(1)} collective-permute-done((s16[2,128,256]{2,1,0:T(8,128)(2,1)S(1)}, s16[2,128,256]{2,1,0:T(8,128)(2,1)S(1)}, u32[]{:S(2)}, u32[]{:S(2)}) %collective-permute-start.2) | collective-permute-done | bytes 131104 | tf_op jit(solution)/shard_map/ppermute | solution.py:651
  149.9 2.0 %all-to-all-done.4.got_ref = s16[128,16,128]{2,1,0:T(8,128)(2,1)S(1)} async-done(((s16[128,16,128]{2,1,0:T(8,128)(2,1)}), s16[128,16,128]{2,1,0:T(8,128)(2,1)S(1)}, u32[]{:S(2)}, u32[]{:S(2)}) %all-to-all-start.4) | async-done | bytes 524320 | tf_op jit(solution)/shard_map/all_to_all | solution.py:647
  151.9 2.9 %shard_map.121 = f32[4,128,256]{2,1,0:T(8,128)} custom-call(s32[1]{0:T(128)} %bitcast.group_ref, s16[128,16,128]{2,1,0:T(8,128)(2,1)S(1)} %all-to-all-done.4.got_ref, s32[4,128,256]{2,1,0:T(8,128)S(1)} %copy-done.3, f32[2,256,256]{2,1,0:T(8,128)S(1)} %copy-done.10, s16[2,128,256]{2,1,0:T(8,128)(2,1)S(1)} %collective-permute-done.2.other_ref, ...), custom_call_target="tpu_custom_call" | custom-call | tf_op jit(solution)/shard_map/pallas_call | solution.py:508
  (36 shorter events, 4.3 us)
Async XLA Ops:
  0.6 5.8 %copy-start.15 = (bf16[1,256,32]{1,2,0:T(8,128)(2,1)S(1)}, bf16[1,256,32]{1,2,0:T(8,128)(2,1)}, u32[]{:S(2)}) copy-start(bf16[1,256,32]{1,2,0:T(8,128)(2,1)} %param.11) | copy-start | bytes 49156
  2.7 15.7 %collective-permute-start = (f16[2,2,128,256]{3,2,1,0:T(8,128)(2,1)S(1)}, f16[2,2,128,256]{3,2,1,0:T(8,128)(2,1)S(1)}, u32[]{:S(2)}, u32[]{:S(2)}) collective-permute-start(f16[2,2,128,256]{3,2,1,0:T(8,128)(2,1)S(1)} %fusion.4), channel_id=1, source_target_pairs={{0,64},{64,0},{1,65},{65,1},{2,66},{66,2},{3,67},{67,3},{4,68},{68... | collective-permute-start | bytes 786440 | tf_op jit(solution)/shard_map/ppermute | solution.py:651
  18.5 9.5 %copy-start.14 = (s32[1,1,64,80]{3,2,1,0:T(8,128)S(1)}, s32[1,1,64,80]{3,2,1,0:T(8,128)}, u32[]{:S(2)}) copy-start(s32[1,1,64,80]{3,2,1,0:T(8,128)} %param.13) | copy-start | bytes 61444
  18.5 32.0 %all-to-all-start = ((bf16[64,88,128]{2,1,0:T(8,128)(2,1)}), bf16[64,88,128]{2,1,0:T(8,128)(2,1)S(1)}, u32[]{:S(2)}, u32[]{:S(2)}) async-start(bf16[64,88,128]{2,1,0:T(8,128)(2,1)} %shard_map.113), calls=%async_computation | async-start | bytes 2883584 | tf_op jit(solution)/shard_map/all_to_all | solution.py:669
  32.0 1.3 copy-start
  50.5 0.7 copy-start.13
  59.2 23.2 %all-to-all-start.1 = ((s16[128,32,128]{2,1,0:T(8,128)(2,1)}), s16[128,32,128]{2,1,0:T(8,128)(2,1)S(1)}, u32[]{:S(2)}, u32[]{:S(2)}) async-start(s16[128,32,128]{2,1,0:T(8,128)(2,1)} %shard_map.116.own_ref), calls=%async_computation.1 | async-start | bytes 2097152 | tf_op jit(solution)/shard_map/all_to_all | solution.py:647
  63.4 44.6 %copy-start.1 = (bf16[1536,256]{1,0:T(8,128)(2,1)S(1)}, bf16[1536,256]{1,0:T(8,128)(2,1)}, u32[]{:S(2)}) copy-start(bf16[1536,256]{1,0:T(8,128)(2,1)} %constant.35.clone.table_hbm.forward_hbm) | copy-start | bytes 2359300
  63.4 44.6 %copy-start.2 = (bf16[1536,256]{1,0:T(8,128)(2,1)S(1)}, bf16[1536,256]{1,0:T(8,128)(2,1)}, u32[]{:S(2)}) copy-start(bf16[1536,256]{1,0:T(8,128)(2,1)} %constant.36.clone.inverse_hbm) | copy-start | bytes 2359300
  82.4 1.0 copy-start.4
  83.5 1.0 copy-start.7
  91.5 0.8 copy-start.11
  92.3 15.7 %all-to-all-start.2 = ((s16[128,8,128]{2,1,0:T(8,128)(2,1)}), s16[128,8,128]{2,1,0:T(8,128)(2,1)S(1)}, u32[]{:S(2)}, u32[]{:S(2)}) async-start(s16[128,8,128]{2,1,0:T(8,128)(2,1)} %get-tuple-element.11), calls=%async_computation.2 | async-start | bytes 524288 | tf_op jit(solution)/shard_map/all_to_all | solution.py:647
  108.0 1.0 copy-start.6
  113.4 0.8 copy-start.9
  114.2 15.5 %copy-start.5 = (bf16[1024,256]{1,0:T(8,128)(2,1)S(1)}, bf16[1024,256]{1,0:T(8,128)(2,1)}, u32[]{:S(2)}) copy-start(bf16[1024,256]{1,0:T(8,128)(2,1)} %constant.37.clone.table_hbm) | copy-start | bytes 1572868
  114.2 15.5 %copy-start.12 = (f32[512,256]{1,0:T(8,128)S(1)}, f32[512,256]{1,0:T(8,128)}, u32[]{:S(2)}) copy-start(f32[512,256]{1,0:T(8,128)} %copy-done.11) | copy-start | bytes 1572868
  114.2 15.5 %all-to-all-start.3 = ((s16[128,8,128]{2,1,0:T(8,128)(2,1)}), s16[128,8,128]{2,1,0:T(8,128)(2,1)S(1)}, u32[]{:S(2)}, u32[]{:S(2)}) async-start(s16[128,8,128]{2,1,0:T(8,128)(2,1)} %get-tuple-element.12), calls=%async_computation.3 | async-start | bytes 524288 | tf_op jit(solution)/shard_map/all_to_all | solution.py:647
  120.6 20.9 %collective-permute-start.1 = (s16[128,16,128]{2,1,0:T(8,128)(2,1)}, s16[128,16,128]{2,1,0:T(8,128)(2,1)}, u32[]{:S(2)}, u32[]{:S(2)}) collective-permute-start(s16[128,16,128]{2,1,0:T(8,128)(2,1)} %pad_add_fusion), channel_id=1, source_target_pairs={{0,64},{64,0},{1,65},{65,1},{2,66},{66,2},{3,67},{67,3},{4,68},{68... | collective-permute-start | bytes 1572872 | tf_op jit(solution)/shard_map/ppermute | solution.py:651
  129.7 11.9 %copy-start.8 = (bf16[3,256,256]{2,1,0:T(8,128)(2,1)S(1)}, bf16[3,256,256]{2,1,0:T(8,128)(2,1)}, u32[]{:S(2)}) copy-start(bf16[3,256,256]{2,1,0:T(8,128)(2,1)} %constant.38.clone.flip_ref.flip_hbm) | copy-start | bytes 1179652
  134.0 17.9 %all-to-all-start.4 = ((s16[128,16,128]{2,1,0:T(8,128)(2,1)}), s16[128,16,128]{2,1,0:T(8,128)(2,1)S(1)}, u32[]{:S(2)}, u32[]{:S(2)}) async-start(s16[128,16,128]{2,1,0:T(8,128)(2,1)} %shard_map.120), calls=%async_computation.4 | async-start | bytes 1048576 | tf_op jit(solution)/shard_map/all_to_all | solution.py:647
  138.5 13.4 %copy-start.3 = (s32[4,128,256]{2,1,0:T(8,128)S(1)}, s32[4,128,256]{2,1,0:T(8,128)}, u32[]{:S(2)}) copy-start(s32[4,128,256]{2,1,0:T(8,128)} %support_hbm.1) | copy-start | bytes 1572868
  138.5 13.4 %copy-start.10 = (f32[2,256,256]{2,1,0:T(8,128)S(1)}, f32[2,256,256]{2,1,0:T(8,128)}, u32[]{:S(2)}) copy-start(f32[2,256,256]{2,1,0:T(8,128)} %copy-done.9) | copy-start | bytes 1572868
  138.6 11.4 %collective-permute-start.2 = (s16[2,128,256]{2,1,0:T(8,128)(2,1)S(1)}, s16[2,128,256]{2,1,0:T(8,128)(2,1)S(1)}, u32[]{:S(2)}, u32[]{:S(2)}) collective-permute-start(s16[2,128,256]{2,1,0:T(8,128)(2,1)S(1)} %constant_dynamic-slice_fusion), channel_id=1, source_target_pairs={{0,64},{64,0},{1,65},{65,1},{2,66},{66,2},{3,67},{67,3},{4,68},{68... | collective-permute-start | bytes 393224 | tf_op jit(solution)/shard_map/ppermute | solution.py:651

commit v3 on v2

v3 whole, which is shorter than its diff:
```python
import functools

import jax
import jax.numpy as jnp
import ml_dtypes
import numpy as np
from jax import lax
from jax.experimental import pallas as pl
from jax.experimental.pallas import tpu as pltpu
from jax.sharding import PartitionSpec as P

N = 256
HALF = N // 2
PLANES = 4
SLABS = 64
DEVS = 128
CAP = 80
ROWS = 4096
BETA = 0.9
SOFTEN = 0.25
BOTH = ("grp", "slab")
MIB = 1024 * 1024


def split_table(table):
    high = table.astype(np.float32).astype(ml_dtypes.bfloat16)
    low = (table - high.astype(np.float64)).astype(np.float32).astype(ml_dtypes.bfloat16)
    return (jnp.asarray(high), jnp.asarray(low))


def phase(rows, columns):
    angle = 2.0 * np.pi / N * ((rows[:, None] * columns[None, :]) % N)
    return (np.cos(angle) / np.sqrt(N), np.sin(angle) / np.sqrt(N))


@functools.cache
def tables():
    z = np.arange(N)
    cos, sin = phase(z, np.arange(HALF))
    nyquist = np.cos(np.pi * z) / np.sqrt(N)
    forward_z = np.concatenate([cos, -sin], axis=1)
    forward_z[:, HALF] = nyquist
    first = np.arange(DEVS)
    frequency = np.concatenate([first, np.where(first == 0, HALF, N - first)])
    cos_y, sin_y = phase(frequency, z)
    order = (np.arange(PLANES)[:, None] + PLANES * np.arange(SLABS)[None, :]).reshape(-1)
    cos_x, sin_x = phase(order, order)

    def split(parts):
        rows = []
        for part in parts:
            high = part.astype(np.float32).astype(ml_dtypes.bfloat16)
            rows += [high, (part - high.astype(np.float64)).astype(np.float32).astype(ml_dtypes.bfloat16)]
        return jnp.asarray(np.concatenate(rows, axis=0))

    return dict(field=split([cos_y, sin_y, forward_z]), slab=split([cos_x, sin_x]))


def halves(values):
    high = values.astype(jnp.bfloat16)
    return (high, (values - high.astype(jnp.float32)).astype(jnp.bfloat16))


def dot(left, right):
    return jnp.dot(left, right, preferred_element_type=jnp.float32)


def table_at(ref, index):
    high = ref[2 * index * N : (2 * index + 1) * N]
    low = ref[(2 * index + 1) * N : (2 * index + 2) * N]
    return [high, low, high]


def along_lanes(values, ref, index, back=False):
    high, low = halves(values)
    top, rest, unused = table_at(ref, index)
    left = jnp.concatenate([high, low, high], axis=1)
    if back:
        right = jnp.concatenate([top, top, rest], axis=1)
        return lax.dot_general(left, right, (((1,), (1,)), ((), ())), preferred_element_type=jnp.float32)
    return dot(left, jnp.concatenate([top, top, rest], axis=0))


def turn(ref, real, imag, sign, back=None):
    real = halves(real)
    imag = halves(imag)
    straight = [jnp.concatenate([a, b], axis=1) for a, b in zip(real, imag)]
    if sign > 0:
        crossed = [jnp.concatenate([-b, a], axis=1) for a, b in zip(real, imag)]
    else:
        crossed = [jnp.concatenate([b, -a], axis=1) for a, b in zip(real, imag)]
    left = table_at(ref, 0) + table_at(ref, 1)
    right = [straight[0], straight[0], straight[1], crossed[0], crossed[0], crossed[1]]
    right = jnp.concatenate(right, axis=0)
    if back is None:
        return dot(jnp.concatenate(left, axis=1), right)
    left = jnp.concatenate(left, axis=0)[:, :back]
    return lax.dot_general(left, right, (((0,), (0,)), ((), ())), preferred_element_type=jnp.float32)


def permutation(size, matches):
    row = lax.broadcasted_iota(jnp.int32, (size, size), 0)
    column = lax.broadcasted_iota(jnp.int32, (size, size), 1)
    return matches(row, column).astype(jnp.bfloat16)


FINE = 2.0**14
OCTAVE = 32767.0 / 30.0
LOG2 = float(np.log(2.0))


def coded(values):
    size = jnp.minimum(jnp.log(1.0 + FINE * jnp.abs(values)) * (OCTAVE / LOG2), 32767.0)
    whole = (size + 0.5).astype(jnp.int32)
    return jnp.where(values < 0.0, -whole, whole).astype(jnp.int16)


def decoded(codes):
    values = codes.astype(jnp.int32).astype(jnp.float32)
    size = (jnp.exp(jnp.abs(values) * (LOG2 / OCTAVE)) - 1.0) * (1.0 / FINE)
    return jnp.where(values < 0.0, -size, size)


def call(kernel, out_shape, mib=16, **kwargs):
    return pl.pallas_call(
        kernel,
        out_shape=out_shape,
        compiler_params=pltpu.CompilerParams(vmem_limit_bytes=mib * MIB),
        **kwargs,
    )


def spec_vmem(count):
    return [pl.BlockSpec(memory_space=pltpu.VMEM)] * count


def smem():
    return pl.BlockSpec(memory_space=pltpu.SMEM)


def hbm():
    return pl.BlockSpec(memory_space=pltpu.HBM)


def fetch(source, target, sem):
    copy = pltpu.make_async_copy(source, target, sem)
    copy.start()
    return copy


BLOCKS = 4


def send_out(rows_ref, code_ref, out_ref, sems):
    count = code_ref.shape[1]
    copies = []
    for block in range(BLOCKS):
        devices = pl.ds(block * (DEVS // BLOCKS), DEVS // BLOCKS)
        code_ref[devices] = coded(rows_ref[devices, :count, :])
        copies.append(fetch(code_ref.at[devices], out_ref.at[devices], sems.at[block]))
    return copies


def code_scratch(rows):
    return pltpu.VMEM((DEVS, rows, 128), jnp.int16)


def sems(count):
    return pltpu.SemaphoreType.DMA((count,))


CUTS = 8
CUT = DEVS // CUTS
EMPTY = 8
SEND = 88


def gather_kernel(
    index_ref, table_ref, probabilities_ref, patterns_ref, out_hbm, block_ref, rows_ref, picked_ref, out_ref, sem
):
    def copy(cut):
        part = pl.ds(cut * CUT * 128, CUT * 128)
        return pltpu.make_async_copy(patterns_ref.at[:, part], block_ref.at[:, part], sem.at[cut])

    for cut in range(CUTS):
        copy(cut).start()
    rows_ref[:EMPTY] = jnp.zeros((EMPTY, 128), jnp.float32)
    left = probabilities_ref[0]
    weight = jnp.sum(left.astype(jnp.float32), axis=1, keepdims=True).astype(jnp.bfloat16).astype(jnp.float32)
    orientation = table_ref[...] >> 7
    weights = jnp.zeros((SLABS, CAP), jnp.float32)
    for r in range(32):
        weights = jnp.where(orientation == r, weight[r : r + 1], weights)
    weights = jnp.concatenate([weights, jnp.zeros((SLABS, 128 - CAP), jnp.float32)], axis=1)
    out_ref[:, CAP:, :] = jnp.broadcast_to(weights[:, None, :], (SLABS, 8, 128)).astype(jnp.bfloat16)
    for cut in range(CUTS):
        copy(cut).wait()
        part = dot(left, block_ref[:, cut * CUT * 128 : (cut + 1) * CUT * 128])
        part = part.astype(jnp.bfloat16).astype(jnp.float32)
        for d in range(CUT):
            rows_ref[pl.ds(EMPTY + cut * CUT + d, 32, stride=128), :] = part[:, d * 128 : (d + 1) * 128]

    sent = []
    for part in range(BLOCKS):
        owners = SLABS // BLOCKS
        for o in range(part * owners, (part + 1) * owners):
            for c in range(CAP):
                picked_ref[o * CAP + c : o * CAP + c + 1, :] = rows_ref[pl.ds(EMPTY + index_ref[o, c], 1), :]
        picked = picked_ref[part * owners * CAP : (part + 1) * owners * CAP].astype(jnp.bfloat16)
        block = pl.ds(part * owners, owners)
        out_ref[block, :CAP, :] = picked.reshape(owners, CAP, 128)
        sent.append(fetch(out_ref.at[block], out_hbm.at[block], sem.at[part]))
    for copy in sent:
        copy.wait()


def gather_rows(source, probabilities, patterns):
    return call(
        gather_kernel,
        jax.ShapeDtypeStruct((SLABS, SEND, 128), jnp.bfloat16),
        mib=60,
        cost_estimate=pl.CostEstimate(flops=2 * 32 * 256 * 16384, bytes_accessed=32 * MIB, transcendentals=0),
        in_specs=[smem()] + spec_vmem(2) + [hbm()],
        out_specs=hbm(),
        scratch_shapes=[
            pltpu.VMEM((256, DEVS * 128), jnp.bfloat16),
            pltpu.VMEM((EMPTY + ROWS, 128), jnp.float32),
            pltpu.VMEM((SLABS * CAP, 128), jnp.float32),
            pltpu.VMEM((SLABS, SEND, 128), jnp.bfloat16),
            sems(CUTS),
        ],
    )(source, source, probabilities, patterns)


SOURCES = 16
TAKEN = SOURCES * CAP
SLOTS = SLABS * CAP


def moved(target):
    y = (target >> 1) & (N - 1)
    pm = y >> 7
    j = jnp.where(pm == 1, (N - y) & (HALF - 1), y)
    return j * 16 + pm * 8 + (target >> 9) * 2 + (target & 1)


def columns_of(table):
    count = table.shape[0]
    square = jnp.concatenate([table, jnp.zeros((128 - count, 128), table.dtype)], axis=0).T
    return jnp.concatenate([square[:CAP, s : s + 1] for s in range(count)], axis=0)


def place_kernel(got_ref, row_ref, column_ref, packet_ref, out_ref, sum_ref, code_ref, sem):
    steps = SLABS // SOURCES
    code_ref[:, 24:, :] = packet_ref[...]
    last = got_ref[:, CAP:, :].astype(jnp.float32)[:, 0, :]
    total = jnp.zeros((32, 128), jnp.float32)
    lane = lax.broadcasted_iota(jnp.int32, (TAKEN, 128), 1).astype(jnp.float32).astype(jnp.bfloat16)
    zero = jnp.bfloat16(0)
    for step in range(steps):
        row = moved(row_ref[step])
        onehot = (lax.broadcasted_iota(jnp.int32, (512, TAKEN), 0) == (row & 511)).astype(jnp.bfloat16)
        rows = got_ref[step * SOURCES : (step + 1) * SOURCES, :CAP].reshape(TAKEN, 128)
        column = moved(column_ref[step * SOURCES : (step + 1) * SOURCES])
        mark = columns_of((((column >> 9) * 16) + (column & 15)).astype(jnp.float32))
        mark = jnp.broadcast_to(mark, (TAKEN, 128)).astype(jnp.bfloat16)
        above = [rows] + [jnp.where(mark >= jnp.bfloat16(16 * q), rows, zero) for q in range(1, 4)]
        parts = [jnp.where(mark < jnp.bfloat16(16 * q + 16), above[q], zero) for q in range(3)] + [above[3]]
        part = dot(onehot, jnp.concatenate(parts, axis=1))
        sum_ref[...] = part if step == 0 else sum_ref[...] + part
        weights = [last[step * SOURCES + s : step * SOURCES + s + 1, :CAP] for s in range(SOURCES)]
        weights = jnp.concatenate(weights, axis=1)
        device = lax.broadcasted_iota(jnp.int32, (32, TAKEN), 0) == ((row >> 4) & 31)
        left = jnp.where(device, weights, 0.0).astype(jnp.bfloat16)
        total += dot(left, jnp.where(mark == lane, jnp.bfloat16(1), zero))
    total = coded(total).astype(jnp.int32)
    sent = []
    for q in range(4):
        devices = pl.ds(q * 32, 32)
        part = sum_ref[:, q * 128 : (q + 1) * 128].reshape(32, 16, 128)
        code_ref[devices, :16, :] = coded(part)
        entries = total if q == 0 else jnp.concatenate([total[:, 16 * q :], total[:, : 16 * q]], axis=1)
        code_ref[devices, 16:24, :] = jnp.broadcast_to(entries[:, None, :], (32, 8, 128)).astype(jnp.int16)
        sent.append(fetch(code_ref.at[devices], out_ref.at[devices], sem.at[q]))
    for copy in sent:
        copy.wait()


def place_rows(got, row, column, packet):
    return call(
        place_kernel,
        jax.ShapeDtypeStruct((DEVS, 32, 128), jnp.int16),
        mib=28,
        in_specs=spec_vmem(4),
        out_specs=hbm(),
        scratch_shapes=[
            pltpu.VMEM((512, 512), jnp.float32),
            code_scratch(32),
            sems(4),
        ],
    )(got, row, column, packet)


def intensity_kernel(group_ref, own_ref, other_ref, out_ref):
    group = group_ref[0]
    own = decoded(own_ref[:, :24, :])
    other = decoded(other_ref[...])
    total = jnp.where(group == 0, own[:, :8, :], own[:, 8:16, :]) + other[:, :8, :]
    weights = own[:, 16, :] + other[:, 8, :]
    divisor = jnp.maximum(jnp.where(group == 0, weights[:, :8], weights[:, 8:16]), 1.0)
    wide = jnp.concatenate([total[:, q, :] / divisor[:, q : q + 1] for q in range(8)], axis=1)
    same = permutation(HALF, lambda row, column: row == column)
    mirrored = permutation(HALF, lambda row, column: ((row + column) & (HALF - 1)) == 0)
    flip = jnp.where(group == 0, same, mirrored)
    high, low = halves(wide)
    turned = dot(flip, high) + dot(flip, low)
    for x in range(PLANES):
        out_ref[x] = turned[:, x * N : (x + 1) * N]


def intensity_of(group, own, other):
    return call(
        intensity_kernel,
        jax.ShapeDtypeStruct((PLANES, HALF, N), jnp.float32),
        in_specs=[smem()] + spec_vmem(2),
        out_specs=spec_vmem(1)[0],
    )(group, own, other)


def amplitudes(first, got_ref):
    scale = 1.0 / jnp.maximum(got_ref[:SLABS, 16, :] + got_ref[SLABS:, 16, :], 1.0)
    got_ref[:SLABS, :16, :] = got_ref[:SLABS, :16, :] + got_ref[SLABS:, :16, :]
    amplitude = []
    for pm in range(2):
        columns = []
        for zh in range(2):
            planes = []
            for x in range(PLANES):
                q = (pm * PLANES + x) * 2 + zh
                planes.append(jnp.sqrt(got_ref[:SLABS, q, :] * scale[:, q : q + 1]))
            columns.append(jnp.concatenate(planes, axis=0))
        amplitude.append(jnp.concatenate(columns, axis=1))
    flip_z = permutation(N, lambda row, column: ((row + column) & (N - 1)) == 0)

    def frequency(index):
        return PLANES * (index & (SLABS - 1)) + (index >> 6)

    flip_x = permutation(N, lambda row, column: ((frequency(row) + frequency(column)) & (N - 1)) == 0)
    mirrored = []
    for pm in range(2):
        high, low = halves(amplitude[pm])
        high = dot(flip_x, high).astype(jnp.bfloat16)
        low = dot(flip_x, low).astype(jnp.bfloat16)
        mirrored.append(dot(high, flip_z) + dot(low, flip_z))
    even = []
    for pm in range(2):
        partner = jnp.where(first == 1, mirrored[pm], mirrored[1 - pm])
        even.append(0.5 * (amplitude[pm] + partner))
    amplitude = jnp.concatenate([part[:, :HALF] for part in even], axis=1)
    return (
        jnp.where(packed_lanes(), amplitude, 2.0 * amplitude),
        jnp.concatenate([part[:, HALF:] for part in even], axis=1),
    )


def packed_lanes():
    return (lax.broadcasted_iota(jnp.int32, (N, N), 1) & (HALF - 1)) == 0


def tile(values, row, column):
    return values[row * 128 : (row + 1) * 128, column * 128 : (column + 1) * 128]


def send_forward(field, table_ref, rows_ref):
    partly = along_lanes(field, table_ref, 2)
    parts = []
    for c in range(2):
        parts.append(jnp.concatenate([partly[x * N : (x + 1) * N, c * HALF : (c + 1) * HALF] for x in range(2)], axis=1))
    result = turn(table_ref, parts[0], parts[1], -1)
    for x in range(2):
        for pm in range(2):
            for c in range(2):
                rows_ref[:, x * 4 + pm * 2 + c, :] = tile(result, pm, c * 2 + x)


def image_from(rows_ref, table_ref, length):
    planes = rows_ref.shape[1] // 4
    parts = []
    for c in range(2):
        columns = []
        for x in range(planes):
            columns.append(jnp.concatenate([rows_ref[:, x * 4 + pm * 2 + c, :] for pm in range(2)], axis=0))
        parts.append(jnp.concatenate(columns, axis=1))
    partly = turn(table_ref, parts[0], parts[1], 1, length)
    rows = []
    for x in range(planes):
        real = partly[:, x * HALF : (x + 1) * HALF]
        imag = partly[:, (planes + x) * HALF : (planes + x + 1) * HALF]
        rows.append(jnp.concatenate([real, imag], axis=1))
    return along_lanes(jnp.concatenate(rows, axis=0), table_ref, 2, True)


def updated(rows_ref, support_ref, density_ref, table_ref):
    image = image_from(rows_ref, table_ref, N)
    support = support_ref[...].reshape(2 * N, N)
    density = density_ref[...].reshape(2 * N, N)
    return jnp.where(support == 1, image, density - BETA * image)


def first_kernel(density_ref, table_ref, out_ref, rows_ref):
    send_forward(density_ref[...].reshape(2 * N, N), table_ref, rows_ref)
    out_ref[...] = coded(rows_ref[...])


def middle_kernel(got_ref, support_ref, density_ref, table_ref, out_ref, rows_ref, code_ref, sem):
    rows_ref[...] = decoded(got_ref[...])
    field = updated(rows_ref, support_ref, density_ref, table_ref)
    send_forward(field, table_ref, rows_ref)
    for copy in send_out(rows_ref, code_ref, out_ref, sem):
        copy.wait()


def keep_kernel(group_ref, got_ref, support_ref, density_ref, table_ref, own_ref, code_ref, rows_ref, field_ref):
    group = group_ref[0]
    rows_ref[...] = decoded(got_ref[...])
    field_ref[...] = updated(rows_ref, support_ref, density_ref, table_ref).reshape(2, N, N)
    own_ref[...] = field_ref[:, pl.ds(pl.multiple_of(group * HALF, HALF), HALF), :]
    code_ref[...] = coded(field_ref[:, pl.ds(pl.multiple_of((1 - group) * HALF, HALF), HALF), :])


def last_kernel(group_ref, got_ref, support_ref, own_ref, other_ref, table_ref, field_ref, rows_ref):
    group = group_ref[0]
    rows_ref[...] = decoded(got_ref[...])
    image = image_from(rows_ref, table_ref, HALF).reshape(PLANES, HALF, N)
    other = decoded(other_ref[...])
    own = own_ref[...]
    for p in range(2):
        before = jnp.where(group == p, own, other)
        part = image[2 * p : 2 * p + 2]
        inside = support_ref[2 * p : 2 * p + 2] == 1
        field_ref[2 * p : 2 * p + 2] = jnp.where(inside, part, before - BETA * part)


PACKET = jax.ShapeDtypeStruct((DEVS, 8, 128), jnp.int16)
WIDE_PACKET = jax.ShapeDtypeStruct((DEVS, 16, 128), jnp.int16)


def scratch(rows):
    return pltpu.VMEM((DEVS, rows, 128), jnp.float32)


def first_field(density, t):
    return call(
        first_kernel, PACKET, in_specs=spec_vmem(2), out_specs=spec_vmem(1)[0], scratch_shapes=[scratch(8)]
    )(density, t["field"])


def middle_field(got, support, density, t):
    return call(
        middle_kernel,
        PACKET,
        in_specs=spec_vmem(4),
        out_specs=hbm(),
        scratch_shapes=[scratch(8), code_scratch(8), sems(BLOCKS)],
    )(got, support, density, t["field"])


def kept_field(group, got, support, density, t):
    shape = (2, HALF, N)
    return call(
        keep_kernel,
        (jax.ShapeDtypeStruct(shape, jnp.float32), jax.ShapeDtypeStruct(shape, jnp.int16)),
        in_specs=[smem()] + spec_vmem(4),
        out_specs=tuple(spec_vmem(2)),
        scratch_shapes=[scratch(8), pltpu.VMEM((2, N, N), jnp.float32)],
    )(group, got, support, density, t["field"])


def last_field(group, got, support, own, other, t):
    return call(
        last_kernel,
        jax.ShapeDtypeStruct((PLANES, HALF, N), jnp.float32),
        in_specs=[smem()] + spec_vmem(5),
        out_specs=spec_vmem(1)[0],
        scratch_shapes=[scratch(16)],
    )(group, got, support, own, other, t["field"])


def project(first, rows_ref, start, amplitude, nyquist, table_ref):
    lanes = []
    for c in range(2):
        for pm in range(2):
            parts = []
            for g in range(2):
                for x in range(2):
                    parts.append(rows_ref[g * SLABS : (g + 1) * SLABS, start + x * 4 + pm * 2 + c, :])
            lanes.append(jnp.concatenate(parts, axis=0))
    high, low = halves(jnp.concatenate(lanes, axis=1))
    right = jnp.concatenate([high, high, low], axis=0)
    by_cos = dot(jnp.concatenate(table_at(table_ref, 0), axis=1), right)
    by_sin = dot(jnp.concatenate(table_at(table_ref, 1), axis=1), right)
    real = by_cos[:, :N] + by_sin[:, N:]
    imag = by_cos[:, N:] - by_sin[:, :N]
    mirror_real = by_cos[:, :N] - by_sin[:, N:]
    mirror_imag = by_cos[:, N:] + by_sin[:, :N]

    def partner(mirror):
        return jnp.where(first == 1, mirror, jnp.concatenate([mirror[:, HALF:], mirror[:, :HALF]], axis=1))

    mirror_real = partner(mirror_real)
    mirror_imag = partner(mirror_imag)
    scale = amplitude * lax.rsqrt(real * real + imag * imag + SOFTEN)
    zero_real = 0.5 * (real + mirror_real)
    zero_imag = 0.5 * (imag - mirror_imag)
    top_real = 0.5 * (imag + mirror_imag)
    top_imag = 0.5 * (mirror_real - real)
    zero_scale = amplitude * lax.rsqrt(zero_real * zero_real + zero_imag * zero_imag + SOFTEN)
    top_scale = nyquist * lax.rsqrt(top_real * top_real + top_imag * top_imag + SOFTEN)
    packed = packed_lanes()
    new_real = jnp.where(packed, zero_scale * zero_real - top_scale * top_imag, scale * real)
    new_imag = jnp.where(packed, zero_scale * zero_imag + top_scale * top_real, scale * imag)
    return turn(table_ref, new_real, new_imag, 1)


def part_of(result, x, pm, c):
    lane = (c * 2 + pm) * HALF
    return result[x * SLABS : (x + 1) * SLABS, lane : lane + HALF]


def once_kernel(place_ref, got_ref, table_ref, out_ref, rows_ref, code_ref, sem):
    first = place_ref[0]
    rows_ref[...] = decoded(got_ref[...])
    amplitude, nyquist = amplitudes(first, rows_ref)
    result = project(first, rows_ref, 24, amplitude, nyquist, table_ref)
    for pm in range(2):
        for c in range(2):
            for g in range(2):
                for x in range(2):
                    rows_ref[g * SLABS : (g + 1) * SLABS, x * 4 + pm * 2 + c, :] = part_of(result, g * 2 + x, pm, c)
    for copy in send_out(rows_ref, code_ref, out_ref, sem):
        copy.wait()


def even_kernel(place_ref, got_ref, even_ref, rows_ref):
    rows_ref[...] = decoded(got_ref[:, :24, :])
    amplitude, nyquist = amplitudes(place_ref[0], rows_ref)
    even_ref[:N] = amplitude
    even_ref[N:] = nyquist


def again_kernel(
    place_ref, got_ref, even_ref, table_ref, out_hbm, rows_ref, code_ref, sem
):
    sign = place_ref[1]
    rows_ref[:, :8, :] = decoded(got_ref[...])
    result = project(place_ref[0], rows_ref, 0, even_ref[:N], even_ref[N:], table_ref)
    for pm in range(2):
        for c in range(2):
            for x in range(PLANES):
                rows_ref[:SLABS, x * 4 + pm * 2 + c, :] = part_of(result, x, pm, c)
    sent = []
    for block in range(2):
        slabs = pl.ds(block * 32, 32)
        others = pl.ds(SLABS + block * 32, 32)
        codes = coded(rows_ref[slabs]).astype(jnp.int32)
        code_ref[slabs] = codes.astype(jnp.int16)
        code_ref[others] = (sign * codes).astype(jnp.int16)
        sent.append(fetch(code_ref.at[slabs], out_hbm.at[slabs], sem.at[2 * block]))
        sent.append(fetch(code_ref.at[others], out_hbm.at[others], sem.at[2 * block + 1]))
    for copy in sent:
        copy.wait()


EVEN = jax.ShapeDtypeStruct((2 * N, N), jnp.float32)


def project_once(place, got, t):
    return call(
        once_kernel,
        PACKET,
        in_specs=[smem()] + spec_vmem(2),
        out_specs=hbm(),
        scratch_shapes=[scratch(32), code_scratch(8), sems(BLOCKS)],
    )(place, got, t["slab"])


def kept_amplitude(place, got):
    return call(
        even_kernel, EVEN, in_specs=[smem()] + spec_vmem(1), out_specs=spec_vmem(1)[0], scratch_shapes=[scratch(24)]
    )(place, got)


def project_again(place, got, even, t):
    return call(
        again_kernel,
        WIDE_PACKET,
        in_specs=[smem()] + spec_vmem(3),
        out_specs=hbm(),
        scratch_shapes=[scratch(16), code_scratch(16), sems(BLOCKS)],
    )(place, got, even, t["slab"])


def exchange(packet):
    return lax.all_to_all(packet, BOTH, split_axis=0, concat_axis=0, tiled=True)


def swap(array):
    return lax.ppermute(array, "grp", [(0, 1), (1, 0)])


def local(patterns, probabilities, source_row, target_row, support, density):
    t = tables()
    group = lax.axis_index("grp")
    slab = lax.axis_index("slab")
    device = group * SLABS + slab
    place = jnp.stack([(device == 0).astype(jnp.int32), 1 - 2 * (device & 1)])
    pad = ((0, 0), (0, 128 - CAP))
    target = target_row[0, 0]

    send = gather_rows(source_row[0, 0], jnp.swapaxes(probabilities, 1, 2), patterns[0])
    got = lax.all_to_all(send, "slab", split_axis=0, concat_axis=0, tiled=True)

    def whole(field, kind):
        other = swap(lax.dynamic_slice_in_dim(field, 2 * (1 - group), 2, 0).astype(kind)).astype(field.dtype)
        own = lax.dynamic_slice_in_dim(field, 2 * group, 2, 0)
        return jnp.concatenate([jnp.where(group == 0, own, other), jnp.where(group == 0, other, own)], axis=1)

    planes = whole(density, jnp.float16)
    packet = first_field(planes, t)
    sums = place_rows(got, target.reshape(SLABS // SOURCES, 1, TAKEN), jnp.pad(target, pad), packet)
    late, sums = lax.optimization_barrier((support, sums))
    got_sums = exchange(sums)
    inside = whole(late, jnp.int16)

    theirs = lax.dynamic_slice_in_dim(sums, (1 - group) * 8, 8, 1)
    other = swap(jnp.concatenate([theirs, sums[:, 16:24]], axis=1))
    intensity = intensity_of(group.reshape(1), sums, other)

    back = exchange(project_once(place, got_sums, t))
    back, even, inside = lax.optimization_barrier((back, kept_amplitude(place, got_sums), inside))
    got = exchange(middle_field(back, inside, planes, t))
    own, theirs = kept_field(group.reshape(1), back, inside, planes, t)
    got, own, other = lax.optimization_barrier((got, own, swap(theirs)))
    back = exchange(project_again(place, got, even, t))
    return (intensity, last_field(group.reshape(1), back, support, own, other, t))


def solution(mesh):
    return jax.shard_map(
        local,
        mesh=mesh,
        in_specs=(
            P("grp", "slab", None),
            P("grp", "slab", None),
            P("grp", "slab", None, None),
            P("grp", "slab", None, None),
            P("slab", "grp", None),
            P("slab", "grp", None),
        ),
        out_specs=(P("slab", "grp", None), P("slab", "grp", None)),
        check_vma=False,
    )
```

time: 156 us -> 150 us (0.962)
  starting transfers between devices: 36.8 us -> 47.6 us
  local copies, waits for them, and re-layouts: 8.4 us -> 2.72 us
  waiting for transfers between devices: 57.7 us -> 53.8 us
  Pallas kernels: 45.9 us -> 42 us
  other arithmetic: 5.13 us -> 2.08 us
    all_to_all x1, waiting for transfers between devices: 15.6 us -> 0.01 us  [local(): got = lax.all_to_all(send, 'slab', split_axis=0, concat_axis=0, tiled=True)]
    ppermute x3 -> x4, waiting for transfers between devices: 3.97 us -> 19.5 us  [swap(): return lax.ppermute(array, 'grp', [(0, 1), (1, 0)])]
    all_to_all x4, starting transfers between devices: 17.8 us -> 27.8 us  [exchange(): return lax.all_to_all(packet, BOTH, split_axis=0, concat_axis=0, tiled=True)]
    unnamed x33 -> x20, local copies, waits for them, and re-layouts: 6.59 us -> 1.54 us
    all_to_all x4, waiting for transfers between devices: 38.1 us -> 34.3 us  [exchange(): return lax.all_to_all(packet, BOTH, split_axis=0, concat_axis=0, tiled=True)]
    pallas_call x1, Pallas kernels: 11.3 us -> 9.4 us  [gather_rows(): call(gather_kernel, jax.ShapeDtypeStruct((SLABS, SEND, 128), jnp.bfloat16...]
    pallas_call x1, Pallas kernels: 7.99 us -> 6.09 us  [place_rows(): call(place_kernel, jax.ShapeDtypeStruct((DEVS, 32, 128), jnp.int16), mib=...]
    all_to_all x1, starting transfers between devices: 9.5 us -> 11.2 us  [local(): got = lax.all_to_all(send, 'slab', split_axis=0, concat_axis=0, tiled=True)]
  transfers between devices with their start and end apart: 8 -> 9, of which waited for: 6 -> 6; matrix products, arithmetic and copies ran while one was open for 4% -> 2% of each run, Pallas kernels for 15% -> 14%
where the time goes in v3:
time: 150 us; the launch traced here: 149 us
  waiting for transfers between devices  53.8 us (36%)
  starting transfers between devices  47.6 us (32%)
  Pallas kernels  42 us (28%)
  local copies, waits for them, and re-layouts  2.72 us (2%)
  other arithmetic  2.08 us (1%)
    all_to_all x4, waiting for transfers between devices, exchange(): return lax.all_to_all(packet, BOTH, split_axis=0, concat_axis=0, tiled=True)  34.3 us
    all_to_all x4, starting transfers between devices, exchange(): return lax.all_to_all(packet, BOTH, split_axis=0, concat_axis=0, tiled=True)  27.8 us
    ppermute x4, waiting for transfers between devices, swap(): return lax.ppermute(array, 'grp', [(0, 1), (1, 0)])  19.5 us
    all_to_all x1, starting transfers between devices, local(): got = lax.all_to_all(send, 'slab', split_axis=0, concat_axis=0, tiled=True)  11.2 us
    pallas_call x1, Pallas kernels, gather_rows(): call(gather_kernel, jax.ShapeDtypeStruct((SLABS, SEND, 128), jnp.bfloat16...  9.4 us
    ppermute x4, starting transfers between devices, swap(): return lax.ppermute(array, 'grp', [(0, 1), (1, 0)])  8.65 us
    pallas_call x1, Pallas kernels, place_rows(): call(place_kernel, jax.ShapeDtypeStruct((DEVS, 32, 128), jnp.int16), mib=...  6.09 us
    pallas_call x1, Pallas kernels, project_once(): call(once_kernel, PACKET, in_specs=[smem()] + spec_vmem(2), out_specs=hbm...  5.8 us
  transfers between devices with their start and end apart: 9, of which 6 were waited for; matrix products, arithmetic and copies ran while one was open for 2% of the time, Pallas kernels for 14%

profile of v3, /device:TPU:1, one launch (start us, length us, event | category | flops | bytes accessed | tf_op | source)
XLA Modules:
  0.0 149.2 jit_solution(3663344137100984328)
XLA Ops:
  0.6 9.4 %shard_map.95 = bf16[64,88,128]{2,1,0:T(8,128)(2,1)} custom-call(s32[64,80]{1,0:T(8,128)} %bitcast.10, s32[64,80]{1,0:T(8,128)} %bitcast.11, bf16[1,32,256]{2,1,0:T(8,128)(2,1)} %bitcast.13, bf16[256,16384]{1,0:T(8,128)(2,1)} %bitcast.9), custom_call_target="tpu_custom_call" | custom-call | flops 268435456 | bytes 33554432 | tf_op jit(solution)/shard_map/pallas_call | solution.py:218
  10.1 11.2 %all-to-all-start = ((bf16[64,88,128]{2,1,0:T(8,128)(2,1)}), bf16[64,88,128]{2,1,0:T(8,128)(2,1)}, u32[]{:S(2)}, u32[]{:S(2)}) async-start(bf16[64,88,128]{2,1,0:T(8,128)(2,1)} %shard_map.95), calls=%async_computation | async-start | bytes 2883584 | tf_op jit(solution)/shard_map/all_to_all | solution.py:621
  21.4 2.5 %collective-permute-start = (f16[2,128,256]{2,1,0:T(8,128)(2,1)S(1)}, f16[2,128,256]{2,1,0:T(8,128)(2,1)S(1)}, u32[]{:S(2)}, u32[]{:S(2)}) collective-permute-start(f16[2,128,256]{2,1,0:T(8,128)(2,1)S(1)} %dynamic-slice_convert_fusion.1), channel_id=1, source_target_pairs={{0,64},{64,0},{1,65},{65,1},{2,66},{66,2},{3,67},{67,3},{4,68},{68... | collective-permute-start | bytes 393224 | tf_op jit(solution)/shard_map/ppermute | solution.py:608
  23.9 0.1 reshape_squeeze.3.row_ref
  24.0 18.6 %collective-permute-done = f16[2,128,256]{2,1,0:T(8,128)(2,1)S(1)} collective-permute-done((f16[2,128,256]{2,1,0:T(8,128)(2,1)S(1)}, f16[2,128,256]{2,1,0:T(8,128)(2,1)S(1)}, u32[]{:S(2)}, u32[]{:S(2)}) %collective-permute-start) | collective-permute-done | bytes 131104 | tf_op jit(solution)/shard_map/ppermute | solution.py:608
  42.7 1.4 shard_map.96.packet_ref
  44.1 6.1 %shard_map.97.own_ref = s16[128,32,128]{2,1,0:T(8,128)(2,1)} custom-call(bf16[64,88,128]{2,1,0:T(8,128)(2,1)} %all-to-all-done.got_ref, s32[4,1,1280]{2,1,0:T(1,128)S(1)} %reshape_squeeze.3.row_ref, s32[64,128]{1,0:T(8,128)S(1)} %pad.4.column_ref, s16[128,8,128]{2,1,0:T(8,128)(2,1)S(1)} %shard_map.96.packet_ref), custom_call_target="tpu_custom_call" | custom-call | tf_op jit(solution)/shard_map/pallas_call | solution.py:290
  50.3 8.2 %all-to-all-start.1 = ((s16[128,32,128]{2,1,0:T(8,128)(2,1)}), s16[128,32,128]{2,1,0:T(8,128)(2,1)S(1)}, u32[]{:S(2)}, u32[]{:S(2)}) async-start(s16[128,32,128]{2,1,0:T(8,128)(2,1)} %shard_map.97.own_ref), calls=%async_computation.1 | async-start | bytes 2097152 | tf_op jit(solution)/shard_map/all_to_all | solution.py:604
  58.5 3.0 %collective-permute-start.2 = (s16[2,128,256]{2,1,0:T(8,128)(2,1)S(1)}, s16[2,128,256]{2,1,0:T(8,128)(2,1)}, u32[]{:S(2)}, u32[]{:S(2)}) collective-permute-start(s16[2,128,256]{2,1,0:T(8,128)(2,1)S(1)} %dynamic-slice_convert_fusion), channel_id=1, source_target_pairs={{0,64},{64,0},{1,65},{65,1},{2,66},{66,2},{3,67},{67,3},{4,68},{68... | collective-permute-start | bytes 393224 | tf_op jit(solution)/shard_map/ppermute | solution.py:608
  61.5 0.1 pad_add_fusion.2.place_ref
  61.5 16.0 %all-to-all-done.1.got_ref = s16[128,32,128]{2,1,0:T(8,128)(2,1)S(1)} async-done(((s16[128,32,128]{2,1,0:T(8,128)(2,1)}), s16[128,32,128]{2,1,0:T(8,128)(2,1)S(1)}, u32[]{:S(2)}, u32[]{:S(2)}) %all-to-all-start.1) | async-done | bytes 1048608 | tf_op jit(solution)/shard_map/all_to_all | solution.py:604
  77.5 5.8 %shard_map.99 = s16[128,8,128]{2,1,0:T(8,128)(2,1)S(1)} custom-call(s32[2]{0:T(128)S(1)} %pad_add_fusion.2.place_ref, s16[128,32,128]{2,1,0:T(8,128)(2,1)S(1)} %all-to-all-done.1.got_ref, bf16[1024,256]{1,0:T(8,128)(2,1)S(1)} %copy-done.5), custom_call_target="tpu_custom_call" | custom-call | tf_op jit(solution)/shard_map/pallas_call | solution.py:578
  83.3 0.7 copy-done.7
  84.0 7.2 %all-to-all-start.2 = ((s16[128,8,128]{2,1,0:T(8,128)(2,1)}), s16[128,8,128]{2,1,0:T(8,128)(2,1)S(1)}, u32[]{:S(2)}, u32[]{:S(2)}) async-start(s16[128,8,128]{2,1,0:T(8,128)(2,1)} %copy-done.7), calls=%async_computation.2 | async-start | bytes 524288 | tf_op jit(solution)/shard_map/all_to_all | solution.py:604
  91.2 1.0 convert_select_fusion.1
  92.2 3.2 %shard_map.100.even_ref = f32[512,256]{1,0:T(8,128)S(1)} custom-call(s32[2]{0:T(128)S(1)} %pad_add_fusion.2.place_ref, s16[128,32,128]{2,1,0:T(8,128)(2,1)S(1)} %all-to-all-done.1.got_ref), custom_call_target="tpu_custom_call" | custom-call | tf_op jit(solution)/shard_map/pallas_call | solution.py:588
  95.5 0.8 copy-done.1
  96.3 5.9 %all-to-all-done.2.got_ref = s16[128,8,128]{2,1,0:T(8,128)(2,1)S(1)} async-done(((s16[128,8,128]{2,1,0:T(8,128)(2,1)}), s16[128,8,128]{2,1,0:T(8,128)(2,1)S(1)}, u32[]{:S(2)}, u32[]{:S(2)}) %all-to-all-start.2) | async-done | bytes 262176 | tf_op jit(solution)/shard_map/all_to_all | solution.py:604
  102.2 3.6 %shard_map.101 = s16[128,8,128]{2,1,0:T(8,128)(2,1)} custom-call(s16[128,8,128]{2,1,0:T(8,128)(2,1)S(1)} %all-to-all-done.2.got_ref, s32[2,256,256]{2,1,0:T(8,128)S(1)} %pad_add_fusion.1.support_ref, f32[2,256,256]{2,1,0:T(8,128)S(1)} %pad_maximum_fusion.density_ref, bf16[1536,256]{1,0:T(8,128)(2,1)S(1)} %copy-done), custom_call_target="tpu_custom_call" | custom-call | tf_op jit(solution)/shard_map/pallas_call | solution.py:459
  105.8 4.5 %all-to-all-start.3 = ((s16[128,8,128]{2,1,0:T(8,128)(2,1)}), s16[128,8,128]{2,1,0:T(8,128)(2,1)S(1)}, u32[]{:S(2)}, u32[]{:S(2)}) async-start(s16[128,8,128]{2,1,0:T(8,128)(2,1)} %shard_map.101), calls=%async_computation.3 | async-start | bytes 524288 | tf_op jit(solution)/shard_map/all_to_all | solution.py:604
  110.3 1.6 %shard_map.102 = (f32[2,128,256]{2,1,0:T(8,128)S(1)}, s16[2,128,256]{2,1,0:T(8,128)(2,1)S(1)}) custom-call(s32[1]{0:T(128)} %bitcast.group_ref, s16[128,8,128]{2,1,0:T(8,128)(2,1)S(1)} %all-to-all-done.2.got_ref, s32[2,256,256]{2,1,0:T(8,128)S(1)} %pad_add_fusion.1.support_ref, f32[2,256,256]{2,1,0:T(8,128)S(1)} %pad_maximum_fusion.density_ref, ...), custom_call_target="tpu_custom_call" | custom-call | tf_op jit(solution)/shard_map/pallas_call | solution.py:470
  112.0 3.0 %collective-permute-start.3 = (s16[2,128,256]{2,1,0:T(8,128)(2,1)S(1)}, s16[2,128,256]{2,1,0:T(8,128)(2,1)S(1)}, u32[]{:S(2)}, u32[]{:S(2)}) collective-permute-start(s16[2,128,256]{2,1,0:T(8,128)(2,1)S(1)} %get-tuple-element.17), channel_id=1, source_target_pairs={{0,64},{64,0},{1,65},{65,1},{2,66},{66,2},{3,67},{67,3},{4,68},{68... | collective-permute-start | bytes 393224 | tf_op jit(solution)/shard_map/ppermute | solution.py:608
  114.9 1.1 constant_dynamic-slice_fusion
  116.0 0.9 pad_add_fusion
  116.9 0.2 collective-permute-start.1
  117.1 0.9 collective-permute-done.3.other_ref
  118.0 3.3 %all-to-all-done.3.got_ref = s16[128,8,128]{2,1,0:T(8,128)(2,1)S(1)} async-done(((s16[128,8,128]{2,1,0:T(8,128)(2,1)}), s16[128,8,128]{2,1,0:T(8,128)(2,1)S(1)}, u32[]{:S(2)}, u32[]{:S(2)}) %all-to-all-start.3) | async-done | bytes 262176 | tf_op jit(solution)/shard_map/all_to_all | solution.py:604
  121.3 3.8 %shard_map.103 = s16[128,16,128]{2,1,0:T(8,128)(2,1)} custom-call(s32[2]{0:T(128)S(1)} %pad_add_fusion.2.place_ref, s16[128,8,128]{2,1,0:T(8,128)(2,1)S(1)} %all-to-all-done.3.got_ref, f32[512,256]{1,0:T(8,128)S(1)} %copy-done.2, bf16[1024,256]{1,0:T(8,128)(2,1)S(1)} %copy-done.6), custom_call_target="tpu_custom_call" | custom-call | tf_op jit(solution)/shard_map/pallas_call | solution.py:594
  125.1 7.9 %all-to-all-start.4 = ((s16[128,16,128]{2,1,0:T(8,128)(2,1)}), s16[128,16,128]{2,1,0:T(8,128)(2,1)S(1)}, u32[]{:S(2)}, u32[]{:S(2)}) async-start(s16[128,16,128]{2,1,0:T(8,128)(2,1)} %shard_map.103), calls=%async_computation.4 | async-start | bytes 1048576 | tf_op jit(solution)/shard_map/all_to_all | solution.py:604
  133.0 4.3 %shard_map.98 = f32[4,128,256]{2,1,0:T(8,128)} custom-call(s32[1]{0:T(128)} %bitcast.group_ref, s16[128,32,128]{2,1,0:T(8,128)(2,1)} %shard_map.97.own_ref, s16[128,16,128]{2,1,0:T(8,128)(2,1)S(1)} %collective-permute-done.1.other_ref), custom_call_target="tpu_custom_call" | custom-call | tf_op jit(solution)/shard_map/pallas_call | solution.py:322
  137.3 9.1 %all-to-all-done.4.got_ref = s16[128,16,128]{2,1,0:T(8,128)(2,1)S(1)} async-done(((s16[128,16,128]{2,1,0:T(8,128)(2,1)}), s16[128,16,128]{2,1,0:T(8,128)(2,1)S(1)}, u32[]{:S(2)}, u32[]{:S(2)}) %all-to-all-start.4) | async-done | bytes 524320 | tf_op jit(solution)/shard_map/all_to_all | solution.py:604
  146.4 2.7 %shard_map.104 = f32[4,128,256]{2,1,0:T(8,128)} custom-call(s32[1]{0:T(128)} %bitcast.group_ref, s16[128,16,128]{2,1,0:T(8,128)(2,1)S(1)} %all-to-all-done.4.got_ref, s32[4,128,256]{2,1,0:T(8,128)S(1)} %copy-done.4, f32[2,128,256]{2,1,0:T(8,128)S(1)} %get-tuple-element.20.own_ref, s16[2,128,256]{2,1,0:T(8,128)(2,1)S(1)} %collective-permute-done.3.other_ref, ...), custom_call_target="tpu_custom_call" | custom-call | tf_op jit(solution)/shard_map/pallas_call | solution.py:480
  (27 shorter events, 0.2 us)
Async XLA Ops:
  10.0 11.3 %copy-start.8 = (f32[4,128,256]{2,1,0:T(8,128)S(1)}, f32[4,128,256]{2,1,0:T(8,128)}, u32[]{:S(2)}) copy-start(f32[4,128,256]{2,1,0:T(8,128)} %param.13) | copy-start | bytes 1572868
  10.1 13.9 %copy-start.9 = (s32[1,1,64,80]{3,2,1,0:T(8,128)S(1)}, s32[1,1,64,80]{3,2,1,0:T(8,128)}, u32[]{:S(2)}) copy-start(s32[1,1,64,80]{3,2,1,0:T(8,128)} %param.11) | copy-start | bytes 61444
  10.1 34.1 %all-to-all-start = ((bf16[64,88,128]{2,1,0:T(8,128)(2,1)}), bf16[64,88,128]{2,1,0:T(8,128)(2,1)}, u32[]{:S(2)}, u32[]{:S(2)}) async-start(bf16[64,88,128]{2,1,0:T(8,128)(2,1)} %shard_map.95), calls=%async_computation | async-start | bytes 2883584 | tf_op jit(solution)/shard_map/all_to_all | solution.py:621
  21.3 21.4 %copy-start = (bf16[1536,256]{1,0:T(8,128)(2,1)S(1)}, bf16[1536,256]{1,0:T(8,128)(2,1)}, u32[]{:S(2)}) copy-start(bf16[1536,256]{1,0:T(8,128)(2,1)} %constant.27.clone.table_ref) | copy-start | bytes 2359300
  21.4 21.2 %collective-permute-start = (f16[2,128,256]{2,1,0:T(8,128)(2,1)S(1)}, f16[2,128,256]{2,1,0:T(8,128)(2,1)S(1)}, u32[]{:S(2)}, u32[]{:S(2)}) collective-permute-start(f16[2,128,256]{2,1,0:T(8,128)(2,1)S(1)} %dynamic-slice_convert_fusion.1), channel_id=1, source_target_pairs={{0,64},{64,0},{1,65},{65,1},{2,66},{66,2},{3,67},{67,3},{4,68},{68... | collective-permute-start | bytes 393224 | tf_op jit(solution)/shard_map/ppermute | solution.py:608
  50.2 8.2 %copy-start.3 = (s32[4,128,256]{2,1,0:T(8,128)S(1)}, s32[4,128,256]{2,1,0:T(8,128)}, u32[]{:S(2)}) copy-start(s32[4,128,256]{2,1,0:T(8,128)} %support_ref.1) | copy-start | bytes 1572868
  50.3 27.3 %copy-start.5 = (bf16[1024,256]{1,0:T(8,128)(2,1)S(1)}, bf16[1024,256]{1,0:T(8,128)(2,1)}, u32[]{:S(2)}) copy-start(bf16[1024,256]{1,0:T(8,128)(2,1)} %constant.28.clone.table_ref) | copy-start | bytes 1572868
  50.3 27.2 %all-to-all-start.1 = ((s16[128,32,128]{2,1,0:T(8,128)(2,1)}), s16[128,32,128]{2,1,0:T(8,128)(2,1)S(1)}, u32[]{:S(2)}, u32[]{:S(2)}) async-start(s16[128,32,128]{2,1,0:T(8,128)(2,1)} %shard_map.97.own_ref), calls=%async_computation.1 | async-start | bytes 2097152 | tf_op jit(solution)/shard_map/all_to_all | solution.py:604
  58.5 32.7 %collective-permute-start.2 = (s16[2,128,256]{2,1,0:T(8,128)(2,1)S(1)}, s16[2,128,256]{2,1,0:T(8,128)(2,1)}, u32[]{:S(2)}, u32[]{:S(2)}) collective-permute-start(s16[2,128,256]{2,1,0:T(8,128)(2,1)S(1)} %dynamic-slice_convert_fusion), channel_id=1, source_target_pairs={{0,64},{64,0},{1,65},{65,1},{2,66},{66,2},{3,67},{67,3},{4,68},{68... | collective-permute-start | bytes 393224 | tf_op jit(solution)/shard_map/ppermute | solution.py:608
  83.3 0.7 copy-start.7
  84.0 18.2 %all-to-all-start.2 = ((s16[128,8,128]{2,1,0:T(8,128)(2,1)}), s16[128,8,128]{2,1,0:T(8,128)(2,1)S(1)}, u32[]{:S(2)}, u32[]{:S(2)}) async-start(s16[128,8,128]{2,1,0:T(8,128)(2,1)} %copy-done.7), calls=%async_computation.2 | async-start | bytes 524288 | tf_op jit(solution)/shard_map/all_to_all | solution.py:604
  95.5 0.8 copy-start.1
  105.8 15.4 %all-to-all-start.3 = ((s16[128,8,128]{2,1,0:T(8,128)(2,1)}), s16[128,8,128]{2,1,0:T(8,128)(2,1)S(1)}, u32[]{:S(2)}, u32[]{:S(2)}) async-start(s16[128,8,128]{2,1,0:T(8,128)(2,1)} %shard_map.101), calls=%async_computation.3 | async-start | bytes 524288 | tf_op jit(solution)/shard_map/all_to_all | solution.py:604
  111.9 9.3 %copy-start.2 = (f32[512,256]{1,0:T(8,128)S(1)}, f32[512,256]{1,0:T(8,128)}, u32[]{:S(2)}) copy-start(f32[512,256]{1,0:T(8,128)} %copy-done.1) | copy-start | bytes 1572868
  111.9 9.3 %copy-start.6 = (bf16[1024,256]{1,0:T(8,128)(2,1)S(1)}, bf16[1024,256]{1,0:T(8,128)(2,1)}, u32[]{:S(2)}) copy-start(bf16[1024,256]{1,0:T(8,128)(2,1)} %constant.28.clone.table_ref) | copy-start | bytes 1572868
  112.0 6.0 %collective-permute-start.3 = (s16[2,128,256]{2,1,0:T(8,128)(2,1)S(1)}, s16[2,128,256]{2,1,0:T(8,128)(2,1)S(1)}, u32[]{:S(2)}, u32[]{:S(2)}) collective-permute-start(s16[2,128,256]{2,1,0:T(8,128)(2,1)S(1)} %get-tuple-element.17), channel_id=1, source_target_pairs={{0,64},{64,0},{1,65},{65,1},{2,66},{66,2},{3,67},{67,3},{4,68},{68... | collective-permute-start | bytes 393224 | tf_op jit(solution)/shard_map/ppermute | solution.py:608
  116.9 16.1 %collective-permute-start.1 = (s16[128,16,128]{2,1,0:T(8,128)(2,1)}, s16[128,16,128]{2,1,0:T(8,128)(2,1)S(1)}, u32[]{:S(2)}, u32[]{:S(2)}) collective-permute-start(s16[128,16,128]{2,1,0:T(8,128)(2,1)} %pad_add_fusion), channel_id=1, source_target_pairs={{0,64},{64,0},{1,65},{65,1},{2,66},{66,2},{3,67},{67,3},{4,68},{68... | collective-permute-start | bytes 1572872 | tf_op jit(solution)/shard_map/ppermute | solution.py:608
  125.1 21.4 %copy-start.4 = (s32[4,128,256]{2,1,0:T(8,128)S(1)}, s32[4,128,256]{2,1,0:T(8,128)}, u32[]{:S(2)}) copy-start(s32[4,128,256]{2,1,0:T(8,128)} %support_ref.1) | copy-start | bytes 1572868
  125.1 21.4 %all-to-all-start.4 = ((s16[128,16,128]{2,1,0:T(8,128)(2,1)}), s16[128,16,128]{2,1,0:T(8,128)(2,1)S(1)}, u32[]{:S(2)}, u32[]{:S(2)}) async-start(s16[128,16,128]{2,1,0:T(8,128)(2,1)} %shard_map.103), calls=%async_computation.4 | async-start | bytes 1048576 | tf_op jit(solution)/shard_map/all_to_all | solution.py:604

commit v4 on v3

--- a/solution.py
+++ b/solution.py
@@ -617,32 +617,34 @@
     pad = ((0, 0), (0, 128 - CAP))
     target = target_row[0, 0]
 
+    def planes_of(first):
+        return [lax.dynamic_slice_in_dim(field, first, 2, 0) for field in (density, support)]
+
+    theirs = jnp.stack([field.astype(jnp.float16) for field in planes_of(2 * (1 - group))])
+    other = swap(theirs)
     send = gather_rows(source_row[0, 0], jnp.swapaxes(probabilities, 1, 2), patterns[0])
+    send, other = lax.optimization_barrier((send, other))
     got = lax.all_to_all(send, "slab", split_axis=0, concat_axis=0, tiled=True)
 
-    def whole(field, kind):
-        other = swap(lax.dynamic_slice_in_dim(field, 2 * (1 - group), 2, 0).astype(kind)).astype(field.dtype)
-        own = lax.dynamic_slice_in_dim(field, 2 * group, 2, 0)
+    def whole(own, other):
+        other = other.astype(own.dtype)
         return jnp.concatenate([jnp.where(group == 0, own, other), jnp.where(group == 0, other, own)], axis=1)
 
-    planes = whole(density, jnp.float16)
+    planes, inside = [whole(own, other[i]) for i, own in enumerate(planes_of(2 * group))]
     packet = first_field(planes, t)
     sums = place_rows(got, target.reshape(SLABS // SOURCES, 1, TAKEN), jnp.pad(target, pad), packet)
-    late, sums = lax.optimization_barrier((support, sums))
     got_sums = exchange(sums)
-    inside = whole(late, jnp.int16)
 
     theirs = lax.dynamic_slice_in_dim(sums, (1 - group) * 8, 8, 1)
     other = swap(jnp.concatenate([theirs, sums[:, 16:24]], axis=1))
     intensity = intensity_of(group.reshape(1), sums, other)
 
     back = exchange(project_once(place, got_sums, t))
-    back, even, inside = lax.optimization_barrier((back, kept_amplitude(place, got_sums), inside))
+    back, even = lax.optimization_barrier((back, kept_amplitude(place, got_sums)))
     got = exchange(middle_field(back, inside, planes, t))
     own, theirs = kept_field(group.reshape(1), back, inside, planes, t)
-    got, own, other = lax.optimization_barrier((got, own, swap(theirs)))
     back = exchange(project_again(place, got, even, t))
-    return (intensity, last_field(group.reshape(1), back, support, own, other, t))
+    return (intensity, last_field(group.reshape(1), back, support, own, swap(theirs), t))
 
 
 def solution(mesh):

time: 150 us -> 144 us (0.960)
  starting transfers between devices: 47.6 us -> 37.2 us
  other arithmetic: 2.08 us -> 4.05 us
  waiting for transfers between devices: 53.8 us -> 55.5 us
    all_to_all x1, waiting for transfers between devices: 0.01 us -> 19.8 us  [local(): got = lax.all_to_all(send, 'slab', split_axis=0, concat_axis=0, tiled=True)]
    ppermute x4 -> x3, waiting for transfers between devices: 19.5 us -> 2.38 us  [swap(): return lax.ppermute(array, 'grp', [(0, 1), (1, 0)])]
    all_to_all x4, starting transfers between devices: 27.8 us -> 17.9 us  [exchange(): return lax.all_to_all(packet, BOTH, split_axis=0, concat_axis=0, tiled=True)]
    another operation x0 -> x3, other arithmetic: none -> 2.02 us  [local(): jnp.stack([field.astype(jnp.float16) for field in planes_of(2 * (1 - grou...]
    ppermute x4 -> x3, starting transfers between devices: 8.65 us -> 9.51 us  [swap(): return lax.ppermute(array, 'grp', [(0, 1), (1, 0)])]
  transfers between devices with their start and end apart: 9 -> 8, of which waited for: 6 -> 6; matrix products, arithmetic and copies ran while one was open for 2% -> 2% of each run, Pallas kernels for 14% -> 17%
where the time goes in v4:
time: 144 us; the launch traced here: 143 us
  waiting for transfers between devices  55.5 us (39%)
  Pallas kernels  42.2 us (29%)
  starting transfers between devices  37.2 us (26%)
  other arithmetic  4.05 us (3%)
  local copies, waits for them, and re-layouts  3.6 us (2%)
    all_to_all x4, waiting for transfers between devices, exchange(): return lax.all_to_all(packet, BOTH, split_axis=0, concat_axis=0, tiled=True)  33.2 us
    all_to_all x1, waiting for transfers between devices, local(): got = lax.all_to_all(send, 'slab', split_axis=0, concat_axis=0, tiled=True)  19.8 us
    all_to_all x4, starting transfers between devices, exchange(): return lax.all_to_all(packet, BOTH, split_axis=0, concat_axis=0, tiled=True)  17.9 us
    all_to_all x1, starting transfers between devices, local(): got = lax.all_to_all(send, 'slab', split_axis=0, concat_axis=0, tiled=True)  9.78 us
    ppermute x3, starting transfers between devices, swap(): return lax.ppermute(array, 'grp', [(0, 1), (1, 0)])  9.51 us
    pallas_call x1, Pallas kernels, gather_rows(): call(gather_kernel, jax.ShapeDtypeStruct((SLABS, SEND, 128), jnp.bfloat16...  9.4 us
    pallas_call x1, Pallas kernels, place_rows(): call(place_kernel, jax.ShapeDtypeStruct((DEVS, 32, 128), jnp.int16), mib=...  6.09 us
    pallas_call x1, Pallas kernels, project_once(): call(once_kernel, PACKET, in_specs=[smem()] + spec_vmem(2), out_specs=hbm...  5.79 us
  transfers between devices with their start and end apart: 8, of which 6 were waited for; matrix products, arithmetic and copies ran while one was open for 2% of the time, Pallas kernels for 17%

profile of v4, /device:TPU:1, one launch (start us, length us, event | category | flops | bytes accessed | tf_op | source)
XLA Modules:
  0.0 143.5 jit_solution(8251287920510750669)
XLA Ops:
  0.6 1.0 fusion.1
  1.6 1.0 fusion
  2.7 3.7 %collective-permute-start = (f16[2,2,128,256]{3,2,1,0:T(8,128)(2,1)S(1)}, f16[2,2,128,256]{3,2,1,0:T(8,128)(2,1)S(1)}, u32[]{:S(2)}, u32[]{:S(2)}) collective-permute-start(f16[2,2,128,256]{3,2,1,0:T(8,128)(2,1)S(1)} %pad_maximum_fusion.1), channel_id=1, source_target_pairs={{0,64},{64,0},{1,65},{65,1},{2,66},{66,2},{3,67},{67,3},{4,68},{68... | collective-permute-start | bytes 786440 | tf_op jit(solution)/shard_map/ppermute | solution.py:608
  6.3 9.4 %shard_map.95 = bf16[64,88,128]{2,1,0:T(8,128)(2,1)} custom-call(s32[64,80]{1,0:T(8,128)} %bitcast.22, s32[64,80]{1,0:T(8,128)} %bitcast.23, bf16[1,32,256]{2,1,0:T(8,128)(2,1)} %bitcast.25, bf16[256,16384]{1,0:T(8,128)(2,1)} %bitcast.21), custom_call_target="tpu_custom_call" | custom-call | flops 268435456 | bytes 33554432 | tf_op jit(solution)/shard_map/pallas_call | solution.py:218
  15.8 9.8 %all-to-all-start = ((bf16[64,88,128]{2,1,0:T(8,128)(2,1)}), bf16[64,88,128]{2,1,0:T(8,128)(2,1)}, u32[]{:S(2)}, u32[]{:S(2)}) async-start(bf16[64,88,128]{2,1,0:T(8,128)(2,1)} %shard_map.95), calls=%async_computation | async-start | bytes 2883584 | tf_op jit(solution)/shard_map/all_to_all | solution.py:627
  25.8 0.9 copy-done
  26.7 1.4 shard_map.96.packet_ref
  28.1 19.8 %all-to-all-done.got_ref = bf16[64,88,128]{2,1,0:T(8,128)(2,1)} async-done(((bf16[64,88,128]{2,1,0:T(8,128)(2,1)}), bf16[64,88,128]{2,1,0:T(8,128)(2,1)}, u32[]{:S(2)}, u32[]{:S(2)}) %all-to-all-start) | async-done | bytes 1441824 | tf_op jit(solution)/shard_map/all_to_all | solution.py:627
  48.0 6.1 %shard_map.97.own_ref = s16[128,32,128]{2,1,0:T(8,128)(2,1)} custom-call(bf16[64,88,128]{2,1,0:T(8,128)(2,1)} %all-to-all-done.got_ref, s32[4,1,1280]{2,1,0:T(1,128)S(1)} %reshape_squeeze.3.row_ref, s32[64,128]{1,0:T(8,128)S(1)} %pad.4.column_ref, s16[128,8,128]{2,1,0:T(8,128)(2,1)S(1)} %shard_map.96.packet_ref), custom_call_target="tpu_custom_call" | custom-call | tf_op jit(solution)/shard_map/pallas_call | solution.py:290
  54.1 4.3 %all-to-all-start.1 = ((s16[128,32,128]{2,1,0:T(8,128)(2,1)}), s16[128,32,128]{2,1,0:T(8,128)(2,1)S(1)}, u32[]{:S(2)}, u32[]{:S(2)}) async-start(s16[128,32,128]{2,1,0:T(8,128)(2,1)} %shard_map.97.own_ref), calls=%async_computation.1 | async-start | bytes 2097152 | tf_op jit(solution)/shard_map/all_to_all | solution.py:604
  58.5 19.1 %all-to-all-done.1.got_ref = s16[128,32,128]{2,1,0:T(8,128)(2,1)S(1)} async-done(((s16[128,32,128]{2,1,0:T(8,128)(2,1)}), s16[128,32,128]{2,1,0:T(8,128)(2,1)S(1)}, u32[]{:S(2)}, u32[]{:S(2)}) %all-to-all-start.1) | async-done | bytes 1048608 | tf_op jit(solution)/shard_map/all_to_all | solution.py:604
  77.6 5.8 %shard_map.99 = s16[128,8,128]{2,1,0:T(8,128)(2,1)S(1)} custom-call(s32[2]{0:T(128)S(1)} %pad_add_fusion.2.place_ref, s16[128,32,128]{2,1,0:T(8,128)(2,1)S(1)} %all-to-all-done.1.got_ref, bf16[1024,256]{1,0:T(8,128)(2,1)S(1)} %copy-done.5), custom_call_target="tpu_custom_call" | custom-call | tf_op jit(solution)/shard_map/pallas_call | solution.py:578
  83.4 0.7 copy-done.7
  84.1 4.7 %all-to-all-start.2 = ((s16[128,8,128]{2,1,0:T(8,128)(2,1)}), s16[128,8,128]{2,1,0:T(8,128)(2,1)S(1)}, u32[]{:S(2)}, u32[]{:S(2)}) async-start(s16[128,8,128]{2,1,0:T(8,128)(2,1)} %copy-done.7), calls=%async_computation.2 | async-start | bytes 524288 | tf_op jit(solution)/shard_map/all_to_all | solution.py:604
  88.8 1.0 convert_select_fusion.1
  89.8 3.2 %shard_map.100.even_ref = f32[512,256]{1,0:T(8,128)S(1)} custom-call(s32[2]{0:T(128)S(1)} %pad_add_fusion.2.place_ref, s16[128,32,128]{2,1,0:T(8,128)(2,1)S(1)} %all-to-all-done.1.got_ref), custom_call_target="tpu_custom_call" | custom-call | tf_op jit(solution)/shard_map/pallas_call | solution.py:588
  93.1 0.8 copy-done.1
  93.9 6.0 %all-to-all-done.2.got_ref = s16[128,8,128]{2,1,0:T(8,128)(2,1)S(1)} async-done(((s16[128,8,128]{2,1,0:T(8,128)(2,1)}), s16[128,8,128]{2,1,0:T(8,128)(2,1)S(1)}, u32[]{:S(2)}, u32[]{:S(2)}) %all-to-all-start.2) | async-done | bytes 262176 | tf_op jit(solution)/shard_map/all_to_all | solution.py:604
  99.9 3.6 %shard_map.101 = s16[128,8,128]{2,1,0:T(8,128)(2,1)} custom-call(s16[128,8,128]{2,1,0:T(8,128)(2,1)S(1)} %all-to-all-done.2.got_ref, s32[2,256,256]{2,1,0:T(8,128)S(1)} %pad_add_fusion.1.support_ref, f32[2,256,256]{2,1,0:T(8,128)S(1)} %pad_maximum_fusion.density_ref, bf16[1536,256]{1,0:T(8,128)(2,1)S(1)} %copy-done), custom_call_target="tpu_custom_call" | custom-call | tf_op jit(solution)/shard_map/pallas_call | solution.py:459
  103.5 4.5 %all-to-all-start.3 = ((s16[128,8,128]{2,1,0:T(8,128)(2,1)}), s16[128,8,128]{2,1,0:T(8,128)(2,1)S(1)}, u32[]{:S(2)}, u32[]{:S(2)}) async-start(s16[128,8,128]{2,1,0:T(8,128)(2,1)} %shard_map.101), calls=%async_computation.3 | async-start | bytes 524288 | tf_op jit(solution)/shard_map/all_to_all | solution.py:604
  108.0 1.1 constant_dynamic-slice_fusion
  109.1 0.9 pad_add_fusion
  110.0 2.9 %collective-permute-start.1 = (s16[128,16,128]{2,1,0:T(8,128)(2,1)}, s16[128,16,128]{2,1,0:T(8,128)(2,1)}, u32[]{:S(2)}, u32[]{:S(2)}) collective-permute-start(s16[128,16,128]{2,1,0:T(8,128)(2,1)} %pad_add_fusion), channel_id=1, source_target_pairs={{0,64},{64,0},{1,65},{65,1},{2,66},{66,2},{3,67},{67,3},{4,68},{68... | collective-permute-start | bytes 1572872 | tf_op jit(solution)/shard_map/ppermute | solution.py:608
  112.9 6.2 %all-to-all-done.3.got_ref = s16[128,8,128]{2,1,0:T(8,128)(2,1)S(1)} async-done(((s16[128,8,128]{2,1,0:T(8,128)(2,1)}), s16[128,8,128]{2,1,0:T(8,128)(2,1)S(1)}, u32[]{:S(2)}, u32[]{:S(2)}) %all-to-all-start.3) | async-done | bytes 262176 | tf_op jit(solution)/shard_map/all_to_all | solution.py:604
  119.0 3.8 %shard_map.102 = s16[128,16,128]{2,1,0:T(8,128)(2,1)} custom-call(s32[2]{0:T(128)S(1)} %pad_add_fusion.2.place_ref, s16[128,8,128]{2,1,0:T(8,128)(2,1)S(1)} %all-to-all-done.3.got_ref, f32[512,256]{1,0:T(8,128)S(1)} %copy-done.2, bf16[1024,256]{1,0:T(8,128)(2,1)S(1)} %copy-done.6), custom_call_target="tpu_custom_call" | custom-call | tf_op jit(solution)/shard_map/pallas_call | solution.py:594
  122.8 4.4 %all-to-all-start.4 = ((s16[128,16,128]{2,1,0:T(8,128)(2,1)}), s16[128,16,128]{2,1,0:T(8,128)(2,1)S(1)}, u32[]{:S(2)}, u32[]{:S(2)}) async-start(s16[128,16,128]{2,1,0:T(8,128)(2,1)} %shard_map.102), calls=%async_computation.4 | async-start | bytes 1048576 | tf_op jit(solution)/shard_map/all_to_all | solution.py:604
  127.3 1.6 %shard_map.103 = (f32[2,128,256]{2,1,0:T(8,128)S(1)}, s16[2,128,256]{2,1,0:T(8,128)(2,1)S(1)}) custom-call(s32[1]{0:T(128)} %bitcast.group_ref, s16[128,8,128]{2,1,0:T(8,128)(2,1)S(1)} %all-to-all-done.2.got_ref, s32[2,256,256]{2,1,0:T(8,128)S(1)} %pad_add_fusion.1.support_ref, f32[2,256,256]{2,1,0:T(8,128)S(1)} %pad_maximum_fusion.density_ref, ...), custom_call_target="tpu_custom_call" | custom-call | tf_op jit(solution)/shard_map/pallas_call | solution.py:470
  128.9 3.0 %collective-permute-start.2 = (s16[2,128,256]{2,1,0:T(8,128)(2,1)S(1)}, s16[2,128,256]{2,1,0:T(8,128)(2,1)S(1)}, u32[]{:S(2)}, u32[]{:S(2)}) collective-permute-start(s16[2,128,256]{2,1,0:T(8,128)(2,1)S(1)} %get-tuple-element.13), channel_id=1, source_target_pairs={{0,64},{64,0},{1,65},{65,1},{2,66},{66,2},{3,67},{67,3},{4,68},{68... | collective-permute-start | bytes 393224 | tf_op jit(solution)/shard_map/ppermute | solution.py:608
  131.9 4.4 %shard_map.98 = f32[4,128,256]{2,1,0:T(8,128)} custom-call(s32[1]{0:T(128)} %bitcast.group_ref, s16[128,32,128]{2,1,0:T(8,128)(2,1)} %shard_map.97.own_ref, s16[128,16,128]{2,1,0:T(8,128)(2,1)} %collective-permute-done.1.other_ref), custom_call_target="tpu_custom_call" | custom-call | tf_op jit(solution)/shard_map/pallas_call | solution.py:322
  136.3 2.4 %collective-permute-done.2.other_ref = s16[2,128,256]{2,1,0:T(8,128)(2,1)S(1)} collective-permute-done((s16[2,128,256]{2,1,0:T(8,128)(2,1)S(1)}, s16[2,128,256]{2,1,0:T(8,128)(2,1)S(1)}, u32[]{:S(2)}, u32[]{:S(2)}) %collective-permute-start.2) | collective-permute-done | bytes 131104 | tf_op jit(solution)/shard_map/ppermute | solution.py:608
  138.7 2.0 %all-to-all-done.4.got_ref = s16[128,16,128]{2,1,0:T(8,128)(2,1)S(1)} async-done(((s16[128,16,128]{2,1,0:T(8,128)(2,1)}), s16[128,16,128]{2,1,0:T(8,128)(2,1)S(1)}, u32[]{:S(2)}, u32[]{:S(2)}) %all-to-all-start.4) | async-done | bytes 524320 | tf_op jit(solution)/shard_map/all_to_all | solution.py:604
  140.7 2.7 %shard_map.104 = f32[4,128,256]{2,1,0:T(8,128)} custom-call(s32[1]{0:T(128)} %bitcast.group_ref, s16[128,16,128]{2,1,0:T(8,128)(2,1)S(1)} %all-to-all-done.4.got_ref, s32[4,128,256]{2,1,0:T(8,128)S(1)} %copy-done.4, f32[2,128,256]{2,1,0:T(8,128)S(1)} %get-tuple-element.12.own_ref, s16[2,128,256]{2,1,0:T(8,128)(2,1)S(1)} %collective-permute-done.2.other_ref, ...), custom_call_target="tpu_custom_call" | custom-call | tf_op jit(solution)/shard_map/pallas_call | solution.py:480
  (28 shorter events, 0.4 us)
Async XLA Ops:
  2.7 13.1 %collective-permute-start = (f16[2,2,128,256]{3,2,1,0:T(8,128)(2,1)S(1)}, f16[2,2,128,256]{3,2,1,0:T(8,128)(2,1)S(1)}, u32[]{:S(2)}, u32[]{:S(2)}) collective-permute-start(f16[2,2,128,256]{3,2,1,0:T(8,128)(2,1)S(1)} %pad_maximum_fusion.1), channel_id=1, source_target_pairs={{0,64},{64,0},{1,65},{65,1},{2,66},{66,2},{3,67},{67,3},{4,68},{68... | collective-permute-start | bytes 786440 | tf_op jit(solution)/shard_map/ppermute | solution.py:608
  15.7 9.9 %copy-start.10 = (s32[1,1,64,80]{3,2,1,0:T(8,128)S(1)}, s32[1,1,64,80]{3,2,1,0:T(8,128)}, u32[]{:S(2)}) copy-start(s32[1,1,64,80]{3,2,1,0:T(8,128)} %param.11) | copy-start | bytes 61444
  15.7 10.0 %copy-start.8 = (f32[4,128,256]{2,1,0:T(8,128)S(1)}, f32[4,128,256]{2,1,0:T(8,128)}, u32[]{:S(2)}) copy-start(f32[4,128,256]{2,1,0:T(8,128)} %param.13) | copy-start | bytes 1572868
  15.8 10.0 %copy-start.9 = (f16[2,2,128,256]{3,2,1,0:T(8,128)(2,1)}, f16[2,2,128,256]{3,2,1,0:T(8,128)(2,1)S(1)}, u32[]{:S(2)}) copy-start(f16[2,2,128,256]{3,2,1,0:T(8,128)(2,1)S(1)} %collective-permute-done) | copy-start | bytes 786436
  15.8 32.2 %all-to-all-start = ((bf16[64,88,128]{2,1,0:T(8,128)(2,1)}), bf16[64,88,128]{2,1,0:T(8,128)(2,1)}, u32[]{:S(2)}, u32[]{:S(2)}) async-start(bf16[64,88,128]{2,1,0:T(8,128)(2,1)} %shard_map.95), calls=%async_computation | async-start | bytes 2883584 | tf_op jit(solution)/shard_map/all_to_all | solution.py:627
  25.6 1.1 copy-start
  54.1 23.6 %copy-start.5 = (bf16[1024,256]{1,0:T(8,128)(2,1)S(1)}, bf16[1024,256]{1,0:T(8,128)(2,1)}, u32[]{:S(2)}) copy-start(bf16[1024,256]{1,0:T(8,128)(2,1)} %constant.28.clone.table_ref) | copy-start | bytes 1572868
  54.1 23.5 %all-to-all-start.1 = ((s16[128,32,128]{2,1,0:T(8,128)(2,1)}), s16[128,32,128]{2,1,0:T(8,128)(2,1)S(1)}, u32[]{:S(2)}, u32[]{:S(2)}) async-start(s16[128,32,128]{2,1,0:T(8,128)(2,1)} %shard_map.97.own_ref), calls=%async_computation.1 | async-start | bytes 2097152 | tf_op jit(solution)/shard_map/all_to_all | solution.py:604
  58.4 30.4 %copy-start.3 = (s32[4,128,256]{2,1,0:T(8,128)S(1)}, s32[4,128,256]{2,1,0:T(8,128)}, u32[]{:S(2)}) copy-start(s32[4,128,256]{2,1,0:T(8,128)} %support_ref.1) | copy-start | bytes 1572868
  83.4 0.7 copy-start.7
  84.1 15.7 %all-to-all-start.2 = ((s16[128,8,128]{2,1,0:T(8,128)(2,1)}), s16[128,8,128]{2,1,0:T(8,128)(2,1)S(1)}, u32[]{:S(2)}, u32[]{:S(2)}) async-start(s16[128,8,128]{2,1,0:T(8,128)(2,1)} %copy-done.7), calls=%async_computation.2 | async-start | bytes 524288 | tf_op jit(solution)/shard_map/all_to_all | solution.py:604
  93.1 0.8 copy-start.1
  103.5 15.5 %copy-start.2 = (f32[512,256]{1,0:T(8,128)S(1)}, f32[512,256]{1,0:T(8,128)}, u32[]{:S(2)}) copy-start(f32[512,256]{1,0:T(8,128)} %copy-done.1) | copy-start | bytes 1572868
  103.5 15.5 %copy-start.6 = (bf16[1024,256]{1,0:T(8,128)(2,1)S(1)}, bf16[1024,256]{1,0:T(8,128)(2,1)}, u32[]{:S(2)}) copy-start(bf16[1024,256]{1,0:T(8,128)(2,1)} %constant.28.clone.table_ref) | copy-start | bytes 1572868
  103.5 15.5 %all-to-all-start.3 = ((s16[128,8,128]{2,1,0:T(8,128)(2,1)}), s16[128,8,128]{2,1,0:T(8,128)(2,1)S(1)}, u32[]{:S(2)}, u32[]{:S(2)}) async-start(s16[128,8,128]{2,1,0:T(8,128)(2,1)} %shard_map.101), calls=%async_computation.3 | async-start | bytes 524288 | tf_op jit(solution)/shard_map/all_to_all | solution.py:604
  110.0 22.0 %collective-permute-start.1 = (s16[128,16,128]{2,1,0:T(8,128)(2,1)}, s16[128,16,128]{2,1,0:T(8,128)(2,1)}, u32[]{:S(2)}, u32[]{:S(2)}) collective-permute-start(s16[128,16,128]{2,1,0:T(8,128)(2,1)} %pad_add_fusion), channel_id=1, source_target_pairs={{0,64},{64,0},{1,65},{65,1},{2,66},{66,2},{3,67},{67,3},{4,68},{68... | collective-permute-start | bytes 1572872 | tf_op jit(solution)/shard_map/ppermute | solution.py:608
  122.8 17.9 %all-to-all-start.4 = ((s16[128,16,128]{2,1,0:T(8,128)(2,1)}), s16[128,16,128]{2,1,0:T(8,128)(2,1)S(1)}, u32[]{:S(2)}, u32[]{:S(2)}) async-start(s16[128,16,128]{2,1,0:T(8,128)(2,1)} %shard_map.102), calls=%async_computation.4 | async-start | bytes 1048576 | tf_op jit(solution)/shard_map/all_to_all | solution.py:604
  128.9 11.8 %copy-start.4 = (s32[4,128,256]{2,1,0:T(8,128)S(1)}, s32[4,128,256]{2,1,0:T(8,128)}, u32[]{:S(2)}) copy-start(s32[4,128,256]{2,1,0:T(8,128)} %support_ref.1) | copy-start | bytes 1572868
  128.9 9.8 %collective-permute-start.2 = (s16[2,128,256]{2,1,0:T(8,128)(2,1)S(1)}, s16[2,128,256]{2,1,0:T(8,128)(2,1)S(1)}, u32[]{:S(2)}, u32[]{:S(2)}) collective-permute-start(s16[2,128,256]{2,1,0:T(8,128)(2,1)S(1)} %get-tuple-element.13), channel_id=1, source_target_pairs={{0,64},{64,0},{1,65},{65,1},{2,66},{66,2},{3,67},{67,3},{4,68},{68... | collective-permute-start | bytes 393224 | tf_op jit(solution)/shard_map/ppermute | solution.py:608

commit v5 on v4

--- a/solution.py
+++ b/solution.py
@@ -620,7 +620,8 @@
     def planes_of(first):
         return [lax.dynamic_slice_in_dim(field, first, 2, 0) for field in (density, support)]
 
-    theirs = jnp.stack([field.astype(jnp.float16) for field in planes_of(2 * (1 - group))])
+    theirs = [field.astype(jnp.float16)[None] for field in planes_of(2 * (1 - group))]
+    theirs = jnp.where(lax.broadcasted_iota(jnp.int32, (2, 1, 1, 1), 0) == 0, *theirs)
     other = swap(theirs)
     send = gather_rows(source_row[0, 0], jnp.swapaxes(probabilities, 1, 2), patterns[0])
     send, other = lax.optimization_barrier((send, other))

time: 144 us -> 144 us (level)
    another operation x3 -> x0, other arithmetic: 2.02 us -> none  [local(): jnp.stack([field.astype(jnp.float16) for field in planes_of(2 * (1 - grou...]
    convert_element_type x0 -> x2, other arithmetic: none -> 1.95 us  [local(): field.astype(jnp.float16)[None]]
where the time goes in v5:
time: 144 us; the launch traced here: 143 us
  waiting for transfers between devices  55.2 us (38%)
  Pallas kernels  42.2 us (29%)
  starting transfers between devices  37.3 us (26%)
  other arithmetic  4.15 us (3%)
  local copies, waits for them, and re-layouts  3.6 us (2%)
    all_to_all x4, waiting for transfers between devices, exchange(): return lax.all_to_all(packet, BOTH, split_axis=0, concat_axis=0, tiled=True)  33.2 us
    all_to_all x1, waiting for transfers between devices, local(): got = lax.all_to_all(send, 'slab', split_axis=0, concat_axis=0, tiled=True)  19.8 us
    all_to_all x4, starting transfers between devices, exchange(): return lax.all_to_all(packet, BOTH, split_axis=0, concat_axis=0, tiled=True)  17.8 us
    all_to_all x1, starting transfers between devices, local(): got = lax.all_to_all(send, 'slab', split_axis=0, concat_axis=0, tiled=True)  9.8 us
    ppermute x3, starting transfers between devices, swap(): return lax.ppermute(array, 'grp', [(0, 1), (1, 0)])  9.77 us
    pallas_call x1, Pallas kernels, gather_rows(): call(gather_kernel, jax.ShapeDtypeStruct((SLABS, SEND, 128), jnp.bfloat16...  9.4 us
    pallas_call x1, Pallas kernels, place_rows(): call(place_kernel, jax.ShapeDtypeStruct((DEVS, 32, 128), jnp.int16), mib=...  6.1 us
    pallas_call x1, Pallas kernels, project_once(): call(once_kernel, PACKET, in_specs=[smem()] + spec_vmem(2), out_specs=hbm...  5.79 us
  transfers between devices with their start and end apart: 8, of which 6 were waited for; matrix products, arithmetic and copies ran while one was open for 2% of the time, Pallas kernels for 17%

profile of v5, /device:TPU:1, one launch (start us, length us, event | category | flops | bytes accessed | tf_op | source)
XLA Modules:
  0.0 143.4 jit_solution(13209145332951544326)
XLA Ops:
  0.7 1.0 dynamic-slice_convert_fusion
  1.6 1.0 dynamic-slice_convert_fusion.1
  2.8 3.7 %collective-permute-start = (f16[2,2,128,256]{3,2,1,0:T(8,128)(2,1)S(1)}, f16[2,2,128,256]{3,2,1,0:T(8,128)(2,1)S(1)}, u32[]{:S(2)}, u32[]{:S(2)}) collective-permute-start(f16[2,2,128,256]{3,2,1,0:T(8,128)(2,1)S(1)} %broadcast_select_fusion), channel_id=1, source_target_pairs={{0,64},{64,0},{1,65},{65,1},{2,66},{66,2},{3,67},{67,3},{4,68},{68... | collective-permute-start | bytes 786440 | tf_op jit(solution)/shard_map/ppermute | solution.py:608
  6.4 9.4 %shard_map.95 = bf16[64,88,128]{2,1,0:T(8,128)(2,1)} custom-call(s32[64,80]{1,0:T(8,128)} %bitcast.18, s32[64,80]{1,0:T(8,128)} %bitcast.19, bf16[1,32,256]{2,1,0:T(8,128)(2,1)} %bitcast.21, bf16[256,16384]{1,0:T(8,128)(2,1)} %bitcast.17), custom_call_target="tpu_custom_call" | custom-call | flops 268435456 | bytes 33554432 | tf_op jit(solution)/shard_map/pallas_call | solution.py:218
  15.9 9.8 %all-to-all-start = ((bf16[64,88,128]{2,1,0:T(8,128)(2,1)}), bf16[64,88,128]{2,1,0:T(8,128)(2,1)}, u32[]{:S(2)}, u32[]{:S(2)}) async-start(bf16[64,88,128]{2,1,0:T(8,128)(2,1)} %shard_map.95), calls=%async_computation | async-start | bytes 2883584 | tf_op jit(solution)/shard_map/all_to_all | solution.py:628
  25.9 0.9 copy-done
  26.8 1.4 shard_map.96.packet_ref
  28.2 19.8 %all-to-all-done.got_ref = bf16[64,88,128]{2,1,0:T(8,128)(2,1)} async-done(((bf16[64,88,128]{2,1,0:T(8,128)(2,1)}), bf16[64,88,128]{2,1,0:T(8,128)(2,1)}, u32[]{:S(2)}, u32[]{:S(2)}) %all-to-all-start) | async-done | bytes 1441824 | tf_op jit(solution)/shard_map/all_to_all | solution.py:628
  48.1 6.1 %shard_map.97.own_ref = s16[128,32,128]{2,1,0:T(8,128)(2,1)} custom-call(bf16[64,88,128]{2,1,0:T(8,128)(2,1)} %all-to-all-done.got_ref, s32[4,1,1280]{2,1,0:T(1,128)S(1)} %reshape_squeeze.3.row_ref, s32[64,128]{1,0:T(8,128)S(1)} %pad.4.column_ref, s16[128,8,128]{2,1,0:T(8,128)(2,1)S(1)} %shard_map.96.packet_ref), custom_call_target="tpu_custom_call" | custom-call | tf_op jit(solution)/shard_map/pallas_call | solution.py:290
  54.2 4.2 %all-to-all-start.1 = ((s16[128,32,128]{2,1,0:T(8,128)(2,1)}), s16[128,32,128]{2,1,0:T(8,128)(2,1)S(1)}, u32[]{:S(2)}, u32[]{:S(2)}) async-start(s16[128,32,128]{2,1,0:T(8,128)(2,1)} %shard_map.97.own_ref), calls=%async_computation.1 | async-start | bytes 2097152 | tf_op jit(solution)/shard_map/all_to_all | solution.py:604
  58.5 19.0 %all-to-all-done.1.got_ref = s16[128,32,128]{2,1,0:T(8,128)(2,1)S(1)} async-done(((s16[128,32,128]{2,1,0:T(8,128)(2,1)}), s16[128,32,128]{2,1,0:T(8,128)(2,1)S(1)}, u32[]{:S(2)}, u32[]{:S(2)}) %all-to-all-start.1) | async-done | bytes 1048608 | tf_op jit(solution)/shard_map/all_to_all | solution.py:604
  77.5 5.8 %shard_map.99 = s16[128,8,128]{2,1,0:T(8,128)(2,1)S(1)} custom-call(s32[2]{0:T(128)S(1)} %pad_add_fusion.2.place_ref, s16[128,32,128]{2,1,0:T(8,128)(2,1)S(1)} %all-to-all-done.1.got_ref, bf16[1024,256]{1,0:T(8,128)(2,1)S(1)} %copy-done.5), custom_call_target="tpu_custom_call" | custom-call | tf_op jit(solution)/shard_map/pallas_call | solution.py:578
  83.3 0.7 copy-done.7
  84.0 4.7 %all-to-all-start.2 = ((s16[128,8,128]{2,1,0:T(8,128)(2,1)}), s16[128,8,128]{2,1,0:T(8,128)(2,1)S(1)}, u32[]{:S(2)}, u32[]{:S(2)}) async-start(s16[128,8,128]{2,1,0:T(8,128)(2,1)} %copy-done.7), calls=%async_computation.2 | async-start | bytes 524288 | tf_op jit(solution)/shard_map/all_to_all | solution.py:604
  88.7 1.0 convert_select_fusion.1
  89.7 3.2 %shard_map.100.even_ref = f32[512,256]{1,0:T(8,128)S(1)} custom-call(s32[2]{0:T(128)S(1)} %pad_add_fusion.2.place_ref, s16[128,32,128]{2,1,0:T(8,128)(2,1)S(1)} %all-to-all-done.1.got_ref), custom_call_target="tpu_custom_call" | custom-call | tf_op jit(solution)/shard_map/pallas_call | solution.py:588
  93.0 0.8 copy-done.1
  93.8 6.0 %all-to-all-done.2.got_ref = s16[128,8,128]{2,1,0:T(8,128)(2,1)S(1)} async-done(((s16[128,8,128]{2,1,0:T(8,128)(2,1)}), s16[128,8,128]{2,1,0:T(8,128)(2,1)S(1)}, u32[]{:S(2)}, u32[]{:S(2)}) %all-to-all-start.2) | async-done | bytes 262176 | tf_op jit(solution)/shard_map/all_to_all | solution.py:604
  99.8 3.6 %shard_map.101 = s16[128,8,128]{2,1,0:T(8,128)(2,1)} custom-call(s16[128,8,128]{2,1,0:T(8,128)(2,1)S(1)} %all-to-all-done.2.got_ref, s32[2,256,256]{2,1,0:T(8,128)S(1)} %pad_add_fusion.1.support_ref, f32[2,256,256]{2,1,0:T(8,128)S(1)} %pad_maximum_fusion.density_ref, bf16[1536,256]{1,0:T(8,128)(2,1)S(1)} %copy-done), custom_call_target="tpu_custom_call" | custom-call | tf_op jit(solution)/shard_map/pallas_call | solution.py:459
  103.4 4.5 %all-to-all-start.3 = ((s16[128,8,128]{2,1,0:T(8,128)(2,1)}), s16[128,8,128]{2,1,0:T(8,128)(2,1)S(1)}, u32[]{:S(2)}, u32[]{:S(2)}) async-start(s16[128,8,128]{2,1,0:T(8,128)(2,1)} %shard_map.101), calls=%async_computation.3 | async-start | bytes 524288 | tf_op jit(solution)/shard_map/all_to_all | solution.py:604
  107.9 1.1 constant_dynamic-slice_fusion
  109.0 0.9 pad_add_fusion
  109.9 2.9 %collective-permute-start.1 = (s16[128,16,128]{2,1,0:T(8,128)(2,1)}, s16[128,16,128]{2,1,0:T(8,128)(2,1)}, u32[]{:S(2)}, u32[]{:S(2)}) collective-permute-start(s16[128,16,128]{2,1,0:T(8,128)(2,1)} %pad_add_fusion), channel_id=1, source_target_pairs={{0,64},{64,0},{1,65},{65,1},{2,66},{66,2},{3,67},{67,3},{4,68},{68... | collective-permute-start | bytes 1572872 | tf_op jit(solution)/shard_map/ppermute | solution.py:608
  112.8 6.2 %all-to-all-done.3.got_ref = s16[128,8,128]{2,1,0:T(8,128)(2,1)S(1)} async-done(((s16[128,8,128]{2,1,0:T(8,128)(2,1)}), s16[128,8,128]{2,1,0:T(8,128)(2,1)S(1)}, u32[]{:S(2)}, u32[]{:S(2)}) %all-to-all-start.3) | async-done | bytes 262176 | tf_op jit(solution)/shard_map/all_to_all | solution.py:604
  118.9 3.8 %shard_map.102 = s16[128,16,128]{2,1,0:T(8,128)(2,1)} custom-call(s32[2]{0:T(128)S(1)} %pad_add_fusion.2.place_ref, s16[128,8,128]{2,1,0:T(8,128)(2,1)S(1)} %all-to-all-done.3.got_ref, f32[512,256]{1,0:T(8,128)S(1)} %copy-done.2, bf16[1024,256]{1,0:T(8,128)(2,1)S(1)} %copy-done.6), custom_call_target="tpu_custom_call" | custom-call | tf_op jit(solution)/shard_map/pallas_call | solution.py:594
  122.7 4.5 %all-to-all-start.4 = ((s16[128,16,128]{2,1,0:T(8,128)(2,1)}), s16[128,16,128]{2,1,0:T(8,128)(2,1)S(1)}, u32[]{:S(2)}, u32[]{:S(2)}) async-start(s16[128,16,128]{2,1,0:T(8,128)(2,1)} %shard_map.102), calls=%async_computation.4 | async-start | bytes 1048576 | tf_op jit(solution)/shard_map/all_to_all | solution.py:604
  127.2 1.6 %shard_map.103 = (f32[2,128,256]{2,1,0:T(8,128)S(1)}, s16[2,128,256]{2,1,0:T(8,128)(2,1)S(1)}) custom-call(s32[1]{0:T(128)} %bitcast.group_ref, s16[128,8,128]{2,1,0:T(8,128)(2,1)S(1)} %all-to-all-done.2.got_ref, s32[2,256,256]{2,1,0:T(8,128)S(1)} %pad_add_fusion.1.support_ref, f32[2,256,256]{2,1,0:T(8,128)S(1)} %pad_maximum_fusion.density_ref, ...), custom_call_target="tpu_custom_call" | custom-call | tf_op jit(solution)/shard_map/pallas_call | solution.py:470
  128.9 3.2 %collective-permute-start.2 = (s16[2,128,256]{2,1,0:T(8,128)(2,1)S(1)}, s16[2,128,256]{2,1,0:T(8,128)(2,1)S(1)}, u32[]{:S(2)}, u32[]{:S(2)}) collective-permute-start(s16[2,128,256]{2,1,0:T(8,128)(2,1)S(1)} %get-tuple-element.13), channel_id=1, source_target_pairs={{0,64},{64,0},{1,65},{65,1},{2,66},{66,2},{3,67},{67,3},{4,68},{68... | collective-permute-start | bytes 393224 | tf_op jit(solution)/shard_map/ppermute | solution.py:608
  132.1 4.4 %shard_map.98 = f32[4,128,256]{2,1,0:T(8,128)} custom-call(s32[1]{0:T(128)} %bitcast.group_ref, s16[128,32,128]{2,1,0:T(8,128)(2,1)} %shard_map.97.own_ref, s16[128,16,128]{2,1,0:T(8,128)(2,1)} %collective-permute-done.1.other_ref), custom_call_target="tpu_custom_call" | custom-call | tf_op jit(solution)/shard_map/pallas_call | solution.py:322
  136.5 2.1 %collective-permute-done.2.other_ref = s16[2,128,256]{2,1,0:T(8,128)(2,1)S(1)} collective-permute-done((s16[2,128,256]{2,1,0:T(8,128)(2,1)S(1)}, s16[2,128,256]{2,1,0:T(8,128)(2,1)S(1)}, u32[]{:S(2)}, u32[]{:S(2)}) %collective-permute-start.2) | collective-permute-done | bytes 131104 | tf_op jit(solution)/shard_map/ppermute | solution.py:608
  138.6 2.0 %all-to-all-done.4.got_ref = s16[128,16,128]{2,1,0:T(8,128)(2,1)S(1)} async-done(((s16[128,16,128]{2,1,0:T(8,128)(2,1)}), s16[128,16,128]{2,1,0:T(8,128)(2,1)S(1)}, u32[]{:S(2)}, u32[]{:S(2)}) %all-to-all-start.4) | async-done | bytes 524320 | tf_op jit(solution)/shard_map/all_to_all | solution.py:604
  140.6 2.7 %shard_map.104 = f32[4,128,256]{2,1,0:T(8,128)} custom-call(s32[1]{0:T(128)} %bitcast.group_ref, s16[128,16,128]{2,1,0:T(8,128)(2,1)S(1)} %all-to-all-done.4.got_ref, s32[4,128,256]{2,1,0:T(8,128)S(1)} %copy-done.4, f32[2,128,256]{2,1,0:T(8,128)S(1)} %get-tuple-element.12.own_ref, s16[2,128,256]{2,1,0:T(8,128)(2,1)S(1)} %collective-permute-done.2.other_ref, ...), custom_call_target="tpu_custom_call" | custom-call | tf_op jit(solution)/shard_map/pallas_call | solution.py:480
  (29 shorter events, 0.5 us)
Async XLA Ops:
  2.8 13.1 %collective-permute-start = (f16[2,2,128,256]{3,2,1,0:T(8,128)(2,1)S(1)}, f16[2,2,128,256]{3,2,1,0:T(8,128)(2,1)S(1)}, u32[]{:S(2)}, u32[]{:S(2)}) collective-permute-start(f16[2,2,128,256]{3,2,1,0:T(8,128)(2,1)S(1)} %broadcast_select_fusion), channel_id=1, source_target_pairs={{0,64},{64,0},{1,65},{65,1},{2,66},{66,2},{3,67},{67,3},{4,68},{68... | collective-permute-start | bytes 786440 | tf_op jit(solution)/shard_map/ppermute | solution.py:608
  15.8 9.9 %copy-start.10 = (s32[1,1,64,80]{3,2,1,0:T(8,128)S(1)}, s32[1,1,64,80]{3,2,1,0:T(8,128)}, u32[]{:S(2)}) copy-start(s32[1,1,64,80]{3,2,1,0:T(8,128)} %param.11) | copy-start | bytes 61444
  15.8 10.0 %copy-start.8 = (f32[4,128,256]{2,1,0:T(8,128)S(1)}, f32[4,128,256]{2,1,0:T(8,128)}, u32[]{:S(2)}) copy-start(f32[4,128,256]{2,1,0:T(8,128)} %param.13) | copy-start | bytes 1572868
  15.9 10.0 %copy-start.9 = (f16[2,2,128,256]{3,2,1,0:T(8,128)(2,1)}, f16[2,2,128,256]{3,2,1,0:T(8,128)(2,1)S(1)}, u32[]{:S(2)}) copy-start(f16[2,2,128,256]{3,2,1,0:T(8,128)(2,1)S(1)} %collective-permute-done) | copy-start | bytes 786436
  15.9 32.2 %all-to-all-start = ((bf16[64,88,128]{2,1,0:T(8,128)(2,1)}), bf16[64,88,128]{2,1,0:T(8,128)(2,1)}, u32[]{:S(2)}, u32[]{:S(2)}) async-start(bf16[64,88,128]{2,1,0:T(8,128)(2,1)} %shard_map.95), calls=%async_computation | async-start | bytes 2883584 | tf_op jit(solution)/shard_map/all_to_all | solution.py:628
  25.7 1.1 copy-start
  54.2 23.3 %copy-start.5 = (bf16[1024,256]{1,0:T(8,128)(2,1)S(1)}, bf16[1024,256]{1,0:T(8,128)(2,1)}, u32[]{:S(2)}) copy-start(bf16[1024,256]{1,0:T(8,128)(2,1)} %constant.29.clone.table_ref) | copy-start | bytes 1572868
  54.2 23.3 %all-to-all-start.1 = ((s16[128,32,128]{2,1,0:T(8,128)(2,1)}), s16[128,32,128]{2,1,0:T(8,128)(2,1)S(1)}, u32[]{:S(2)}, u32[]{:S(2)}) async-start(s16[128,32,128]{2,1,0:T(8,128)(2,1)} %shard_map.97.own_ref), calls=%async_computation.1 | async-start | bytes 2097152 | tf_op jit(solution)/shard_map/all_to_all | solution.py:604
  58.4 30.3 %copy-start.3 = (s32[4,128,256]{2,1,0:T(8,128)S(1)}, s32[4,128,256]{2,1,0:T(8,128)}, u32[]{:S(2)}) copy-start(s32[4,128,256]{2,1,0:T(8,128)} %support_ref.1) | copy-start | bytes 1572868
  83.3 0.7 copy-start.7
  84.0 15.7 %all-to-all-start.2 = ((s16[128,8,128]{2,1,0:T(8,128)(2,1)}), s16[128,8,128]{2,1,0:T(8,128)(2,1)S(1)}, u32[]{:S(2)}, u32[]{:S(2)}) async-start(s16[128,8,128]{2,1,0:T(8,128)(2,1)} %copy-done.7), calls=%async_computation.2 | async-start | bytes 524288 | tf_op jit(solution)/shard_map/all_to_all | solution.py:604
  93.0 0.8 copy-start.1
  103.4 15.5 %copy-start.2 = (f32[512,256]{1,0:T(8,128)S(1)}, f32[512,256]{1,0:T(8,128)}, u32[]{:S(2)}) copy-start(f32[512,256]{1,0:T(8,128)} %copy-done.1) | copy-start | bytes 1572868
  103.4 15.5 %copy-start.6 = (bf16[1024,256]{1,0:T(8,128)(2,1)S(1)}, bf16[1024,256]{1,0:T(8,128)(2,1)}, u32[]{:S(2)}) copy-start(bf16[1024,256]{1,0:T(8,128)(2,1)} %constant.29.clone.table_ref) | copy-start | bytes 1572868
  103.4 15.5 %all-to-all-start.3 = ((s16[128,8,128]{2,1,0:T(8,128)(2,1)}), s16[128,8,128]{2,1,0:T(8,128)(2,1)S(1)}, u32[]{:S(2)}, u32[]{:S(2)}) async-start(s16[128,8,128]{2,1,0:T(8,128)(2,1)} %shard_map.101), calls=%async_computation.3 | async-start | bytes 524288 | tf_op jit(solution)/shard_map/all_to_all | solution.py:604
  109.9 22.2 %collective-permute-start.1 = (s16[128,16,128]{2,1,0:T(8,128)(2,1)}, s16[128,16,128]{2,1,0:T(8,128)(2,1)}, u32[]{:S(2)}, u32[]{:S(2)}) collective-permute-start(s16[128,16,128]{2,1,0:T(8,128)(2,1)} %pad_add_fusion), channel_id=1, source_target_pairs={{0,64},{64,0},{1,65},{65,1},{2,66},{66,2},{3,67},{67,3},{4,68},{68... | collective-permute-start | bytes 1572872 | tf_op jit(solution)/shard_map/ppermute | solution.py:608
  122.7 17.9 %all-to-all-start.4 = ((s16[128,16,128]{2,1,0:T(8,128)(2,1)}), s16[128,16,128]{2,1,0:T(8,128)(2,1)S(1)}, u32[]{:S(2)}, u32[]{:S(2)}) async-start(s16[128,16,128]{2,1,0:T(8,128)(2,1)} %shard_map.102), calls=%async_computation.4 | async-start | bytes 1048576 | tf_op jit(solution)/shard_map/all_to_all | solution.py:604
  128.8 11.8 %copy-start.4 = (s32[4,128,256]{2,1,0:T(8,128)S(1)}, s32[4,128,256]{2,1,0:T(8,128)}, u32[]{:S(2)}) copy-start(s32[4,128,256]{2,1,0:T(8,128)} %support_ref.1) | copy-start | bytes 1572868
  128.9 9.8 %collective-permute-start.2 = (s16[2,128,256]{2,1,0:T(8,128)(2,1)S(1)}, s16[2,128,256]{2,1,0:T(8,128)(2,1)S(1)}, u32[]{:S(2)}, u32[]{:S(2)}) collective-permute-start(s16[2,128,256]{2,1,0:T(8,128)(2,1)S(1)} %get-tuple-element.13), channel_id=1, source_target_pairs={{0,64},{64,0},{1,65},{65,1},{2,66},{66,2},{3,67},{67,3},{4,68},{68... | collective-permute-start | bytes 393224 | tf_op jit(solution)/shard_map/ppermute | solution.py:608
